TPU v7x, 32 devices: a whole 2x2x4 slice. The times are simulated.
32 devices in a mesh: wide: 16 (over z, y, x), narrow: 2 (over core).
Axes of the slice: x: 2, y: 2, z: 4, core: 2. Of those that a mesh axis runs over, the one named last changes fastest.
Arguments:
- tokens: bfloat16 [16384, 768], P(('wide', 'narrow')), may hold values from -6 to 6
- segment: int32 [16384], P(('wide', 'narrow')), may hold values from 0 to 3, as said below
- cotangent: bfloat16 [16384, 768], P(('wide', 'narrow')), may hold values from -6 to 6
- w_up: bfloat16 [768, 3072], P(('wide', 'narrow')), may hold values from -0.21875 to 0.21875
- w_value: bfloat16 [768, 1536], P(('wide', 'narrow')), may hold values from -0.21875 to 0.21875
- w_proj: bfloat16 [3072, 1536], P(('wide', 'narrow')), may hold values from -0.109375 to 0.109375
- w_out: bfloat16 [1536, 768], P(('wide', 'narrow')), may hold values from -0.3125 to 0.3125
- norm_gain: bfloat16 [768], P(('wide', 'narrow')), may hold values from 0.5 to 1.5
- norm_bias: bfloat16 [768], P(('wide', 'narrow')), may hold values from -3 to 3
- bias_up: bfloat16 [3072], P(('wide', 'narrow')), may hold values from -3 to 3
- bias_value: bfloat16 [1536], P(('wide', 'narrow')), may hold values from -3 to 3
- bias_proj: bfloat16 [1536], P(('wide', 'narrow')), may hold values from -3 to 3
- bias_out: bfloat16 [768], P(('wide', 'narrow')), may hold values from -3 to 3
- log_rate: bfloat16 [1536, 64], P(('wide', 'narrow')), may hold values from -1 to 1
- log_step: bfloat16 [1536], P(('wide', 'narrow')), may hold values from -7 to -2.5
- input_map: bfloat16 [1536, 64], P(('wide', 'narrow')), may hold values from -3 to 3
- output_map: bfloat16 [1536, 64], P(('wide', 'narrow')), may hold values from -3 to 3
- skip_gain: bfloat16 [1536], P(('wide', 'narrow')), may hold values from -4 to 4
Outputs:
- result: bfloat16 [16384, 768], P(('wide', 'narrow'))
- grad_tokens: float32 [16384, 768], P(('wide', 'narrow'))
- grad_w_up: float32 [768, 3072], P(('wide', 'narrow'))
- grad_w_value: float32 [768, 1536], P(('wide', 'narrow'))
- grad_w_proj: float32 [3072, 1536], P(('wide', 'narrow'))
- grad_w_out: float32 [1536, 768], P(('wide', 'narrow'))
- grad_norm_gain: float32 [768], P(('wide', 'narrow'))
- grad_norm_bias: float32 [768], P(('wide', 'narrow'))
- grad_bias_up: float32 [3072], P(('wide', 'narrow'))
- grad_bias_value: float32 [1536], P(('wide', 'narrow'))
- grad_bias_proj: float32 [1536], P(('wide', 'narrow'))
- grad_bias_out: float32 [768], P(('wide', 'narrow'))
- grad_log_rate: float32 [1536, 64], P(('wide', 'narrow'))
- grad_log_step: float32 [1536], P(('wide', 'narrow'))
- grad_input_map: float32 [1536, 64], P(('wide', 'narrow'))
- grad_output_map: float32 [1536, 64], P(('wide', 'narrow'))
- grad_skip_gain: float32 [1536], P(('wide', 'narrow'))
Inputs may be any that keep to these rules, and one draw needn't show every extreme that they name: Within each device's block of 512 tokens, segment numbers whole sequences from 0 upward: first some sequences of 512 tokens, then sequences of 128 tokens; some device holds only short ones.
All inputs are finite; a program needn't handle non-finite values.
Results may differ from a plain program's by a relative error of at most 0.007.
Values may be sent and summed in bfloat16 or wider, within the bound.
No kernel may reach another device: no remote copies, remote signals or barrier semaphores. Data moves between devices by JAX's collectives and lax.ppermute only.
A program may use at most 384 MiB of HBM per device.

v0:
```python
import jax
import jax.numpy as jnp
from jax import lax
from jax.sharding import PartitionSpec as P

BLOCK = 32


def contract(left, right, left_dim, right_dim):
    return lax.dot_general(
        left, right, (((left_dim,), (right_dim,)), ((), ())), preferred_element_type=jnp.float32
    )


def ssm_half(values, labels, log_rate, log_step, input_map, output_map):
    length, width = values.shape
    count = length // BLOCK
    rate = -jnp.exp(log_rate)
    step_size = jnp.exp(log_step)[:, None]
    decay_log = (step_size * rate).T
    factor = jnp.exp(decay_log)
    weight = (output_map * (jnp.exp(step_size * rate) - 1.0) / rate * input_map).T
    lags = jnp.arange(BLOCK, dtype=jnp.float32)
    powers = jnp.exp(lags[:, None, None] * decay_log[None])
    kernel = jnp.einsum("lnh,nh->lh", powers, weight, precision=lax.Precision.HIGHEST)
    places = jnp.arange(BLOCK)
    onehot = (places[:, None, None] - places[None, :, None] == places[None, None, :]).astype(
        jnp.float32
    )
    toeplitz = jnp.einsum("tsl,lh->tsh", onehot, kernel, precision=lax.Precision.HIGHEST)
    blocks = values.reshape(count, BLOCK, width)
    inner = jnp.einsum("tsh,bsh->bth", toeplitz, blocks, precision=lax.Precision.HIGHEST)
    ends = jnp.einsum("snh,bsh->bnh", powers[::-1], blocks, precision=lax.Precision.HIGHEST)
    heads = labels.reshape(count, BLOCK)
    carry_on = jnp.concatenate(
        [jnp.zeros((1,), jnp.float32), (heads[1:, 0] == heads[:-1, -1]).astype(jnp.float32)]
    )
    full_decay = jnp.exp(BLOCK * decay_log)

    def advance(state, item):
        flag, local = item
        entering = flag * state
        return (full_decay * entering + local, entering)

    start = jnp.zeros(decay_log.shape, jnp.float32)
    finals, entering = lax.scan(advance, start, (carry_on, ends))
    lead = powers * factor[None] * weight[None]
    outer = jnp.einsum("tnh,bnh->bth", lead, entering, precision=lax.Precision.HIGHEST)
    return (inner + outer).reshape(length, width)


def mixer(values, labels, log_rate, log_step, input_map, output_map, skip_gain):
    half = values.shape[1] // 2
    forward_part = ssm_half(
        values[:, :half],
        labels,
        log_rate[:half],
        log_step[:half],
        input_map[:half],
        output_map[:half],
    )
    backward_part = ssm_half(
        values[::-1, half:],
        labels[::-1],
        log_rate[half:],
        log_step[half:],
        input_map[half:],
        output_map[half:],
    )[::-1]
    return jnp.concatenate([forward_part, backward_part], axis=1) + skip_gain * values


def norm_rows(inputs, norm_gain, norm_bias):
    average = jnp.mean(inputs, axis=-1, keepdims=True)
    centred = inputs - average
    spread = jnp.mean(centred * centred, axis=-1, keepdims=True)
    return centred * lax.rsqrt(spread + 1e-05) * norm_gain + norm_bias


def gather_all(shards):
    return (
        lax.all_gather(shards[0], ("wide", "narrow"), axis=0, tiled=True),
        lax.all_gather(shards[1], ("wide", "narrow"), axis=0, tiled=True),
        lax.all_gather(shards[2], ("wide", "narrow"), axis=0, tiled=True),
        lax.all_gather(shards[3], ("wide", "narrow"), axis=0, tiled=True),
        lax.all_gather(shards[4], ("wide", "narrow"), axis=0, tiled=True),
        lax.all_gather(shards[5], ("wide", "narrow"), axis=0, tiled=True),
        lax.all_gather(shards[6], ("wide", "narrow"), axis=0, tiled=True),
        lax.all_gather(shards[7], ("wide", "narrow"), axis=0, tiled=True),
        lax.all_gather(shards[8], ("wide", "narrow"), axis=0, tiled=True),
        lax.all_gather(shards[9], ("wide", "narrow"), axis=0, tiled=True),
        lax.all_gather(shards[10], ("wide", "narrow"), axis=0, tiled=True),
        lax.all_gather(shards[11], ("wide", "narrow"), axis=0, tiled=True),
        lax.all_gather(shards[12], ("wide", "narrow"), axis=0, tiled=True),
        lax.all_gather(shards[13], ("wide", "narrow"), axis=0, tiled=True),
        lax.all_gather(shards[14], ("wide", "narrow"), axis=0, tiled=True),
    )


def per_device(
    tokens,
    segment,
    cotangent,
    w_up,
    w_value,
    w_proj,
    w_out,
    norm_gain,
    norm_bias,
    bias_up,
    bias_value,
    bias_proj,
    bias_out,
    log_rate,
    log_step,
    input_map,
    output_map,
    skip_gain,
):
    shards = (
        w_up,
        w_value,
        w_proj,
        w_out,
        norm_gain,
        norm_bias,
        bias_up,
        bias_value,
        bias_proj,
        bias_out,
        log_rate,
        log_step,
        input_map,
        output_map,
        skip_gain,
    )
    whole = gather_all(shards)
    small = tuple((p.astype(jnp.float32) for p in whole[4:]))
    (
        gain_f,
        shift_f,
        up_bias,
        value_bias,
        proj_bias,
        out_bias,
        rate_f,
        step_f,
        inmap_f,
        outmap_f,
        skip_f,
    ) = small
    full_up, full_value, full_proj, full_out = (whole[0], whole[1], whole[2], whole[3])
    inputs = tokens.astype(jnp.float32)
    normed, norm_back = jax.vjp(norm_rows, inputs, gain_f, shift_f)
    normed_low = normed.astype(jnp.bfloat16)
    up_pre = jnp.dot(normed_low, full_up, preferred_element_type=jnp.float32) + up_bias
    up_act, up_back = jax.vjp(jax.nn.gelu, up_pre)
    up_low = up_act.astype(jnp.bfloat16)
    value_pre = jnp.dot(normed_low, full_value, preferred_element_type=jnp.float32) + value_bias

    def branch(value_in, rate_in, step_in, inmap_in, outmap_in, skip_in):
        return mixer(jax.nn.gelu(value_in), segment, rate_in, step_in, inmap_in, outmap_in, skip_in)

    mixed, mix_back = jax.vjp(branch, value_pre, rate_f, step_f, inmap_f, outmap_f, skip_f)
    proj = jnp.dot(up_low, full_proj, preferred_element_type=jnp.float32) + proj_bias
    gated_low = (mixed * proj).astype(jnp.bfloat16)
    result = (
        inputs + jnp.dot(gated_low, full_out, preferred_element_type=jnp.float32) + out_bias
    ).astype(jnp.bfloat16)
    whole = gather_all(shards)
    full_up, full_value, full_proj, full_out = (whole[0], whole[1], whole[2], whole[3])
    upstream = cotangent.astype(jnp.float32)
    grad_w_out = contract(gated_low, cotangent, 0, 0)
    grad_bias_out = jnp.sum(upstream, axis=0)
    grad_gated = contract(cotangent, full_out, 1, 1)
    grad_mixed = grad_gated * proj
    grad_proj_low = (grad_gated * mixed).astype(jnp.bfloat16)
    grad_bias_proj = jnp.sum(grad_proj_low.astype(jnp.float32), axis=0)
    grad_w_proj = contract(up_low, grad_proj_low, 0, 0)
    early = (
        lax.psum_scatter(grad_w_proj, ("wide", "narrow"), scatter_dimension=0, tiled=True),
        lax.psum_scatter(grad_bias_proj, ("wide", "narrow"), scatter_dimension=0, tiled=True),
        lax.psum_scatter(grad_bias_out, ("wide", "narrow"), scatter_dimension=0, tiled=True),
    )
    grad_up_act = contract(grad_proj_low, full_proj, 1, 1)
    grad_up_low = up_back(grad_up_act)[0].astype(jnp.bfloat16)
    grad_bias_up = jnp.sum(grad_up_low.astype(jnp.float32), axis=0)
    grad_w_up = contract(normed_low, grad_up_low, 0, 0)
    grad_value, grad_rate, grad_step, grad_inmap, grad_outmap, grad_skip = mix_back(grad_mixed)
    grad_value_low = grad_value.astype(jnp.bfloat16)
    grad_bias_value = jnp.sum(grad_value_low.astype(jnp.float32), axis=0)
    grad_w_value = contract(normed_low, grad_value_low, 0, 0)
    grad_normed = contract(grad_up_low, full_up, 1, 1) + contract(grad_value_low, full_value, 1, 1)
    grad_inputs, grad_gain, grad_shift = norm_back(grad_normed)
    grad_inputs = grad_inputs + upstream
    rest = (
        grad_w_up,
        grad_w_value,
        grad_w_out,
        grad_gain,
        grad_shift,
        grad_bias_up,
        grad_bias_value,
        grad_rate,
        grad_step,
        grad_inmap,
        grad_outmap,
        grad_skip,
    )
    late = (
        lax.psum_scatter(rest[0], ("wide", "narrow"), scatter_dimension=0, tiled=True),
        lax.psum_scatter(rest[1], ("wide", "narrow"), scatter_dimension=0, tiled=True),
        lax.psum_scatter(rest[2], ("wide", "narrow"), scatter_dimension=0, tiled=True),
        lax.psum_scatter(rest[3], ("wide", "narrow"), scatter_dimension=0, tiled=True),
        lax.psum_scatter(rest[4], ("wide", "narrow"), scatter_dimension=0, tiled=True),
        lax.psum_scatter(rest[5], ("wide", "narrow"), scatter_dimension=0, tiled=True),
        lax.psum_scatter(rest[6], ("wide", "narrow"), scatter_dimension=0, tiled=True),
        lax.psum_scatter(rest[7], ("wide", "narrow"), scatter_dimension=0, tiled=True),
        lax.psum_scatter(rest[8], ("wide", "narrow"), scatter_dimension=0, tiled=True),
        lax.psum_scatter(rest[9], ("wide", "narrow"), scatter_dimension=0, tiled=True),
        lax.psum_scatter(rest[10], ("wide", "narrow"), scatter_dimension=0, tiled=True),
        lax.psum_scatter(rest[11], ("wide", "narrow"), scatter_dimension=0, tiled=True),
    )
    return (
        result,
        grad_inputs,
        late[0],
        late[1],
        early[0],
        late[2],
        late[3],
        late[4],
        late[5],
        late[6],
        early[1],
        early[2],
        late[7],
        late[8],
        late[9],
        late[10],
        late[11],
    )


def solution(mesh):
    placed = (
        P(("wide", "narrow"), None),
        P(("wide", "narrow")),
        P(("wide", "narrow"), None),
        P(("wide", "narrow"), None),
        P(("wide", "narrow"), None),
        P(("wide", "narrow"), None),
        P(("wide", "narrow"), None),
        P(("wide", "narrow")),
        P(("wide", "narrow")),
        P(("wide", "narrow")),
        P(("wide", "narrow")),
        P(("wide", "narrow")),
        P(("wide", "narrow")),
        P(("wide", "narrow"), None),
        P(("wide", "narrow")),
        P(("wide", "narrow"), None),
        P(("wide", "narrow"), None),
        P(("wide", "narrow")),
    )
    return jax.shard_map(
        per_device,
        mesh=mesh,
        in_specs=placed,
        out_specs=(
            P(("wide", "narrow"), None),
            P(("wide", "narrow"), None),
            P(("wide", "narrow"), None),
            P(("wide", "narrow"), None),
            P(("wide", "narrow"), None),
            P(("wide", "narrow"), None),
            P(("wide", "narrow")),
            P(("wide", "narrow")),
            P(("wide", "narrow")),
            P(("wide", "narrow")),
            P(("wide", "narrow")),
            P(("wide", "narrow")),
            P(("wide", "narrow"), None),
            P(("wide", "narrow")),
            P(("wide", "narrow"), None),
            P(("wide", "narrow"), None),
            P(("wide", "narrow")),
        ),
        check_vma=False,
    )
```

profile of v0, /device:TPU:0, one launch (start us, length us, event | category | flops | bytes accessed | tf_op | source)
XLA Modules:
  0.0 2045.1 jit_solution(7294124378924133998)
XLA Ops:
  11.6 44.8 %all_gather.55 = bf16[1536,64]{1,0:T(8,128)(2,1)S(1)} all-gather(bf16[48,64]{1,0:T(8,128)(2,1)} %param.39), channel_id=1, replica_groups=mesh['wide'=16,'narrow'=2] {'wide','narrow'}, dimensions={0}, use_global_device_ids=true | all-gather | bytes 202752 | tf_op jit(solution)/shard_map/all_gather | solution.py:92
  63.2 38.0 %all-reduce.27 = (bf16[1536]{0:T(1024)(128)(2,1)S(1)}, bf16[768]{0:T(1024)(128)(2,1)S(1)}, bf16[768]{0:T(1024)(128)(2,1)S(1)}, bf16[3072]{0:T(1024)(128)(2,1)S(1...) all-reduce(bf16[1536]{0:T(1024)(128)(2,1)S(1)} %dynamic-update-slic, ...), channel_id=1, replica_groups=mesh['wide'=16,'narrow'=2] {'wide','narrow'}, use_global_device_ids=true, to_apply=%add.16 | all-reduce | flops 11520 | bytes 46080
  114.2 41.7 %all_gather.56 = bf16[1536,64]{1,0:T(8,128)(2,1)S(1)} all-gather(bf16[48,64]{1,0:T(8,128)(2,1)S(1)} %copy-done.76), channel_id=1, replica_groups=mesh['wide'=16,'narrow'=2] {'wide','narrow'}, dimensions={0}, use_global_device_ids=true | all-gather | bytes 202752 | tf_op jit(solution)/shard_map/all_gather | solution.py:94
  156.0 38.8 %all_gather.53 = bf16[1536,64]{1,0:T(8,128)(2,1)S(1)} all-gather(bf16[48,64]{1,0:T(8,128)(2,1)S(1)} %copy-done.77), channel_id=1, replica_groups=mesh['wide'=16,'narrow'=2] {'wide','narrow'}, dimensions={0}, use_global_device_ids=true | all-gather | bytes 202752 | tf_op jit(solution)/shard_map/all_gather | solution.py:95
  326.6 24.0 %fusion.155 = f32[768,16,32]{2,1,0:T(8,128)} fusion(f32[16,32,768]{1,0,2:T(8,128)} %copy.162, f32[32,32,768]{1,0,2:T(8,128)} %copy.163), kind=kOutput, calls=%fused_computation.223 | convolution fusion | flops 150994944 | bytes 6291456 | tf_op jit(solution)/shard_map/jvp(tsh,bsh->bth)/dot_general | solution.py:32
  374.0 58.7 %while.65 = (s32[]{:T(128)}, f32[64,768]{1,0:T(8,128)S(1)}, f32[16,64,768]{2,1,0:T(8,128)}, f32[16]{0:T(128)S(1)}, f32[64,768]{1,0:T(8,128)S(1)}, /*index=5*/f32[16,64,768]{2,1,0:T(8,128)}, s32[]{:T(128)}, s32[]{:T(128)}) while((s32[]{:T(128)}, f32[64,768]{1,0:T(8,128)S(1)}, f32[16,64,768]{2,1,0:T(8,128)}, f32[16]{0:T(128)S(1)}, ...), condition=%wide.region_5.6_spmd.clone, body=%wide.region_4.5_spmd.clone.sunk | while | flops 294915 | bytes 1180288 | solution.py:46
  469.5 58.7 %while.64 = (s32[]{:T(128)}, f32[64,768]{1,0:T(8,128)S(1)}, f32[16,64,768]{2,1,0:T(8,128)}, f32[16]{0:T(128)S(1)}, f32[64,768]{1,0:T(8,128)S(1)}, /*index=5*/f32[16,64,768]{2,1,0:T(8,128)}, s32[]{:T(128)}, s32[]{:T(128)}) while((s32[]{:T(128)}, f32[64,768]{1,0:T(8,128)S(1)}, f32[16,64,768]{2,1,0:T(8,128)}, f32[16]{0:T(128)S(1)}, ...), condition=%wide.region_3.4_spmd.clone, body=%wide.region_2.3_spmd.clone.sunk | while | flops 294915 | bytes 1180288 | solution.py:46
  528.2 24.5 %add_bitcast_fusion.2 = f32[16,32,768]{1,0,2:T(8,128)} fusion(f32[768,16,32]{2,1,0:T(8,128)} %fusion.155, f32[16,64,768]{1,0,2:T(8,128)} %copy.167, f32[64,768]{0,1:T(8,128)S(1)} %bitcast.293, f32[64,768]{0,1:T(8,128)S(1)} %copy-done.39, f32[64,768]{0,1:T(8,128)S(1)} %get-tuple-element.747), kind=kOutput, calls=%fused_computation.77 | convolution fusion | flops 307101696 | bytes 6881280 | tf_op jit(solution)/shard_map/jvp(tnh,bnh->bth)/dot_general | solution.py:48
  682.3 23.3 %fusion.72 = f32[32,32,768]{1,0,2:T(8,128)} fusion(f32[16,32,768]{1,0,2:T(8,128)S(1)} %bitcast.275, f32[16,32,768]{1,0,2:T(8,128)S(1)} %copy-done.3), kind=kOutput, calls=%fused_computation.98 | convolution fusion | flops 150994944 | bytes 6291456 | tf_op jit(solution)/shard_map/transpose(jvp(tsh,bsh->bth))/dot_general | solution.py:32
  714.2 49.7 %while.67 = (s32[]{:T(128)}, f32[64,768]{1,0:T(8,128)S(1)}, f32[64,768]{1,0:T(8,128)S(1)}, f32[16,64,768]{2,1,0:T(8,128)}, f32[16,64,768]{2,1,0:T(8,128)}, /*ind...) while((s32[]{:T(128)}, f32[64,768]{1,0:T(8,128)S(1)}, ...), condition=%wide.region_9.10_spmd.clone, body=%wide.region_8.9_spmd.clone.sunk | while | flops 393220 | bytes 1769636 | solution.py:46
  770.9 24.2 %fusion.158 = f32[768,16,32]{2,1,0:T(8,128)} fusion(f32[768,16,64]{2,1,0:T(8,128)} %copy.178, f32[32,64,768]{1,0,2:T(8,128)} %rev.27), kind=kOutput, calls=%fused_computation.226 | convolution fusion | flops 301989888 | bytes 11010048 | tf_op jit(solution)/shard_map/transpose(jvp(snh,bsh->bnh))/dot_general | solution.py:33
  853.8 23.0 %fusion.69 = f32[32,32,768]{1,0,2:T(8,128)} fusion(f32[16,32,768]{1,0,2:T(8,128)S(1)} %bitcast.271, f32[16,32,768]{1,0,2:T(8,128)S(1)} %copy-done.4), kind=kOutput, calls=%fused_computation.97 | convolution fusion | flops 150994944 | bytes 6291456 | tf_op jit(solution)/shard_map/transpose(jvp(tsh,bsh->bth))/dot_general | solution.py:32
  883.8 50.8 %while.66 = (s32[]{:T(128)}, f32[64,768]{1,0:T(8,128)}, f32[64,768]{1,0:T(8,128)S(1)}, f32[16,64,768]{2,1,0:T(8,128)S(1)}, f32[16,64,768]{2,1,0:T(8,128)}, /*ind...) while((s32[]{:T(128)}, f32[64,768]{1,0:T(8,128)}, ...), condition=%wide.region_7.8_spmd.clone, body=%wide.region_6.7_spmd.clone.sunk | while | flops 393220 | bytes 1769636 | solution.py:46
  943.2 23.6 %fusion.157 = f32[768,16,32]{2,1,0:T(8,128)} fusion(f32[768,16,64]{2,1,0:T(8,128)} %copy.172, f32[32,64,768]{1,0,2:T(8,128)} %rev.30), kind=kOutput, calls=%fused_computation.225 | convolution fusion | flops 301989888 | bytes 11010048 | tf_op jit(solution)/shard_map/transpose(jvp(snh,bsh->bnh))/dot_general | solution.py:33
  966.9 23.5 %convolution_bitcast_fusion.1 = f32[32,64,768]{1,0,2:T(8,128)} fusion(f32[768,16,64]{2,1,0:T(8,128)S(1)} %copy-done.2, f32[16,32,768]{1,0,2:T(8,128)S(1)} %bitcast.273), kind=kOutput, calls=%fused_computation.100 | convolution fusion | flops 301989888 | bytes 11010048 | tf_op jit(solution)/shard_map/transpose(jvp(snh,bsh->bnh))/dot_general | solution.py:33
  1092.0 35.3 %fusion.7 = (f32[64,768]{0,1:T(8,128)S(1)}, f32[64,768]{0,1:T(8,128)S(1)}, f32[64,768]{0,1:T(8,128)S(1)}) fusion(f32[64,768]{0,1:T(8,128)S(1)} %copy-done.42, f32[64,768]{0,1:T(8,128)S(1)} %copy-done.20, f32[768,64]{1,0:T(8,128)} %get-tuple-element.736, f32[768,32]{1,0:T(8,128)} %copy.194, f32[32,64,768]{1,0,2:T(8,128)} %rev.35, f32[64,768]{0,1:T(8,128)} %bitcast.297, ...), kind=kOutput, calls=%fused_computation.22 | convolution fusion | flops 323862528 | bytes 12484608 | tf_op jit(solution)/shard_map/transpose(jvp(tnh,bnh->bth))/dot_general | solution.py:48
  1127.5 33.5 %fusion.11 = (f32[64,768]{0,1:T(8,128)S(1)}, f32[64,768]{0,1:T(8,128)S(1)}, f32[64,768]{0,1:T(8,128)S(1)}) fusion(f32[64,768]{0,1:T(8,128)S(1)} %copy-done.40, f32[64,768]{0,1:T(8,128)S(1)} %copy-done.23, f32[768,64]{1,0:T(8,128)S(1)} %copy-done.46, f32[768,32]{1,0:T(8,128)S(1)} %copy-done.57, f32[32,64,768]{1,0,2:T(8,128)} %rev.34, ...), kind=kOutput, calls=%fused_computation.29 | convolution fusion | flops 323862528 | bytes 12484608 | tf_op jit(solution)/shard_map/transpose(jvp(tnh,bnh->bth))/dot_general | solution.py:48
  1266.5 38.0 %all-reduce.26 = (f32[768]{0:T(1024)S(1)}, f32[768]{0:T(1024)S(1)}, f32[3072]{0:T(1024)S(1)}, f32[1536]{0:T(1024)S(1)}, f32[1536]{0:T(1024)S(1)}, /*index=5*/f32...) all-reduce(f32[768]{0:T(1024)S(1)} %get-tuple-element.623, ...), channel_id=6, replica_groups=mesh['wide'=16,'narrow'=2] {'wide','narrow'}, use_global_device_ids=true, to_apply=%region_17.18.clone | all-reduce | flops 11520 | bytes 92160
  1313.2 44.9 %reduce-scatter.18.cloned.1.call-done = f32[48,64]{1,0:T(8,128)} async-done(((f32[1536,64]{1,0:T(8,128)}), f32[48,64]{1,0:T(8,128)}) %reduce-scatter.18.cloned.1.call-update) | async-done | bytes 12304 | tf_op jit(solution)/shard_map/reduce_scatter | solution.py:220
  1358.1 100.3 %reduce-scatter.20.cloned.1.call-done = f32[48,64]{1,0:T(8,128)} async-done(((f32[1536,64]{1,0:T(8,128)}), f32[48,64]{1,0:T(8,128)}) %reduce-scatter.20.cloned.1.call-update) | async-done | bytes 12304 | tf_op jit(solution)/shard_map/reduce_scatter | solution.py:221
  1458.4 112.1 %reduce-scatter.10.cloned.1.call-done = f32[24,1536]{1,0:T(8,128)} async-done(((f32[768,1536]{1,0:T(8,128)}), f32[24,1536]{1,0:T(8,128)}) %reduce-scatter.10.cloned.1.call-update) | async-done | bytes 147472 | tf_op jit(solution)/shard_map/reduce_scatter | solution.py:212
  1570.6 113.1 %reduce-scatter.14.cloned.1.call-done = f32[48,768]{1,0:T(8,128)} async-done(((f32[1536,768]{1,0:T(8,128)}), f32[48,768]{1,0:T(8,128)}) %reduce-scatter.14.cloned.1.call-update) | async-done | bytes 147472 | tf_op jit(solution)/shard_map/reduce_scatter | solution.py:213
  1683.7 141.1 %reduce-scatter.8.cloned.1.call-done = f32[24,3072]{1,0:T(8,128)} async-done(((f32[768,3072]{1,0:T(8,128)}), f32[24,3072]{1,0:T(8,128)}) %reduce-scatter.8.cloned.1.call-update) | async-done | bytes 294928 | tf_op jit(solution)/shard_map/reduce_scatter | solution.py:211
  1824.8 213.7 %reduce-scatter.12.cloned.1.call-done = f32[96,1536]{1,0:T(8,128)} async-done(((f32[3072,1536]{1,0:T(8,128)}), f32[96,1536]{1,0:T(8,128)}) %reduce-scatter.12.cloned.1.call-update) | async-done | bytes 589840 | tf_op jit(solution)/shard_map/reduce_scatter | solution.py:181
  (562 shorter events, 867.7 us)
Async XLA Ops:
  7.2 293.3 %all-gather.5.cloned.1.call-start = ((), (), s32[]{:S(2)}) async-start(), calls=%async_computation.7 | async-start | bytes 2433024 | tf_op jit(solution)/shard_map/all_gather | solution.py:83
  7.9 622.5 %all-gather.7.cloned.1.call-start = ((), (), s32[]{:S(2)}) async-start(), calls=%async_computation.8 | async-start | bytes 4866048 | tf_op jit(solution)/shard_map/all_gather | solution.py:82
  8.7 629.0 %all-gather.9.cloned.1.call-start = ((), (), s32[]{:S(2)}) async-start(), calls=%async_computation.9 | async-start | bytes 9732096 | tf_op jit(solution)/shard_map/all_gather | solution.py:84
  9.4 640.0 %all-gather.11.cloned.1.call-start = ((), (), s32[]{:S(2)}) async-start(), calls=%async_computation.10 | async-start | bytes 2433024 | tf_op jit(solution)/shard_map/all_gather | solution.py:85
  10.0 1303.3 %reduce-scatter.16.cloned.1.call-start = ((), (), s32[]{:S(2)}) async-start(), calls=%async_computation.15 | async-start | bytes 811008 | tf_op jit(solution)/shard_map/reduce_scatter | solution.py:218
  10.0 258.6 %copy-start.55 = (s32[32,32]{1,0:T(8,128)}, s32[32,32]{1,0:T(8,128)S(1)}, u32[]{:S(2)}) copy-start(s32[32,32]{1,0:T(8,128)S(1)} %iota_subtract_fusion) | copy-start | bytes 12292
  56.4 138.5 %copy-start.5 = (f32[1536,64]{1,0:T(8,128)}, f32[1536,64]{1,0:T(8,128)S(1)}, u32[]{:S(2)}) copy-start(f32[1536,64]{1,0:T(8,128)S(1)} %convert_element_type.86) | copy-start | bytes 1179652
  101.2 93.7 %copy-start.66 = (f32[768]{0:T(1024)}, f32[768]{0:T(1024)S(1)}, u32[]{:S(2)}) copy-start(f32[768]{0:T(1024)S(1)} %get-tuple-element.750) | copy-start | bytes 9220
  101.2 93.7 %copy-start.68 = (f32[768]{0:T(1024)}, f32[768]{0:T(1024)S(1)}, u32[]{:S(2)}) copy-start(f32[768]{0:T(1024)S(1)} %get-tuple-element.751) | copy-start | bytes 9220
  102.5 563.3 %copy-start.19 = (f32[64,768]{0,1:T(8,128)}, f32[64,768]{0,1:T(8,128)S(1)}, u32[]{:S(2)}) copy-start(f32[64,768]{0,1:T(8,128)S(1)} %get-tuple-element.722) | copy-start | bytes 589828
  102.5 734.7 %copy-start.21 = (f32[64,768]{0,1:T(8,128)}, f32[64,768]{0,1:T(8,128)S(1)}, u32[]{:S(2)}) copy-start(f32[64,768]{0,1:T(8,128)S(1)} %get-tuple-element.747) | copy-start | bytes 589828
  113.0 517.4 %copy-start.62 = (f32[768]{0:T(1024)}, f32[768]{0:T(1024)S(1)}, u32[]{:S(2)}) copy-start(f32[768]{0:T(1024)S(1)} %convert_element_type.81) | copy-start | bytes 9220
  113.0 517.4 %copy-start.58 = (f32[768]{0:T(1024)}, f32[768]{0:T(1024)S(1)}, u32[]{:S(2)}) copy-start(f32[768]{0:T(1024)S(1)} %convert_element_type.80) | copy-start | bytes 9220
  113.2 517.2 %copy-start.60 = (f32[512]{0:T(512)}, f32[512]{0:T(512)S(1)}, u32[]{:S(2)}) copy-start(f32[512]{0:T(512)S(1)} %broadcast_multiply_fusion) | copy-start | bytes 6148
  114.2 516.3 %copy-start.64 = (f32[512]{0:T(512)}, f32[512]{0:T(512)S(1)}, u32[]{:S(2)}) copy-start(f32[512]{0:T(512)S(1)} %fusion.137) | copy-start | bytes 6148
  114.2 535.2 %copy-start.72 = (f32[1536]{0:T(1024)}, f32[1536]{0:T(1024)S(1)}, u32[]{:S(2)}) copy-start(f32[1536]{0:T(1024)S(1)} %convert_element_type.90) | copy-start | bytes 18436
  300.4 337.2 %copy-start.78 = (f32[3072]{0:T(1024)}, f32[3072]{0:T(1024)S(1)}, u32[]{:S(2)}) copy-start(f32[3072]{0:T(1024)S(1)} %convert_element_type.91) | copy-start | bytes 36868
  467.5 60.6 %copy-start.44 = (f32[768,64]{1,0:T(8,128)S(1)}, f32[768,64]{1,0:T(8,128)}, u32[]{:S(2)}) copy-start(f32[768,64]{1,0:T(8,128)} %copy-done.43) | copy-start | bytes 589828
  1165.2 193.0 %reduce-scatter.18.cloned.1.call-start = ((), (), s32[]{:S(2)}) async-start(), calls=%async_computation.16 | async-start | bytes 811008 | tf_op jit(solution)/shard_map/reduce_scatter | solution.py:220
  1168.6 289.9 %reduce-scatter.20.cloned.1.call-start = ((), (), s32[]{:S(2)}) async-start(), calls=%async_computation.17 | async-start | bytes 811008 | tf_op jit(solution)/shard_map/reduce_scatter | solution.py:221
  1209.1 361.4 %reduce-scatter.10.cloned.1.call-start = ((), (), s32[]{:S(2)}) async-start(), calls=%async_computation.12 | async-start | bytes 4866048 | tf_op jit(solution)/shard_map/reduce_scatter | solution.py:212
  1219.1 464.6 %reduce-scatter.14.cloned.1.call-start = ((), (), s32[]{:S(2)}) async-start(), calls=%async_computation.14 | async-start | bytes 4866048 | tf_op jit(solution)/shard_map/reduce_scatter | solution.py:213
  1222.8 602.0 %reduce-scatter.8.cloned.1.call-start = ((), (), s32[]{:S(2)}) async-start(), calls=%async_computation.11 | async-start | bytes 9732096 | tf_op jit(solution)/shard_map/reduce_scatter | solution.py:211
  1243.0 795.5 %reduce-scatter.12.cloned.1.call-start = ((), (), s32[]{:S(2)}) async-start(), calls=%async_computation.13 | async-start | bytes 19464192 | tf_op jit(solution)/shard_map/reduce_scatter | solution.py:181
  (86 other events, 1617.8 us)
Sparse Core Ops, SparseCore 0:
  10.9 60.0 all-gather.4
  73.9 65.1 all-gather.6
  142.0 82.0 all-gather.8
  226.8 55.8 all-gather.10
  1165.3 92.6 reduce-scatter.15
  1263.5 94.5 reduce-scatter.17
  1363.8 94.5 reduce-scatter.19
  1464.5 106.0 reduce-scatter.9
  1577.5 106.1 reduce-scatter.13
  1690.0 134.7 reduce-scatter.7
  1832.9 205.5 reduce-scatter.11
where the time goes:
time: 2060 us; the launch traced here: 2050 us
  waiting for transfers between devices  728 us (35%)
  matrix products  574 us (28%)
  local copies, waits for them, and re-layouts  317 us (15%)
  other arithmetic  209 us (10%)
  blocking collectives  201 us (10%)
    reduce_scatter x1, waiting for transfers between devices, per_device(): lax.psum_scatter(grad_w_proj, ('wide', 'narrow'), scatter_dimension=0, ti...  214 us
    dot_general x6, matrix products, ssm_half(): jnp.einsum('tnh,bnh->bth', lead, entering, precision=lax.Precision.HIGHEST)  149 us
    reduce_scatter x1, waiting for transfers between devices, per_device(): lax.psum_scatter(rest[0], ('wide', 'narrow'), scatter_dimension=0, tiled=...  141 us
    dot_general x6, matrix products, ssm_half(): jnp.einsum('tsh,bsh->bth', toeplitz, blocks, precision=lax.Precision.HIGH...  125 us
    dot_general x6, matrix products, ssm_half(): jnp.einsum('snh,bsh->bnh', powers[::-1], blocks, precision=lax.Precision....  124 us
    reduce_scatter x1, waiting for transfers between devices, per_device(): lax.psum_scatter(rest[2], ('wide', 'narrow'), scatter_dimension=0, tiled=...  113 us
    reduce_scatter x1, waiting for transfers between devices, per_device(): lax.psum_scatter(rest[1], ('wide', 'narrow'), scatter_dimension=0, tiled=...  112 us
    reduce_scatter x1, waiting for transfers between devices, per_device(): lax.psum_scatter(rest[10], ('wide', 'narrow'), scatter_dimension=0, tiled...  100 us
  transfers between devices with their start and end apart: 11, of which 6 were waited for; matrix products, arithmetic and copies ran while one was open for 28% of the time, Pallas kernels for 0%

commit v1 on v0

v1 whole, which is shorter than its diff:
```python
import functools

import jax
import jax.numpy as jnp
from jax import lax
from jax.experimental import pallas as pl
from jax.experimental.pallas import tpu as pltpu
from jax.sharding import PartitionSpec as P

T = 32
NB = 32
f32, bf16 = jnp.float32, jnp.bfloat16

def iota(shape, dim): return lax.broadcasted_iota(jnp.int32, shape, dim)

def take(x, index, axis):
    return jnp.take_along_axis(x, index, axis=axis, mode="promise_in_bounds")

def turn(x, sign):
    row, lane = iota((8, 128), 0), iota((8, 128), 1)
    return take(x, (lane - sign * 32 * (row & 3)) & 127, 1)

def skew(x):
    row, chunk = iota((8, 128), 0), iota((8, 128), 1) >> 5
    return take(x, (row & 4) | ((chunk - row) & 3), 0)

def swap_chunks(x):
    return turn(skew(turn(x, 1)), -1)

def to_blocks(x):
    z = [swap_chunks(x[:, 128 * j:128 * j + 128]) for j in range(8)]
    low = iota((8, 128), 0) < 4
    left = [jnp.where(low, z[2 * i], pltpu.roll(z[2 * i + 1], 4, 0)) for i in range(4)]
    right = [jnp.where(low, pltpu.roll(z[2 * i], 4, 0), z[2 * i + 1]) for i in range(4)]
    return jnp.concatenate([jnp.concatenate(left, 0), jnp.concatenate(right, 0)], 1)

def from_blocks(y):
    low = iota((8, 128), 0) < 4
    out = []
    for i in range(4):
        l, r = y[8 * i:8 * i + 8, :128], y[8 * i:8 * i + 8, 128:]
        for z in (jnp.where(low, l, pltpu.roll(r, 4, 0)), jnp.where(low, pltpu.roll(l, 4, 0), r)):
            out.append(swap_chunks(z))
    return jnp.concatenate(out, 1)

def diagonal(y, half):
    part = y[:, 128 * half:128 * half + 128]
    chunk = iota(part.shape, 1) >> 5
    return jnp.concatenate([jnp.where(chunk == c, part, jnp.zeros_like(part)) for c in range(4)], 0)

def dot(a, b, dims=((1,), (0,))):
    return lax.dot_general(a, b, (dims, ((), ())), preferred_element_type=f32)

def two(parts): return jnp.concatenate(parts, 1)

def shift(x, k, back):
    n = 128 - k if back else k
    return two([pltpu.roll(x[:, :128], n, 1), pltpu.roll(x[:, 128:], n, 1)])

def spread(x3):
    r = ((iota((24, 256), 0) & 7) == (iota((24, 256), 1) >> 5)).astype(f32).astype(bf16)
    return dot(x3, r, ((0,), (0,)))

def roll_halves(x, amount, **kw):
    return two([pltpu.roll(x[:, :128], amount, 1, **kw), pltpu.roll(x[:, 128:], amount, 1, **kw)])

def lag_rows(row, amount):
    row = roll_halves(jnp.broadcast_to(row, (8, 256)), amount)
    return roll_halves(jnp.concatenate([row] * 4, 0), 0, stride=1, stride_axis=0)

def gelu_parts(x):
    k = 0.7978845608028654
    t = jnp.tanh(k * (x + 0.044715 * (x * x * x)))
    return t, k

def gelu(x):
    t, k = gelu_parts(x)
    return 0.5 * x * (1.0 + t)

def gelu_grad(x):
    t, k = gelu_parts(x)
    return 0.5 * (1.0 + t) + 0.5 * x * (1.0 - t * t) * k * (1.0 + 3 * 0.044715 * x * x)

def halved(x):
    hi = x.astype(bf16)
    return hi, (x - hi.astype(f32)).astype(bf16)

def each(f, *lists):
    return [f(*items) for items in zip(*lists)]

def scans(es, fs, mask_ref, first, back):
    for i in range(4):
        moved = each(lambda e: shift(e, 1 << i, back), es)
        m = mask_ref[first + i:first + i + 1, :]
        es = each(lambda e, f, s: e + (f * m) * s, es, fs, moved)
        if i < 3: fs = each(lambda f: f * f, fs)
    return es

def halves_dot(lhs, rights, width):
    return two([dot(lhs[:, width * h:width * h + width], rights[h]) for h in range(2)])

def fwd_groups(rev, xs, d3s, w3s, drows, wrows, skips, masks):
    vs = each(gelu, xs)
    vys = each(lambda v: to_blocks(v).astype(bf16), vs)
    d1s, w1s = each(spread, d3s), each(spread, w3s)
    pos = iota((64, 256), 1) & 31
    p = (pos if rev else 31 - pos).astype(f32)
    pts = each(lambda d1: jnp.exp(p * d1), d1s)
    krows = each(lambda w1, pt: jnp.sum(w1 * pt, axis=0, keepdims=True), w1s, pts)
    row, lane = iota((T, 256), 0), iota((T, 256), 1) & 31
    valid = (lane >= row if rev else row >= lane)
    toeps = each(lambda k: jnp.where(valid, lag_rows(k, 0 if rev else 97), 0.0), krows)
    lhss = each(lambda pt, t: jnp.concatenate([pt, t], 0).astype(bf16), pts, toeps)
    boths = each(lambda lhs, vy: halves_dot(lhs, [diagonal(vy, h) for h in range(2)], 128), lhss, vys)
    fs = each(lambda d1: jnp.exp(float(T) * d1), d1s)
    hs = scans([b[:64] for b in boths], fs, masks, 0, rev)
    hes = each(lambda h: masks[0:1, :] * shift(h, 1, rev), hs)
    col = iota((T, 512), 0)
    q = (T - col if rev else col + 1).astype(f32)
    leads = each(lambda wrow, drow: (wrow * jnp.exp(q * drow)).astype(bf16), wrows, drows)
    outers = each(lambda lead, he: halves_dot(lead, [diagonal(he.astype(bf16), h) for h in range(2)], 256), leads, hes)
    return each(lambda b, o, skip, v: from_blocks(b[64:] + o) + skip * v, boths, outers, skips, vs), hes

def fwd_kernel(groups, unroll, dir_ref, x_ref, d3_ref, w3_ref, drow_ref, wrow_ref, skip_ref, mask_ref, out_ref, enter_ref):
    def body(rev, i, _):
        gs = [i * unroll + u for u in range(unroll)]
        rows = [pl.ds(pl.multiple_of(g * 8, 8), 8) for g in gs]
        pick = lambda ref, at: [ref[a] for a in at]
        pickr = lambda ref: [ref[r, :] for r in rows]
        pickf = lambda ref: [ref[pl.ds(g, 1), :] for g in gs]
        outs, enters = fwd_groups(rev, pickr(x_ref), pick(d3_ref, gs), pick(w3_ref, gs), pickf(drow_ref), pickf(wrow_ref), pickr(skip_ref), mask_ref)
        for g, r, o, e in zip(gs, rows, outs, enters):
            out_ref[r, :] = o
            enter_ref[g] = e
        return 0
    for rev in (False, True):
        @pl.when(dir_ref[0] == int(rev))
        def _(rev=rev):
            lax.fori_loop(0, groups // unroll, functools.partial(body, rev), 0)

def flip_rows(y):
    row = iota((8, 128), 0)
    tiles = [[take(y[8 * i : 8 * i + 8, 128 * h : 128 * h + 128], 7 - row, 0) for h in range(2)] for i in (3, 2, 1, 0)]
    return jnp.concatenate([two(t) for t in tiles], 0)

def bwd_groups(rev, at_group, xs, gms, hes, d3s, w3s, drows, skips, masks):
    vs = each(gelu, xs)
    vys = each(lambda v: to_blocks(v).astype(bf16), vs)
    gfs = each(to_blocks, gms)
    gys = each(lambda g: g.astype(bf16), gfs)
    gyrs = each(lambda g: flip_rows(g).astype(bf16), gfs)
    d1s, w1s = each(spread, d3s), each(spread, w3s)
    pos = iota((64, 256), 1) & 31
    p = (pos if rev else 31 - pos).astype(f32)
    pts = each(lambda d1: jnp.exp(p * d1), d1s)
    ppts = each(lambda pt: p * pt, pts)
    rs = each(lambda d1: jnp.exp((31.0 - p) * d1), d1s)
    ats = each(lambda r, d1: r * jnp.exp(d1), rs, d1s)
    apts = each(lambda at: (32.0 - p) * at, ats)
    krows = each(lambda w1, r: jnp.sum(w1 * r, axis=0, keepdims=True), w1s, rs)
    row, lane = iota((T, 256), 0), iota((T, 256), 1) & 31
    ok2 = (row >= lane if rev else lane >= row)
    toeps = each(lambda k: jnp.where(ok2, lag_rows(k, 97 if rev else 0), 0.0), krows)
    lhs_v = each(lambda ppt: ppt.astype(bf16), ppts)
    lhs_g = each(lambda at, apt, t: jnp.concatenate([at, apt, t], 0).astype(bf16), ats, apts, toeps)
    bdvs = each(lambda vy: [diagonal(vy, h) for h in range(2)], vys)
    bdgs = each(lambda gy: [diagonal(gy, h) for h in range(2)], gys)
    ees = each(lambda l, b: halves_dot(l, b, 128), lhs_v, bdvs)
    qqs = each(lambda l, b: halves_dot(l, b, 128), lhs_g, bdgs)
    ms = each(lambda gy, b: two([dot(gy[:, 128 * h:128 * h + 128], b[h], ((1,), (1,))) for h in range(2)]), gyrs, bdvs)
    fs = each(lambda d1: jnp.exp(float(T) * d1), d1s)
    n = len(xs)
    downs = scans(each(lambda w1, q: w1 * q[:64], w1s, qqs), fs, masks, 4, not rev)
    des = each(lambda h: masks[4:5, :] * shift(h, 1, not rev), downs)
    col = iota((T, 512), 0)
    pw = (col if rev else 31 - col).astype(f32)
    p2s = each(lambda drow: jnp.exp(pw * drow).astype(bf16), drows)
    dvs = each(lambda qq, p2, de: qq[128:] + halves_dot(p2, [diagonal(de.astype(bf16), h) for h in range(2)], 256), qqs, p2s, des)
    ok = (lane + row >= 31 if rev else lane + row <= 31)
    ms = each(lambda m: roll_halves(jnp.where(ok, m, 0.0), 0, stride=1, stride_axis=0), ms)
    dks = each(lambda m: jnp.sum(m, axis=0, keepdims=True), ms)
    if rev: dks = each(lambda dk: roll_halves(jnp.broadcast_to(dk, (8, 256)), 97)[:1], dks)
    zws = each(lambda he, qq, pt, dk: he * qq[:64] + pt * dk, hes, qqs, pts, dks)
    zds = each(lambda w1, he, qq, ppt, dk, de, ee, f: w1 * (he * qq[64:128] + ppt * dk) + de * (ee + float(T) * f * he), w1s, hes, qqs, ppts, dks, des, ees, fs)
    total = 0.0
    for u, (zw, zd) in enumerate(zip(zws, zds)):
        column = 8 * (at_group + u) + (iota((256, 128), 0) >> 5)
        ones = (iota((256, 128), 1) == column).astype(f32).astype(bf16)
        both = dot(jnp.concatenate([*halved(zw), *halved(zd)], 0), ones)
        total = total + jnp.concatenate([both[:64] + both[64:128], both[128:192] + both[192:]], 0)
    dvals = each(lambda dv, skip, gm, x: (from_blocks(dv) + skip * gm) * gelu_grad(x), dvs, skips, gms, xs)
    dskips = each(lambda gm, v: jnp.sum(gm * v, axis=1, keepdims=True), gms, vs)
    return dvals, total, dskips

def bwd_kernel(groups, unroll, dir_ref, x_ref, gm_ref, enter_ref, d3_ref, w3_ref, drow_ref, skip_ref, mask_ref, gv_ref, grads_ref, dskip_ref, dbias_ref):
    grads_ref[...] = jnp.zeros_like(grads_ref)
    def body(rev, i, _):
        gs = [i * unroll + u for u in range(unroll)]
        rows = [pl.ds(pl.multiple_of(g * 8, 8), 8) for g in gs]
        pick = lambda ref: [ref[a] for a in gs]
        pickr = lambda ref: [ref[r, :] for r in rows]
        pickf = lambda ref: [ref[pl.ds(g, 1), :] for g in gs]
        gms = pickr(gm_ref)
        dvals, total, dskips = bwd_groups(rev, i * unroll, pickr(x_ref), gms, pick(enter_ref), pick(d3_ref), pick(w3_ref), pickf(drow_ref), pickr(skip_ref), mask_ref)
        grads_ref[...] += total
        for r, a, c in zip(rows, dvals, dskips):
            dskip_ref[r, :] = c
            dbias_ref[r, :] = jnp.sum(a.astype(bf16).astype(f32), axis=1, keepdims=True)
        for u in range(0, unroll, 2):
            gv_ref[pl.ds(pl.multiple_of((i * unroll + u) * 8, 16), 16), :] = jnp.concatenate(dvals[u : u + 2], 0).astype(bf16)
        return 0
    for rev in (False, True):
        @pl.when(dir_ref[0] == int(rev))
        def _(rev=rev):
            lax.fori_loop(0, groups // unroll, functools.partial(body, rev), 0)

def specs(cb, first):
    g = cb // 8
    rows = lambda lanes: pl.BlockSpec((cb, lanes), lambda i: (i + first, 0))
    per = lambda a, b: pl.BlockSpec((g, a, b), lambda i: (i + first, 0, 0))
    flat = lambda lanes: pl.BlockSpec((g, lanes), lambda i: (i + first, 0))
    return rows, per, flat

def mix_call(kernel, name, out_shape, in_specs, out_specs, steps, done, args):
    n = len(args)
    if done is None:
        body, aliases, done = kernel, {}, ()
    else:
        body = lambda *refs: kernel(*refs[:n], *refs[n + len(done):])
        aliases = {n + i: i for i in range(len(done))}
        in_specs = in_specs + [pl.BlockSpec(memory_space=pl.ANY)] * len(done)
    return pl.pallas_call(
        body,
        out_shape=out_shape,
        grid=(steps,),
        in_specs=in_specs,
        out_specs=out_specs,
        input_output_aliases=aliases,
        compiler_params=pltpu.CompilerParams(vmem_limit_bytes=60 << 20),
        name=name,
    )(*args, *done)

MASKS = pl.BlockSpec((8, 256), lambda i: (0, 0))
SCALAR = pl.BlockSpec(memory_space=pltpu.SMEM)

def ssm_fwd(direction, x, d3, w3, drow, wrow, skip, masks, part=0, parts=1, done=None, cb=64, unroll=8):
    c, tok = x.shape
    steps = c // cb // parts
    rows, per, flat = specs(cb, part * steps)
    return mix_call(
        functools.partial(fwd_kernel, cb // 8, unroll),
        f"mix_forward_{part}",
        (jax.ShapeDtypeStruct((c, tok), f32), jax.ShapeDtypeStruct((c // 8, 64, 256), f32)),
        [SCALAR, rows(tok), per(24, 64), per(24, 64), flat(512), flat(512), rows(1), MASKS],
        (rows(tok), per(64, 256)),
        steps, done, (direction, x, d3, w3, drow, wrow, skip, masks),
    )

def ssm_bwd(direction, x, gm, enter, d3, w3, drow, skip, masks, part=0, parts=1, done=None, cb=128, unroll=8):
    c, tok = x.shape
    steps = c // cb // parts
    first = part * steps
    rows, per, flat = specs(cb, first)
    return mix_call(
        functools.partial(bwd_kernel, cb // 8, unroll),
        f"mix_backward_{part}",
        (jax.ShapeDtypeStruct((c, tok), bf16), jax.ShapeDtypeStruct((128, c), f32), jax.ShapeDtypeStruct((c, 1), f32), jax.ShapeDtypeStruct((c, 1), f32)),
        [SCALAR, rows(tok), rows(tok), per(64, 256), per(24, 64), per(24, 64), flat(512), rows(1), MASKS],
        (rows(tok), pl.BlockSpec((128, cb), lambda i: (0, i + first)), rows(1), rows(1)),
        steps, done, (direction, x, gm, enter, d3, w3, drow, skip, masks),
    )

def thirds(x):
    hi = x.astype(bf16)
    rest = x - hi.astype(f32)
    mid = rest.astype(bf16)
    lo = (rest - mid.astype(f32)).astype(bf16)
    c = x.shape[0]
    return jnp.concatenate([a.reshape(c // 8, 8, 64) for a in (hi, mid, lo)], 1)

def block_masks(labels, rev):
    idx = jnp.arange(16)[None, :]
    def reach(k, back):
        other = jnp.roll(labels, -k if back else k, axis=1)
        inside = (idx + k < 16) if back else (idx >= k)
        return (inside & (other == labels)).astype(f32).reshape(32)
    ahead = jnp.stack([reach(k, False) for k in (1, 2, 4, 8)])
    behind = jnp.stack([reach(k, True) for k in (1, 2, 4, 8)])
    both = jnp.where(rev, jnp.concatenate([behind, ahead]), jnp.concatenate([ahead, behind]))
    return jnp.tile(both, (1, 8))


ROUNDS = (
    {"y": "own", "z": "own", "x": "own", "o": "own", "m": "own"},
    {"z": (0, "m"), "m": (0, "z"), "y": (0, "x"), "x": (0, "z"), "o": (0, "y")},
    {"x": (1, "z"), "m": (1, "z"), "y": (1, "z"), "z": (1, "m"), "o": (1, "z")},
    {"z": (0, "y"), "y": (2, "z"), "m": (2, "x"), "x": (2, "z"), "o": (0, "z")},
    {"x": (3, "y"), "o": (3, "x"), "y": (2, "x"), "z": (1, "y")},
)
PERMS = {
    "x": [(w, w ^ 1) for w in range(16)],
    "y": [(w, w ^ 2) for w in range(16)],
    "z": [(w, w ^ 4) for w in range(16)],
    "m": [(w, w + 4) for w in range(4, 8)] + [(w, w - 4) for w in range(8, 12)],
}


def trace_rounds():
    end, mid = {"own": (0, 0, 0)}, {"own": (0, 0, 1)}
    for r, sends in enumerate(ROUNDS):
        new_end, new_mid = {}, {}
        for d, bit in (("x", 0), ("y", 1)):
            for held, new in ((end, new_end), (mid, new_mid)):
                item = list(held[sends[d]])
                item[bit] ^= 1
                new[(r, d)] = tuple(item)
        new_end[(r, "z")], new_mid[(r, "z")] = mid[sends["z"]], end[sends["o"]]
        if "m" in sends:
            dx, dy, layer = mid[sends["m"]]
            new_end[(r, "m")], new_mid[(r, "m")] = None, (dx, dy, 3 - layer)
        end.update(new_end)
        mid.update(new_mid)

    def firsts(held):
        seen, first = set(), {}
        for slot, item in held.items():
            first[slot] = item is not None and item not in seen
            seen.add(item)
        return first

    return end, mid, firsts(end), firsts(mid)


END, MID, FIRST_END, FIRST_MID = trace_rounds()
SLOTS = tuple(END)


def at_end():
    layer = lax.axis_index("wide") >> 2
    return (layer == 0) | (layer == 3)


def owner(slot):
    w = lax.axis_index("wide")
    x, y, layer = w & 1, (w >> 1) & 1, w >> 2

    def of(held):
        dx, dy, z = held[slot] or (0, 0, 0)
        return jnp.where(layer >= 2, 3 - z, z) * 4 + (y ^ dy) * 2 + (x ^ dx)

    return jnp.where(at_end(), of(END), of(MID))


def is_first(slot):
    return jnp.where(at_end(), int(FIRST_END[slot]), int(FIRST_MID[slot]))


def core_index():
    return lax.axis_index("narrow") & 1


def within_half(w, rows):
    return pl.multiple_of((w & 7) * rows, 16)


ANY = pl.BlockSpec(memory_space=pl.ANY)
HBM = pl.BlockSpec(memory_space=pltpu.HBM)
VM = pl.BlockSpec(memory_space=pltpu.VMEM)


def params(mib=60):
    return pltpu.CompilerParams(vmem_limit_bytes=mib << 20)


def shape(dims, dtype):
    return jax.ShapeDtypeStruct(dims, dtype)


def ones_where(condition):
    return jnp.where(condition, 1.0, 0.0).astype(bf16)


def pack_kernel(up, value, proj, out, rate, in_map, out_map, vectors, keep, send, rows):
    def lanes(n, first):
        return ones_where(iota((n, 256), 1) == iota((n, 256), 0) + first)

    rows[...] = jnp.zeros((16, 48), f32)
    for k in range(6):
        rows[k : k + 1, :] = vectors[:, 48 * k : 48 * k + 48]
    for k, n in enumerate((24, 24, 24, 16)):
        rows[6 + k : 7 + k, :n] = vectors[:, 288 + 24 * k : 288 + 24 * k + n]
    small = dot(rows[...].astype(bf16), lanes(16, 192), ((0,), (0,)))
    for k, ref in enumerate((rate, in_map, out_map)):
        small = small + dot(ref[...], lanes(64, 64 * k))
    for core in range(2):

        @pl.when(core_index() == core)
        def _(core=core):
            for ref, half in ((keep, core), (send, 1 - core)):
                a = up[...].astype(f32)
                for q in range(2):
                    ref[24 * q : 24 * q + 24, :] = a[:, 1536 * half + 768 * q : 1536 * half + 768 * q + 768]
                ref[48:72, :] = value[...].astype(f32)[:, 768 * half : 768 * half + 768]
                ref[72:168, :] = proj[...].astype(f32)[:, 768 * half : 768 * half + 768]
                b = out[...].astype(f32)[:, 384 * half : 384 * half + 384]
                ref[168:192, :384] = b[:24]
                ref[168:192, 384:] = b[24:]
                for j in range(3):
                    ref[192:208, 256 * j : 256 * j + 256] = small[16 * j : 16 * j + 16, :]


def pack(*shards):
    return pl.pallas_call(
        pack_kernel,
        out_shape=(shape((208, 768), f32),) * 2,
        in_specs=[VM] * len(shards),
        out_specs=(VM, VM),
        scratch_shapes=[pltpu.VMEM((16, 48), f32)],
        compiler_params=params(),
        name="pack_shards",
    )(*shards)


def merge_kernel(keep, recv, blob):
    for core in range(2):

        @pl.when(core_index() == core)
        def _(core=core):
            lo, hi = (keep, recv) if core == 0 else (recv, keep)

            def both(a, n):
                return jnp.concatenate([lo[a : a + n, :], hi[a : a + n, :]], 0)

            for q in range(2):
                blob[48 * q : 48 * q + 48, :] = both(24 * q, 24).astype(bf16)
            blob[96:144, :] = both(48, 24).astype(bf16)
            s = [ref[192:208, 256 * j : 256 * j + 256] for ref in (lo, hi) for j in range(3)]
            for j in range(3):
                blob[144:176, 256 * j : 256 * j + 256] = jnp.concatenate(s[2 * j : 2 * j + 2], 0).astype(bf16)
            blob[176:368, :] = both(72, 96).astype(bf16)
            for k, ref in enumerate((lo, hi)):
                rows = jnp.concatenate([ref[168:192, :384], ref[168:192, 384:]], 0)
                blob[368:416, 384 * k : 384 * k + 384] = rows.astype(bf16)


def merge(keep, recv):
    return pl.pallas_call(
        merge_kernel,
        out_shape=shape((416, 768), bf16),
        in_specs=[VM, VM],
        out_specs=VM,
        compiler_params=params(),
        name="merge_pair",
    )(keep, recv)


def together(*trees):
    return lax.optimization_barrier(trees)


def gather_rounds(own, work, state=None):
    held = {"own": own}
    end = at_end()
    for r, sends in enumerate(ROUNDS):
        blocks = {}
        for d in "xyzm":
            if d in sends:
                block = held[sends[d]]
                if d == "z" and sends["z"] != sends["o"]:
                    block = jnp.where(end, held[sends["o"]], block)
                blocks[d] = block
        blocks, state = together(blocks, state)
        came = {d: lax.ppermute(block, "wide", PERMS[d]) for d, block in blocks.items()}
        state = work[r](state)
        if r == len(ROUNDS) - 1:
            early = dict(held)
            early[sends["x"]] = blocks["x"]
            placed = place_all(tuple(early), tuple(early.values()))
            came, placed, state = together(came, placed, state)
            late = {(r, d): block for d, block in came.items()}
            return place_all(tuple(late), tuple(late.values()), placed), state
        came, state = together(came, state)
        held.update({(r, d): block for d, block in came.items()})


def place_kernel(slots, pieces, outs, held, *refs):
    n = len(slots)
    blocks, refs = refs[:n], refs[n + held :]
    dests, (buf, in_sem, out_sem) = refs[:outs], refs[outs:]

    def each_slot(act):
        for i, slot in enumerate(slots):
            if FIRST_END[slot] and FIRST_MID[slot]:
                act(i, owner(slot))
            else:
                pl.when(is_first(slot) == 1)(functools.partial(act, i, owner(slot)))

    def load(i):
        return pltpu.make_async_copy(blocks[i], buf.at[i], in_sem.at[i])

    def stores(i, w):
        mine = (w >> 3) == core_index()
        for src, which, dst in pieces:

            def go(at, src=src, dst=dst):
                pltpu.make_async_copy(buf.at[(i,) + src], dests[at].at[dst(w)], out_sem.at[i]).start()

            if isinstance(which, int):
                go(which)
            else:
                pl.when(mine)(functools.partial(go, which[0]))
                pl.when(jnp.logical_not(mine))(functools.partial(go, which[1]))

    def load_start(i, w):
        load(i).start()

    def pass_on(i, w):
        load(i).wait()
        stores(i, w)

    def finish(i, w):
        pltpu.make_async_copy(blocks[i], buf.at[i], out_sem.at[i]).wait()

    for act in (load_start, pass_on, finish):
        each_slot(act)


def place(slots, blocks, pieces, out_shapes, done, name):
    n, held = len(slots), len(done)
    return pl.pallas_call(
        functools.partial(place_kernel, slots, pieces, len(out_shapes), held),
        out_shape=out_shapes,
        in_specs=[ANY] * (n + held),
        out_specs=tuple(ANY for _ in out_shapes),
        input_output_aliases={n + k: k for k in range(held)},
        scratch_shapes=[
            pltpu.VMEM((n,) + blocks[0].shape, bf16),
            pltpu.SemaphoreType.DMA((n,)),
            pltpu.SemaphoreType.DMA((n,)),
        ],
        compiler_params=params(),
        name=name,
    )(*blocks, *done)


def place_all(slots, blocks, done=()):
    full = slice(None)
    pieces = [
        ((slice(0, 48), full), 0, lambda w: (pl.ds(pl.multiple_of(w * 48, 16), 48), slice(0, 768))),
        ((slice(48, 96), full), 0, lambda w: (pl.ds(pl.multiple_of(w * 48, 16), 48), slice(768, 1536))),
        ((slice(96, 144), full), 1, lambda w: (pl.ds(pl.multiple_of(w * 48, 16), 48), full)),
        ((slice(176, 368), full), (3, 4), lambda w: (pl.ds(within_half(w, 192), 192), full)),
    ]
    for j in range(3):
        pieces.append(
            (
                (slice(144, 176), slice(256 * j, 256 * j + 256)),
                2,
                lambda w, j=j: (pl.ds(pl.multiple_of(w * 96 + 32 * j, 16), 32), full),
            )
        )
    for k in range(2):
        pieces.append(
            (
                (slice(368, 416), slice(384 * k, 384 * k + 384)),
                (5, 6),
                lambda w, k=k: (pl.ds(within_half(w, 96) + 48 * k, 48), full),
            )
        )
    dims = ((768, 1536), (768, 768), (1536, 256), (1536, 768), (1536, 768), (768, 384), (768, 384))
    name = "place_last" if done else "place_first"
    return place(slots, blocks, pieces, tuple(shape(d, bf16) for d in dims), done, name)


def divided_by_48(x):
    return (x * 1366) >> 16


def row_of_wide(shape_of, width_dim):
    d = iota(shape_of, width_dim)
    w = divided_by_48(d)
    rest = d - 48 * w
    c = jnp.where(rest >= 24, 1, 0)
    return 96 * w + 48 * c + rest - 24 * c


def row_of_up(shape_of, up_dim):
    f = iota(shape_of, up_dim)
    q = divided_by_48(f)
    return 96 * (q >> 2) + 48 * ((q >> 1) & 1) + f - 48 * q, q & 1


def mix_parameters(mine):
    rate = -jnp.exp(mine[:, :64])
    step = jnp.exp(mine[:, 192:193])
    decay_log = step * rate
    decay = jnp.exp(decay_log)
    gap = (decay - 1.0) / rate
    return rate, step, decay_log, decay, gap


def coefficients_kernel(table, labels, d3, w3, drow, wrow, skip, value_b, proj_b, up_b, wide, masks, buf):
    half = pl.ds(pl.multiple_of(core_index() * 768, 256), 768)
    mine = table[half, :].astype(f32)
    rate, step, decay_log, decay, gap = mix_parameters(mine)
    weight = mine[:, 128:192] * gap * mine[:, 64:128]
    for v, three, row in ((decay_log, d3, drow), (weight, w3, wrow)):
        rest = v
        for k in range(3):
            part = rest.astype(bf16)
            three[:, 8 * k : 8 * k + 8, :] = part.reshape(96, 8, 64)
            rest = rest - part.astype(f32)
        buf[...] = v
        for c in range(8):
            row[:, 64 * c : 64 * c + 64] = buf[pl.ds(c, 96, stride=8), :]
    skip[...] = mine[:, 193:194]
    value_b[...] = mine[:, 194:195]
    low = table[half, 128:]
    proj_b[...] = mine[:, 128:].T[67:68, :]
    r, k = row_of_up((768, 1536), 1)
    at = r == iota((768, 1536), 0)
    pick = lambda which: dot(low, ones_where(at & (k == which)), ((0,), (0,)))
    up_b[...] = pick(0)[68:69, :] + pick(1)[69:70, :]
    spread_wide = ones_where(row_of_wide((1536, 768), 1) == iota((1536, 768), 0))
    wide[...] = dot(table[:, 128:], spread_wide, ((0,), (0,)))[70:73, :]
    lane = iota((8, 256), 1)
    each_lane = ones_where((iota((32, 256), 1) & 31) == iota((32, 256), 0))
    label = dot(jnp.broadcast_to(labels[...], (8, 32)).astype(bf16), each_lane)
    rows = []
    for k in (1, 2, 4, 8):
        before = jnp.where(((lane & 15) >= k) & (roll_halves(label, k) == label), 1.0, 0.0)
        behind = jnp.where(((lane & 15) + k < 16) & (roll_halves(label, 128 - k) == label), 1.0, 0.0)
        rows.append((before, behind))
    back = core_index() == 1
    for i, (before, behind) in enumerate(rows):
        masks[i : i + 1, :] = jnp.where(back, behind, before)[:1]
        masks[4 + i : 5 + i, :] = jnp.where(back, before, behind)[:1]


def coefficients(table, labels):
    dims = [((96, 24, 64), bf16)] * 2 + [((96, 512), f32)] * 2 + [((768, 1), f32)] * 2 + [((1, 768), f32), ((1, 1536), f32), ((3, 768), f32), ((8, 256), f32)]
    return pl.pallas_call(
        coefficients_kernel,
        out_shape=tuple(shape(*d) for d in dims),
        in_specs=[VM, VM],
        out_specs=(VM,) * len(dims),
        scratch_shapes=[pltpu.VMEM((768, 64), f32)],
        compiler_params=params(),
        name="coefficients",
    )(table, labels)


def small_sums_kernel(table, grads, skip, value_b, proj_b, up_b, gain, shift, out_b, out, buf, turn_buf):
    half = pl.ds(pl.multiple_of(core_index() * 768, 256), 768)
    theirs = pl.ds(pl.multiple_of((1 - core_index()) * 768, 256), 768)
    mine = table[half, :].astype(f32)
    rate, step, decay_log, decay, gap = mix_parameters(mine)
    in_p, out_p = mine[:, 64:128], mine[:, 128:192]
    both = grads[...].T
    weight, slope = both[:, :64], both[:, 64:]
    product = out_p * in_p
    through = slope * decay_log
    buf[theirs, :] = jnp.zeros((768, 256), f32)
    buf[half, 128:] = jnp.zeros((768, 128), f32)
    turn_buf[...] = jnp.zeros((128, 128), f32)
    buf[half, 0:64] = through + weight * (product * (decay * step - gap))
    buf[half, 64:128] = weight * out_p * gap
    buf[half, 128:192] = weight * in_p * gap
    buf[half, 192:193] = jnp.sum(through + weight * (product * decay * step), axis=1, keepdims=True)
    for k, ref in enumerate((skip, value_b)):
        buf[half, 193 + k : 194 + k] = ref[...]
    buf[half, 195:196] = jnp.broadcast_to(proj_b[...], (8, 768)).T[:, :1]
    for q in range(32):
        turn_buf[q : q + 1, 0:48] = up_b[:, 48 * q : 48 * q + 48]
        for k, ref in enumerate((gain, shift, out_b)):
            turn_buf[32 + 3 * q + k : 33 + 3 * q + k, 0:24] = ref[:, 24 * q : 24 * q + 24]
    columns = turn_buf[...].T
    for q in range(16):
        buf[pl.ds(pl.multiple_of(core_index() * 768 + 48 * q, 16), 48), 196:198] = columns[:48, 2 * q : 2 * q + 2]
    for q in range(32):
        buf[48 * q : 48 * q + 24, 198:201] = columns[:24, 32 + 3 * q : 35 + 3 * q]
    for w in range(16):
        for j in range(3):
            out[w, :, 256 * j : 256 * j + 256] = buf[96 * w + 32 * j : 96 * w + 32 * j + 32, :]


def small_sums(*args):
    return pl.pallas_call(
        small_sums_kernel,
        out_shape=shape((16, 32, 768), f32),
        in_specs=[VM] * len(args),
        out_specs=VM,
        scratch_shapes=[pltpu.VMEM((1536, 256), f32), pltpu.VMEM((128, 128), f32)],
        compiler_params=params(),
        name="small_sums",
    )(*args)


def children_of():
    kids = {s: [] for s in SLOTS}
    for r, sends in enumerate(ROUNDS):
        for d in "xyzm":
            if d not in sends:
                continue
            if d != "z" or sends["z"] == sends["o"]:
                kids[sends[d]].append(((r, d), None))
            else:
                kids[sends["z"]].append(((r, "z"), "mid"))
                kids[sends["o"]].append(((r, "z"), "end"))
    return kids


KIDS = children_of()


def sum_kernel(slots, pieces, n_own, arrived, rows, final, *refs):
    owns, refs = refs[:n_own], refs[n_own:]
    ins, refs = refs[: len(arrived)], refs[len(arrived) :]
    n_out = 2 if final else len(slots)
    outs, (own_buf, small_buf, in_buf, out_buf, own_sem, small_sem, in_sem, out_sem) = refs[:n_out], refs[n_out:]
    in_copies = []

    def start_own(p):
        w = owner(slots[p])
        mine = (w >> 3) == core_index()
        for choices, dst in pieces:
            for choice, (which, src) in enumerate(choices):

                def go(which=which, src=src, dst=dst):
                    buf, sem = (own_buf, own_sem) if owns[which].dtype == bf16 else (small_buf, small_sem)
                    pltpu.make_async_copy(owns[which].at[src(w)], buf.at[(p,) + dst], sem.at[p]).start()

                if len(choices) == 1:
                    go()
                else:
                    pl.when(mine == (choice == 0))(go)

    def wait_own(p):
        for buf, sem in ((own_buf, own_sem), (small_buf, small_sem)):
            pltpu.make_async_copy(buf.at[p], buf.at[p], sem.at[p]).wait()

    for p in range(len(slots)):
        start_own(p)
    for k in range(len(arrived)):
        in_copies.append(pltpu.make_async_copy(ins[k], in_buf.at[k], in_sem.at[k]))
        in_copies[-1].start()
    end = at_end()
    waited = set()
    sent = []
    for p, slot in enumerate(slots):
        wait_own(p)
        parts = []
        for kid, layers in KIDS[slot]:
            k = arrived.index(kid)
            if k not in waited:
                in_copies[k].wait()
                waited.add(k)
            parts.append((k, None if layers is None else jnp.where(end == (layers == "end"), 1.0, 0.0)))
        whole = FIRST_END[slot] and FIRST_MID[slot]
        keep = None if whole else is_first(slot).astype(f32)

        def add(i, _, p=p, parts=parts, keep=keep, own=own_buf, first=0):
            at = pl.ds(pl.multiple_of(i * 32, 32), 32)
            to = pl.ds(pl.multiple_of(first + i * 32, 32), 32)
            total = own[p, at, :].astype(f32)
            if keep is not None:
                total = total * keep
            for k, mask in parts:
                v = in_buf[k, to, :].astype(f32)
                total = total + (v if mask is None else v * mask)
            out_buf[p, to, :] = total.astype(out_buf.dtype)
            return 0

        low_rows, small_rows = own_buf.shape[1], small_buf.shape[1]
        lax.fori_loop(0, low_rows // 32, add, 0, unroll=4)
        lax.fori_loop(0, small_rows // 32, functools.partial(add, own=small_buf, first=low_rows), 0)
        if not final:
            sent.append(pltpu.make_async_copy(out_buf.at[p], outs[p], out_sem.at[p]))
            sent[-1].start()
    if final:
        for i, (ref, core) in enumerate(((outs[0], core_index()), (outs[1], 1 - core_index()))):
            for k, (src, dst) in enumerate(final):
                sent.append(pltpu.make_async_copy(out_buf.at[(0,) + src(core)], ref.at[dst], out_sem.at[i * len(final) + k]))
                sent[-1].start()
    for c in sent:
        c.wait()


def sum_slots(slots, owns, pieces, came, rows, final=None, final_rows=None, name="sum"):
    arrived = []
    for slot in slots:
        for kid, _ in KIDS[slot]:
            if kid not in arrived:
                arrived.append(kid)
    if final:
        out_shapes = (shape((final_rows, 768), f32),) * 2
    else:
        out_shapes = tuple(shape((rows, 768), bf16) for _ in slots)
    return pl.pallas_call(
        functools.partial(sum_kernel, slots, pieces, len(owns), arrived, rows, final),
        out_shape=out_shapes,
        in_specs=[ANY] * (len(owns) + len(arrived)),
        out_specs=tuple(HBM for _ in out_shapes),
        scratch_shapes=[
            pltpu.VMEM((len(slots), rows - 32, 768), bf16),
            pltpu.VMEM((len(slots), 32, 768), f32),
            pltpu.VMEM((max(1, len(arrived)), rows, 768), bf16),
            pltpu.VMEM((len(slots), rows, 768), f32 if final else bf16),
            pltpu.SemaphoreType.DMA((len(slots),)),
            pltpu.SemaphoreType.DMA((len(slots),)),
            pltpu.SemaphoreType.DMA((max(1, len(arrived)),)),
            pltpu.SemaphoreType.DMA((2 * len(final) if final else len(slots),)),
        ],
        compiler_params=params(),
        name=name,
    )(*owns, *[came[k] for k in arrived])


def scatter_rounds(owns, pieces, rows, final, final_rows, name, work, state=None):
    came = {}
    for r in reversed(range(len(ROUNDS))):
        slots = [(r, d) for d in "xyzm" if d in ROUNDS[r]]
        blocks = sum_slots(slots, owns, pieces, came, rows, name=f"{name}_{r}")
        blocks, state = together(blocks, state)
        new = {slot: lax.ppermute(block, "wide", PERMS[slot[1]]) for slot, block in zip(slots, blocks)}
        state = work[len(ROUNDS) - 1 - r](state)
        new, state = together(new, state)
        came.update(new)
    return sum_slots(["own"], owns, pieces, came, rows, final, final_rows, name=f"{name}_own"), state


def scatter_all(proj_mine, proj_theirs, out, out_theirs, up, value, small, work, state):
    full = slice(None)

    def lanes():
        return pl.ds(pl.multiple_of(core_index() * 384, 128), 384)

    pieces = [([(i, lambda w: (pl.ds(within_half(w, 192), 192), full)) for i in (0, 1)], (slice(0, 192), full))]
    for k in range(2):
        pieces.append(
            (
                [
                    (2, lambda w, k=k: (pl.ds(within_half(w, 96) + 48 * k, 48), lanes())),
                    (3, lambda w, k=k: (pl.ds(within_half(w, 96) + 48 * k, 48), full)),
                ],
                (slice(192, 240), slice(384 * k, 384 * k + 384)),
            )
        )
        pieces.append(
            (
                [(4, lambda w, k=k: (pl.ds(pl.multiple_of(w * 48, 16), 48), slice(768 * k, 768 * k + 768)))],
                (slice(240 + 48 * k, 288 + 48 * k), full),
            )
        )
    pieces.append(([(5, lambda w: (pl.ds(pl.multiple_of(w * 48, 16), 48), full))], (slice(336, 384), full)))
    pieces.append(([(6, lambda w: (w,))], (slice(0, 32), full)))
    final = [
        (lambda c: (pl.ds(pl.multiple_of(c * 96, 8), 96), full), (slice(0, 96), full)),
        (lambda c: (slice(192, 240), pl.ds(pl.multiple_of(c * 384, 128), 384)), (slice(96, 144), slice(0, 384))),
        (lambda c: (slice(384, 416), full), (slice(216, 248), full)),
    ] + [
        (
            lambda c, q=q: (pl.ds(pl.multiple_of(240 + q * 48 + c * 24, 8), 24), full),
            (slice(144 + 24 * q, 168 + 24 * q), full),
        )
        for q in range(3)
    ]
    owns = (proj_mine, proj_theirs, out, out_theirs, up, value, small)
    return scatter_rounds(owns, pieces, 416, final, 248, "sum", work, state)


def unpack_kernel(mine, recv, proj, out, up, value, rate, in_map, out_map, vectors, small):
    for core in range(2):

        @pl.when(core_index() == core)
        def _(core=core):
            for ref, half in ((mine, core), (recv, 1 - core)):
                proj[:, 768 * half : 768 * half + 768] = ref[:96, :]
                out[:, 384 * half : 384 * half + 384] = ref[96:144, :384]
                for q in range(2):
                    up[:, 1536 * half + 768 * q : 1536 * half + 768 * q + 768] = ref[144 + 24 * q : 168 + 24 * q, :]
                value[:, 768 * half : 768 * half + 768] = ref[192:216, :]
            s = mine[216:248, :] + recv[216:248, :]
            if core == 0:
                small[:32, :] = s[:, :256]
                small[32:, :] = s[:16, 256:512]
            else:
                small[:16, :] = s[16:, 256:512]
                small[16:, :] = s[:, 512:]

    rate[...] = small[:, :64]
    in_map[...] = small[:, 64:128]
    out_map[...] = small[:, 128:192]
    vectors[...] = small[:, 128:].T[64:80, :]


def unpack(mine, recv):
    dims = ((96, 1536), (48, 768), (24, 3072), (24, 1536), (48, 64), (48, 64), (48, 64), (16, 48))
    return pl.pallas_call(
        unpack_kernel,
        out_shape=tuple(shape(d, f32) for d in dims),
        in_specs=[VM, VM],
        out_specs=(VM,) * len(dims),
        scratch_shapes=[pltpu.VMEM((48, 256), f32)],
        compiler_params=params(),
        name="unpack_sums",
    )(mine, recv)


TILE = 256


def tokens_by(width):
    return pl.BlockSpec((TILE, width), lambda i: (i, 0))


def by_tokens(rows):
    return pl.BlockSpec((rows, TILE), lambda i: (0, i))


def whole_block(*dims):
    return pl.BlockSpec(dims, lambda i: (0,) * len(dims))


def enter_kernel(unit, wide, up_w, up_b, value_w, value_b, normed, up_pre, up_low, value_pre):
    low = (unit[...] * wide[0:1, :] + wide[1:2, :]).astype(bf16)
    normed[...] = low
    value_pre[...] = dot(low, value_w[...]).T + value_b[...]
    for k in range(0, up_w.shape[1], 512):
        at = slice(k, k + 512)
        pre = dot(low, up_w[:, at]) + up_b[:, at]
        up_pre[:, at] = pre
        up_low[:, at] = gelu(pre).astype(bf16)


def enter(unit, wide, up_w, up_b, value_w, value_b):
    n, d = unit.shape
    f, c = up_w.shape[1], value_w.shape[1]
    return pl.pallas_call(
        enter_kernel,
        out_shape=(shape((n, d), bf16), shape((n, f), f32), shape((n, f), bf16), shape((c, n), f32)),
        grid=(n // TILE,),
        in_specs=[tokens_by(d)] + [whole_block(*v.shape) for v in (wide, up_w, up_b, value_w, value_b)],
        out_specs=(tokens_by(d), tokens_by(f), tokens_by(f), by_tokens(c)),
        compiler_params=params(),
        name="enter",
    )(unit, wide, up_w, up_b, value_w, value_b)


def gate_kernel(up, up_other, g, mixed, proj_mine, proj_theirs, proj_b, out_a, out_b, gm, gated, gp, grad_b, grad_mine, grad_theirs, grad_out, acc, acc_out, out_w):
    step, steps = pl.program_id(0), pl.num_programs(0)

    @pl.when(step == 0)
    def _():
        acc[...] = jnp.zeros_like(acc)
        acc_out[...] = jnp.zeros_like(acc_out)
        grad_b[...] = jnp.zeros_like(grad_b)
        for core in range(2):

            @pl.when(core_index() == core)
            def _(core=core):
                out_w[:, 384 * core : 384 * core + 384] = out_a[...]
                out_w[:, 384 - 384 * core : 768 - 384 * core] = out_b[...]

    proj = dot(up[...], proj_mine[...]) + dot(up_other[...], proj_theirs[...]) + proj_b[...]
    gg = dot(g[...], out_w[...], ((1,), (1,)))
    gm[...] = (gg * proj).T
    mix = mixed[...].T
    low = (mix * proj).astype(bf16)
    gated[...] = low
    gp_low = (gg * mix).astype(bf16)
    gp[...] = gp_low
    grad_b[...] += jnp.sum(gp_low.astype(f32), axis=0, keepdims=True)
    for k, ref in enumerate((up, up_other)):
        acc[k] += dot(ref[...], gp_low, ((0,), (0,)))
    acc_out[...] += dot(low, g[...], ((0,), (0,)))

    @pl.when(step == steps - 1)
    def _():
        grad_mine[...] = acc[0].astype(bf16)
        grad_theirs[...] = acc[1].astype(bf16)
        grad_out[...] = acc_out[...].astype(bf16)


def gate(up, up_other, g, mixed, proj_mine, proj_theirs, proj_b, out_a, out_b):
    n, f = up.shape
    c, d = out_a.shape[0], g.shape[1]
    return pl.pallas_call(
        gate_kernel,
        out_shape=(
            shape((c, n), f32),
            shape((n, c), bf16),
            shape((n, c), bf16),
            shape((1, c), f32),
            shape((f, c), bf16),
            shape((f, c), bf16),
            shape((c, d), bf16),
        ),
        grid=(n // TILE,),
        in_specs=[tokens_by(f), tokens_by(f), tokens_by(d), by_tokens(c)]
        + [whole_block(*v.shape) for v in (proj_mine, proj_theirs, proj_b, out_a, out_b)],
        out_specs=(by_tokens(c), tokens_by(c), tokens_by(c), whole_block(1, c))
        + (whole_block(f, c), whole_block(f, c), whole_block(c, d)),
        scratch_shapes=[pltpu.VMEM((2, f, c), f32), pltpu.VMEM((c, d), f32), pltpu.VMEM((c, d), bf16)],
        compiler_params=params(),
        name="gate",
    )(up, up_other, g, mixed, proj_mine, proj_theirs, proj_b, out_a, out_b)


def contract(left, right, left_dim, right_dim):
    return lax.dot_general(left, right, (((left_dim,), (right_dim,)), ((), ())), preferred_element_type=f32)


def by_core(core, zero, one):
    return jnp.where(core == 0, zero, one)


def in_order(core, mine, other, axis):
    return by_core(core, jnp.concatenate([mine, other], axis), jnp.concatenate([other, mine], axis))


def half_of(x, which, axis):
    size = x.shape[axis] // 2
    return lax.dynamic_slice_in_dim(x, which * size, size, axis)


def per_device(
    sizes,
    tokens,
    segment,
    cotangent,
    w_up,
    w_value,
    w_proj,
    w_out,
    norm_gain,
    norm_bias,
    bias_up,
    bias_value,
    bias_proj,
    bias_out,
    log_rate,
    log_step,
    input_map,
    output_map,
    skip_gain,
):
    both = ("wide", "narrow")
    core = core_index()
    pairs = [(i, i ^ 1) for i in range(sizes["narrow"])]
    staged = sizes["wide"] == 16 and sizes["narrow"] == 2

    def swap(x):
        return lax.ppermute(x, "narrow", pairs)

    tok, width = tokens.shape
    blocks = tok // T

    def by_place(x):
        return x.reshape(blocks, T, width).transpose(1, 0, 2)

    labels = segment.reshape(blocks, T)[:, 0].astype(f32)
    own_x, own_g = by_place(tokens), by_place(cotangent)

    def whole_chip(mine, other):
        return by_core(core, jnp.stack([mine, other], 1), jnp.stack([other, mine], 1)).reshape(2 * tok, width)

    def normalise(x):
        x = x.astype(f32)
        average = jnp.mean(x, axis=-1, keepdims=True)
        centred = x - average
        scale = lax.rsqrt(jnp.mean(centred * centred, axis=-1, keepdims=True) + 1e-05)
        return centred * scale, scale

    if staged:
        vectors = (log_step, skip_gain, bias_value, bias_proj, bias_up, norm_gain, norm_bias, bias_out, labels)
        vectors = jnp.concatenate([v.astype(f32) for v in vectors])[None]
        keep, send = pack(w_up, w_value, w_proj, w_out, log_rate, input_map, output_map, vectors)
        recv = swap(send)
        other_labels = recv[192:208, 201]
        blob = merge(keep, recv)
        other_x, other_g = swap(own_x), swap(own_g)
        idle = lambda state: state

        def chip_tokens(state):
            (mine_x, their_x), (mine_g, their_g) = state
            return whole_chip(mine_x, their_x), whole_chip(mine_g, their_g)

        def chip_unit(state):
            return normalise(state[0])[0], state[1]

        state = (own_x, other_x), (own_g, other_g)
        placed, (unit_chip, g_chip) = gather_rounds(blob, [idle, chip_tokens, chip_unit, idle, idle], state)
        up_w, value_w, table, proj_mine, proj_theirs, out_mine, out_theirs = placed
        proj_cross = swap(proj_theirs)
        out_cross = swap(out_theirs)
        out_w = in_order(core, out_mine, out_cross, 1)
        label_row = in_order(core, labels, other_labels, 0)[None]
        coefs = coefficients(table, label_row)
        decay3, weight3, decay_row, weight_row, skip_p, value_b, proj_b, up_b, wide, masks = coefs
    else:
        other_x, other_g = swap(own_x), swap(own_g)
        unit_chip, g_chip = normalise(whole_chip(own_x, other_x))[0], whole_chip(own_g, other_g)
        other_labels = swap(labels)
        whole = lambda p: lax.all_gather(p, both, axis=0, tiled=True)
        up_w = half_of(whole(w_up), core, 1)
        value_w = half_of(whole(w_value), core, 1)
        full = whole(w_proj)
        proj_mine = half_of(half_of(full, core, 1), core, 0)
        proj_theirs = half_of(half_of(full, core, 1), 1 - core, 0)
        proj_cross = half_of(half_of(full, 1 - core, 1), core, 0)
        out_w = half_of(whole(w_out), core, 0)
        out_mine, out_cross = half_of(out_w, core, 1), half_of(out_w, 1 - core, 1)
        rate_p, in_p, out_p = (half_of(whole(p).astype(f32), core, 0) for p in (log_rate, input_map, output_map))
        step_p, skip_p, value_b, proj_b = (
            half_of(whole(p).astype(f32), core, 0)[:, None] for p in (log_step, skip_gain, bias_value, bias_proj)
        )
        proj_b = proj_b.T
        up_b = half_of(whole(bias_up).astype(f32), core, 0)[None]
        wide = jnp.stack([whole(p).astype(f32) for p in (norm_gain, norm_bias, bias_out)])

    direction = core.astype(jnp.int32).reshape(1)
    if not staged:
        rate = -jnp.exp(rate_p)
        step = jnp.exp(step_p)
        decay_log = step * rate
        decay = jnp.exp(decay_log)
        gap = (decay - 1.0) / rate
        weight = out_p * gap * in_p
        masks = block_masks(in_order(core, labels[None], other_labels[None], 0), core == 1)
        decay_row, weight_row = (v.reshape(-1, 512) for v in (decay_log, weight))
        decay3, weight3 = thirds(decay_log), thirds(weight)
    normed_low, up_pre, up_low, value_pre = enter(unit_chip, wide, up_w, up_b, value_w, value_b)
    up_other = swap(up_low)
    mixed, entering = ssm_fwd(direction, value_pre, decay3, weight3, decay_row, weight_row, skip_p, masks)
    grad_mixed, gated_low, grad_proj_low, grad_proj_b, grad_proj_mine, grad_proj_theirs, grad_out_w = gate(
        up_low, up_other, g_chip, mixed, proj_mine, proj_theirs, proj_b, out_mine, out_cross
    )

    grad_proj_other = swap(grad_proj_low)
    grad_value_low, grad_mix, grad_skip, grad_value_b = ssm_bwd(
        direction, value_pre, grad_mixed, entering, decay3, weight3, decay_row, skip_p, masks
    )
    grad_up_act = contract(grad_proj_low, proj_mine, 1, 1) + contract(grad_proj_other, proj_cross, 1, 1)
    grad_up_low = (grad_up_act * gelu_grad(up_pre)).astype(bf16)
    grad_up_b = jnp.sum(grad_up_low.astype(f32), axis=0, keepdims=True)
    grad_up_w = contract(normed_low, grad_up_low, 0, 0).astype(bf16)
    grad_value_w = contract(normed_low, grad_value_low, 0, 1).astype(bf16)

    def own_and_theirs(x):
        x = x.reshape(T, 2, blocks, width)
        return lax.dynamic_index_in_dim(x, core, 1, False), lax.dynamic_index_in_dim(x, 1 - core, 1, False)

    def by_token(x):
        return x.transpose(1, 0, 2).reshape(tok, width)

    grad_part = contract(grad_up_low, up_w, 1, 1) + contract(grad_value_low, value_w, 0, 1)
    grad_gain = jnp.sum(grad_part * unit_chip, axis=0, keepdims=True)
    grad_shift = jnp.sum(grad_part, axis=0, keepdims=True)
    own_gf = own_g.astype(f32)
    grad_out_b = jnp.sum(own_gf, axis=(0, 1))[None]

    def split_parts(state):
        gated, part = state
        mine, theirs = zip(own_and_theirs(contract(gated, out_w, 1, 0)), own_and_theirs(part))
        return mine, jnp.stack([t.astype(bf16) for t in theirs])

    def exchange_parts(state):
        return state[0], swap(state[1])

    def finish_result(state):
        mine, came = state
        return by_token((own_x.astype(f32) + mine[0] + came[0] + wide[2]).astype(bf16)), mine[1] + came[1]

    def finish_tokens(state):
        result, grad_normed = state
        unit, scale = normalise(own_x)
        h = grad_normed * wide[0]
        inner = h - jnp.mean(h, axis=-1, keepdims=True) - unit * jnp.mean(h * unit, axis=-1, keepdims=True)
        return result, by_token(own_gf + inner * scale)

    if staged:
        vectors = (grad_skip, grad_value_b, grad_proj_b, grad_up_b, grad_gain, grad_shift, grad_out_b)
        small = small_sums(table, grad_mix, *vectors)
        theirs = swap(half_of(grad_out_w, 1 - core, 1))
        work = [split_parts, exchange_parts, finish_result, finish_tokens, idle]
        grads = (grad_proj_mine, grad_proj_theirs, grad_out_w, theirs, grad_up_w, grad_value_w, small)
        (mine, send), (result, grad_tokens) = scatter_all(*grads, work, (gated_low, grad_part))
        sum_proj_w, sum_out_w, sum_up_w, sum_value_w, sum_rate, sum_in, sum_out, sums = unpack(mine, swap(send))
        sum_step, sum_skip, sum_value_b, sum_proj_b = (sums[k] for k in range(4))
        sum_up_b = sums[4:6].reshape(96)
        sum_gain, sum_shift, sum_out_b = (sums[6 + k, :24] for k in range(3))
    else:

        grad_mix = grad_mix.T
        grad_weight, grad_decay = grad_mix[:, :64], grad_mix[:, 64:]
        product = out_p * in_p
        grad_ssm = (
            grad_decay * decay_log + grad_weight * (product * (decay * step - gap)),
            grad_weight * out_p * gap,
            grad_weight * in_p * gap,
            jnp.sum(grad_decay * decay_log + grad_weight * (product * decay * step), axis=1, keepdims=True),
        )

        def share(x):
            return lax.psum_scatter(x.astype(f32), both, scatter_dimension=0, tiled=True)

        def halves(x, axis):
            zero = jnp.zeros_like(x)
            return share(in_order(core, x, zero, axis))

        result, grad_tokens = finish_tokens(finish_result(exchange_parts(split_parts((gated_low, grad_part)))))
        sum_up_w, sum_value_w = halves(grad_up_w, 1), halves(grad_value_w, 1)
        sum_proj_w = halves(in_order(core, grad_proj_mine, grad_proj_theirs, 0), 1)
        sum_out_w = halves(grad_out_w, 0)
        sum_rate, sum_in, sum_out, sum_step = (halves(v, 0) for v in grad_ssm)
        sum_step = sum_step[:, 0]
        sum_skip, sum_value_b, sum_proj_b = (halves(v, 0) for v in (grad_skip[:, 0], grad_value_b[:, 0], grad_proj_b[0]))
        sum_up_b = halves(grad_up_b[0], 0)
        sum_gain, sum_shift, sum_out_b = share(grad_gain[0]), share(grad_shift[0]), share(grad_out_b[0])

    return (
        result,
        grad_tokens,
        sum_up_w,
        sum_value_w,
        sum_proj_w,
        sum_out_w,
        sum_gain,
        sum_shift,
        sum_up_b,
        sum_value_b,
        sum_proj_b,
        sum_out_b,
        sum_rate,
        sum_step,
        sum_in,
        sum_out,
        sum_skip,
    )


def solution(mesh):
    rows, vector = P(("wide", "narrow"), None), P(("wide", "narrow"))
    sizes = dict(mesh.shape)
    return jax.shard_map(
        functools.partial(per_device, sizes),
        mesh=mesh,
        in_specs=(rows, vector, rows, rows, rows, rows, rows) + (vector,) * 6 + (rows, vector, rows, rows, vector),
        out_specs=(rows,) * 6 + (vector,) * 6 + (rows, vector, rows, rows, vector),
        check_vma=False,
    )
```

time: 2060 us -> 382 us (0.19)
  waiting for transfers between devices: 728 us -> 89.4 us
  matrix products: 574 us -> 26.4 us
  local copies, waits for them, and re-layouts: 317 us -> 24.5 us
  blocking collectives: 201 us -> 0 us
  other arithmetic: 209 us -> 22.8 us
  Pallas kernels: 0 us -> 141 us
  starting transfers between devices: 0.44 us -> 69.5 us
    reduce_scatter x7 -> x0, waiting for transfers between devices: 725 us -> none  [the longest x1 214 us: per_device(): lax.psum_scatter(grad_w_proj, ('wide', 'narrow'), scatter_dimension=0, ti...]
    dot_general x30 -> x0, matrix products: 520 us -> none  [the longest x6 149 us: ssm_half(): jnp.einsum('tnh,bnh->bth', lead, entering, precision=lax.Precision.HIGHEST)]
    pallas_call x0 -> x17, Pallas kernels: none -> 141 us  [the longest x2 60.2 us: mix_call(): pl.pallas_call(body, out_shape=out_shape, grid=(steps,), in_specs=in_spec...]
    all_gather x3 -> x0, blocking collectives: 125 us -> none  [the longest x1 44.8 us: gather_all(): lax.all_gather(shards[10], ('wide', 'narrow'), axis=0, tiled=True)]
    rev x9 -> x0, local copies, waits for them, and re-layouts: 119 us -> none  [the longest x4 69.1 us: ssm_half(): powers[::-1]]
    ppermute x0 -> x48, waiting for transfers between devices: none -> 89.4 us  [the longest x19 43.5 us: scatter_rounds(): lax.ppermute(block, 'wide', PERMS[slot[1]])]
    unnamed x2 -> x0, blocking collectives: 75.9 us -> none
    mul x36 -> x1, other arithmetic: 74.1 us -> 2.08 us  [normalise(): return (centred * scale, scale)]
  transfers between devices with their start and end apart: 11 -> 48, of which waited for: 6 -> 30; matrix products, arithmetic and copies ran while one was open for 28% -> 16% of each run, Pallas kernels for 0% -> 26%
where the time goes in v1:
time: 382 us; the launch traced here: 375 us
  Pallas kernels  141 us (37%)
  waiting for transfers between devices  89.4 us (23%)
  starting transfers between devices  69.5 us (18%)
  matrix products  26.4 us (7%)
  local copies, waits for them, and re-layouts  24.5 us (6%)
  other arithmetic  22.8 us (6%)
    pallas_call x2, Pallas kernels, mix_call(): pl.pallas_call(body, out_shape=out_shape, grid=(steps,), in_specs=in_spec...  60.2 us
    ppermute x19, waiting for transfers between devices, scatter_rounds(): lax.ppermute(block, 'wide', PERMS[slot[1]])  43.5 us
    ppermute x19, waiting for transfers between devices, gather_rounds(): lax.ppermute(block, 'wide', PERMS[d])  41.3 us
    ppermute x19, starting transfers between devices, gather_rounds(): lax.ppermute(block, 'wide', PERMS[d])  32.9 us
    ppermute x19, starting transfers between devices, scatter_rounds(): lax.ppermute(block, 'wide', PERMS[slot[1]])  31.8 us
    dot_general x7, matrix products, contract(): lax.dot_general(left, right, (((left_dim,), (right_dim,)), ((), ())), pre...  26.4 us
    pallas_call x6, Pallas kernels, sum_slots(): pl.pallas_call(functools.partial(sum_kernel, slots, pieces, len(owns), ar...  23.3 us
    pallas_call x1, Pallas kernels, gate(): pl.pallas_call(gate_kernel, out_shape=(shape((c, n), f32), shape((n, c),...  21.5 us
  transfers between devices with their start and end apart: 48, of which 30 were waited for; matrix products, arithmetic and copies ran while one was open for 16% of the time, Pallas kernels for 26%

profile of v1, /device:TPU:0, one launch (start us, length us, event | category | flops | bytes accessed | tf_op | source)
XLA Modules:
  0.0 375.1 jit_solution(17053291687248244511)
XLA Ops:
  17.6 4.4 %collective-permute-start.6 = (bf16[416,768]{1,0:T(8,128)(2,1)}, bf16[416,768]{1,0:T(8,128)(2,1)}, u32[]{:S(2)}, u32[]{:S(2)}) collective-permute-start(bf16[416,768]{1,0:T(8,128)(2,1)} %merge_pair.1.refs_0_), channel_id=1, source_target_pairs={{0,8},{2,10},{4,12},{6,14},{8,0},{10,2},{12,4},{14,6},{16,24},{18,... | collective-permute-start | bytes 1916936 | tf_op jit(solution)/shard_map/ppermute | solution.py:473
  22.0 9.1 %collective-permute-done.4.refs_2_ = bf16[416,768]{1,0:T(8,128)(2,1)} collective-permute-done((bf16[416,768]{1,0:T(8,128)(2,1)}, bf16[416,768]{1,0:T(8,128)(2,1)}, u32[]{:S(2)}, u32[]{:S(2)}) %collective-permute-start.4) | collective-permute-done | bytes 639008 | tf_op jit(solution)/shard_map/ppermute | solution.py:473
  47.6 6.2 %collective-permute-done.10.refs_8_ = bf16[416,768]{1,0:T(8,128)(2,1)S(1)} collective-permute-done((bf16[416,768]{1,0:T(8,128)(2,1)}, bf16[416,768]{1,0:T(8,128)(2,1)S(1)}, u32[]{:S(2)}, u32[]{:S(2)}) %collective-permute-start.10) | collective-permute-done | bytes 639008 | tf_op jit(solution)/shard_map/ppermute | solution.py:473
  59.9 5.2 %collective-permute-start.14 = (bf16[416,768]{1,0:T(8,128)(2,1)S(1)}, bf16[416,768]{1,0:T(8,128)(2,1)S(1)}, u32[]{:S(2)}, u32[]{:S(2)}) collective-permute-start(bf16[416,768]{1,0:T(8,128)(2,1)S(1)} %broadcast_select_fusion.2), channel_id=1, source_target_pairs={{0,8},{2,10},{4,12},{6,14},{8,0},{10,2},{12,4},{14,6},{16,24},{18,... | collective-permute-start | bytes 1916936 | tf_op jit(solution)/shard_map/ppermute | solution.py:473
  82.0 6.7 %collective-permute-done.16.refs_14_ = bf16[416,768]{1,0:T(8,128)(2,1)S(1)} collective-permute-done((bf16[416,768]{1,0:T(8,128)(2,1)S(1)}, bf16[416,768]{1,0:T(8,128)(2,1)S(1)}, u32[]{:S(2)}, u32[]{:S(2)}) %collective-permute-start.16) | collective-permute-done | bytes 639008 | tf_op jit(solution)/shard_map/ppermute | solution.py:473
  98.4 6.4 %place_first.1 = (bf16[768,1536]{1,0:T(8,128)(2,1)}, bf16[768,768]{1,0:T(8,128)(2,1)}, bf16[1536,256]{1,0:T(8,128)(2,1)}, bf16[1536,768]{1,0:T(8,128)(2,1)}, bf1...) custom-call(bf16[416,768]{1,0:T(8,128)(2,1)} %merge_pair.1.refs_0_, ...), custom_call_target="tpu_custom_call" | custom-call | tf_op jit(solution)/shard_map/place_first/pallas_call | solution.py:530
  108.5 4.3 %coefficients.1 = (bf16[96,24,64]{2,1,0:T(8,128)(2,1)}, bf16[96,24,64]{2,1,0:T(8,128)(2,1)}, f32[96,512]{1,0:T(8,128)}, f32[96,512]{1,0:T(8,128)}, f32[768,1]{1,...) custom-call(bf16[1536,256]{1,0:T(8,128)(2,1)} %get-tuple-element.301, ...), custom_call_target="tpu_custom_call" | custom-call | tf_op jit(solution)/shard_map/coefficients/pallas_call | solution.py:642
  112.8 10.3 %enter.1 = (bf16[1024,768]{1,0:T(8,128)(2,1)}, f32[1024,1536]{1,0:T(8,128)}, bf16[1024,1536]{1,0:T(8,128)(2,1)}, f32[768,1024]{1,0:T(8,128)}) custom-call(f32[1024,768]{1,0:T(8,128)} %fusion.9.unit, f32[3,768]{1,0:T(4,128)} %get-tuple-element.302.wide, bf16[768,1536]{1,0:T(8,128)(2,1)} %get-tuple-element.303.up_w, f32[1,1536]{1,0:T(1,128)} %get-tuple-element.304.up_b, ...), custom_call_target="tpu_custom_call" | custom-call | tf_op jit(solution)/shard_map/enter/pallas_call | solution.py:939
  123.7 24.2 %mix_forward_0.1 = (f32[768,1024]{1,0:T(8,128)}, f32[96,64,256]{2,1,0:T(8,128)}) custom-call(s32[1]{0:T(128)} %bitcast.10.dir_ref, f32[768,1024]{1,0:T(8,128)} %get-tuple-element.309.x_ref, bf16[96,24,64]{2,1,0:T(8,128)(2,1)} %get-tuple-element.310.d3_ref, bf16[96,24,64]{2,1,0:T(8,128)(2,1)} %get-tuple-element.311.w3_ref, ...), custom_call_target="tpu_custom_call" | custom-call | tf_op jit(solution)/shard_map/mix_forward_0/pallas_call | solution.py:232
  148.0 21.5 %gate.1 = (f32[768,1024]{1,0:T(8,128)}, bf16[1024,768]{1,0:T(8,128)(2,1)}, bf16[1024,768]{1,0:T(8,128)(2,1)}, f32[1,768]{1,0:T(1,128)}, bf16[1536,768]{1,0:T(8,1...) custom-call(bf16[1024,1536]{1,0:T(8,128)(2,1)} %get-tuple-element.307.up, ...), custom_call_target="tpu_custom_call" | custom-call | tf_op jit(solution)/shard_map/gate/pallas_call | solution.py:988
  173.0 36.0 %mix_backward_0.1 = (bf16[768,1024]{1,0:T(8,128)(2,1)}, f32[128,768]{1,0:T(8,128)}, f32[768,1]{1,0:T(8,128)}, f32[768,1]{1,0:T(8,128)}) custom-call(s32[1]{0:T(128)} %bitcast.10.dir_ref, f32[768,1024]{1,0:T(8,128)} %get-tuple-element.309.x_ref, f32[768,1024]{1,0:T(8,128)} %get-tuple-element.328.gm_ref, f32[96,64,256]{2,1,0:T(8,128)} %get-tuple-element.329.enter_ref, ...), custom_call_target="tpu_custom_call" | custom-call | tf_op jit(solution)/shard_map/mix_backward_0/pallas_call | solution.py:232
  209.0 4.6 %convolution_convert_fusion.1.refs_5_ = bf16[768,768]{1,0:T(8,128)(2,1)} fusion(bf16[1024,768]{1,0:T(8,128)(2,1)} %get-tuple-element.325, bf16[768,1024]{1,0:T(8,128)(2,1)} %get-tuple-element.330), kind=kOutput, calls=%fused_computation.45 | convolution fusion | flops 1208549376 | bytes 4325376 | tf_op jit(solution)/shard_map/dot_general | solution.py:1011
  216.3 4.9 %fusion.39 = f32[1024,1536]{1,0:T(8,128)S(1)} fusion(bf16[1024,768]{1,0:T(8,128)(2,1)} %collective-permute-done.25, bf16[1536,768]{1,0:T(8,128)(2,1)} %collective-permute-done.26), kind=kOutput, calls=%fused_computation.87 | convolution fusion | flops 2415919104 | bytes 10223616 | tf_op jit(solution)/shard_map/dot_general | solution.py:1011
  221.2 4.7 %convert_reduce_fusion = (f32[1536]{0:T(1024)S(1)}, bf16[1024,1536]{1,0:T(8,128)(2,1)S(1)}) fusion(f32[1024,1536]{1,0:T(8,128)S(1)} %bitcast.103, f32[1024,1536]{1,0:T(8,128)S(1)} %fusion.38, f32[1024,1536]{1,0:T(8,128)S(1)} %fusion.39), kind=kLoop, calls=%fused_computation.11 | loop fusion | flops 34601472 | bytes 22026240 | tf_op jit(solution)/shard_map/reduce_sum | solution.py:1146
  233.7 5.1 %small_sums.1.refs_6_ = f32[16,32,768]{2,1,0:T(8,128)} custom-call(bf16[1536,256]{1,0:T(8,128)(2,1)} %get-tuple-element.301.table, f32[128,768]{1,0:T(8,128)} %get-tuple-element.331.grads, f32[768,1]{1,0:T(8,128)} %get-tuple-element.332.skip, f32[768,1]{1,0:T(8,128)} %get-tuple-element.333.value_b, f32[1,768]{1,0:T(1,128)} %get-tuple-element.334.proj_b, ...), custom_call_target="tpu_custom_call" | custom-call | tf_op jit(solution)/shard_map/small_sums/pallas_call | solution.py:688
  238.8 6.5 %convolution_convert_fusion.refs_4_ = bf16[768,1536]{1,0:T(8,128)(2,1)} fusion(bf16[1024,768]{1,0:T(8,128)(2,1)} %get-tuple-element.325, bf16[1024,1536]{1,0:T(8,128)(2,1)} %copy-done.10), kind=kOutput, calls=%fused_computation.16 | convolution fusion | flops 2417098752 | bytes 7077888 | tf_op jit(solution)/shard_map/dot_general | solution.py:1011
  276.6 4.4 %collective-permute-start.33 = (bf16[416,768]{1,0:T(8,128)(2,1)}, bf16[416,768]{1,0:T(8,128)(2,1)}, u32[]{:S(2)}, u32[]{:S(2)}) collective-permute-start(bf16[416,768]{1,0:T(8,128)(2,1)} %get-tuple-element.356), channel_id=1, source_target_pairs={{0,8},{2,10},{4,12},{6,14},{8,0},{10,2},{12,4},{14,6},{16,24},{18,... | collective-permute-start | bytes 1916936 | tf_op jit(solution)/shard_map/ppermute | solution.py:825
  281.6 9.8 %collective-permute-done.31.refs_9_ = bf16[416,768]{1,0:T(8,128)(2,1)} collective-permute-done((bf16[416,768]{1,0:T(8,128)(2,1)}, bf16[416,768]{1,0:T(8,128)(2,1)}, u32[]{:S(2)}, u32[]{:S(2)}) %collective-permute-start.31) | collective-permute-done | bytes 639008 | tf_op jit(solution)/shard_map/ppermute | solution.py:825
  295.1 4.1 %sum_2.1 = (bf16[416,768]{1,0:T(8,128)(2,1)}, bf16[416,768]{1,0:T(8,128)(2,1)}, bf16[416,768]{1,0:T(8,128)(2,1)}, bf16[416,768]{1,0:T(8,128)(2,1)}) custom-call(bf16[1536,768]{1,0:T(8,128)(2,1)} %get-tuple-element.322.refs_0_, bf16[1536,768]{1,0:T(8,128)(2,1)} %get-tuple-element.323.refs_1_, bf16[768,768]{1,0:T(8,128)(2,1)} %get-tuple-element.324.refs_2_, ...), custom_call_target="tpu_custom_call" | custom-call | tf_op jit(solution)/shard_map/sum_2/pallas_call | solution.py:799
  309.4 6.7 %collective-permute-done.36.refs_8_ = bf16[416,768]{1,0:T(8,128)(2,1)} collective-permute-done((bf16[416,768]{1,0:T(8,128)(2,1)}, bf16[416,768]{1,0:T(8,128)(2,1)}, u32[]{:S(2)}, u32[]{:S(2)}) %collective-permute-start.36) | collective-permute-done | bytes 639008 | tf_op jit(solution)/shard_map/ppermute | solution.py:825
  318.0 4.5 %sum_1.1 = (bf16[416,768]{1,0:T(8,128)(2,1)}, bf16[416,768]{1,0:T(8,128)(2,1)}, bf16[416,768]{1,0:T(8,128)(2,1)}, bf16[416,768]{1,0:T(8,128)(2,1)}) custom-call(bf16[1536,768]{1,0:T(8,128)(2,1)} %get-tuple-element.322.refs_0_, bf16[1536,768]{1,0:T(8,128)(2,1)} %get-tuple-element.323.refs_1_, bf16[768,768]{1,0:T(8,128)(2,1)} %get-tuple-element.324.refs_2_, ...), custom_call_target="tpu_custom_call" | custom-call | tf_op jit(solution)/shard_map/sum_1/pallas_call | solution.py:799
  325.5 4.5 %collective-permute-start.42 = (bf16[416,768]{1,0:T(8,128)(2,1)}, bf16[416,768]{1,0:T(8,128)(2,1)}, u32[]{:S(2)}, u32[]{:S(2)}) collective-permute-start(bf16[416,768]{1,0:T(8,128)(2,1)} %get-tuple-element.391), channel_id=1, source_target_pairs={{0,8},{2,10},{4,12},{6,14},{8,0},{10,2},{12,4},{14,6},{16,24},{18,... | collective-permute-start | bytes 1916936 | tf_op jit(solution)/shard_map/ppermute | solution.py:825
  340.7 4.4 %sum_0.1 = (bf16[416,768]{1,0:T(8,128)(2,1)}, bf16[416,768]{1,0:T(8,128)(2,1)}, bf16[416,768]{1,0:T(8,128)(2,1)}, bf16[416,768]{1,0:T(8,128)(2,1)}) custom-call(bf16[1536,768]{1,0:T(8,128)(2,1)} %get-tuple-element.322.refs_0_, bf16[1536,768]{1,0:T(8,128)(2,1)} %get-tuple-element.323.refs_1_, bf16[768,768]{1,0:T(8,128)(2,1)} %get-tuple-element.324.refs_2_, ...), custom_call_target="tpu_custom_call" | custom-call | tf_op jit(solution)/shard_map/sum_0/pallas_call | solution.py:799
  351.4 6.2 %collective-permute-done.44.refs_7_ = bf16[416,768]{1,0:T(8,128)(2,1)S(1)} collective-permute-done((bf16[416,768]{1,0:T(8,128)(2,1)}, bf16[416,768]{1,0:T(8,128)(2,1)S(1)}, u32[]{:S(2)}, u32[]{:S(2)}) %collective-permute-start.44) | collective-permute-done | bytes 639008 | tf_op jit(solution)/shard_map/ppermute | solution.py:825
  (239 shorter events, 168.6 us)
Async XLA Ops:
  13.2 17.9 %collective-permute-start.4 = (bf16[416,768]{1,0:T(8,128)(2,1)}, bf16[416,768]{1,0:T(8,128)(2,1)}, u32[]{:S(2)}, u32[]{:S(2)}) collective-permute-start(bf16[416,768]{1,0:T(8,128)(2,1)} %merge_pair.1.refs_0_), channel_id=1, source_target_pairs={{0,2},{2,0},{4,6},{6,4},{8,10},{10,8},{12,14},{14,12},{16,18},{18,... | collective-permute-start | bytes 1916936 | tf_op jit(solution)/shard_map/ppermute | solution.py:473
  16.1 16.5 %collective-permute-start.5 = (bf16[416,768]{1,0:T(8,128)(2,1)}, bf16[416,768]{1,0:T(8,128)(2,1)}, u32[]{:S(2)}, u32[]{:S(2)}) collective-permute-start(bf16[416,768]{1,0:T(8,128)(2,1)} %merge_pair.1.refs_0_), channel_id=1, source_target_pairs={{0,4},{2,6},{4,0},{6,2},{8,12},{10,14},{12,8},{14,10},{16,20},{18,... | collective-permute-start | bytes 1916936 | tf_op jit(solution)/shard_map/ppermute | solution.py:473
  17.6 18.5 %collective-permute-start.6 = (bf16[416,768]{1,0:T(8,128)(2,1)}, bf16[416,768]{1,0:T(8,128)(2,1)}, u32[]{:S(2)}, u32[]{:S(2)}) collective-permute-start(bf16[416,768]{1,0:T(8,128)(2,1)} %merge_pair.1.refs_0_), channel_id=1, source_target_pairs={{0,8},{2,10},{4,12},{6,14},{8,0},{10,2},{12,4},{14,6},{16,24},{18,... | collective-permute-start | bytes 1916936 | tf_op jit(solution)/shard_map/ppermute | solution.py:473
  38.7 15.2 %collective-permute-start.10 = (bf16[416,768]{1,0:T(8,128)(2,1)}, bf16[416,768]{1,0:T(8,128)(2,1)S(1)}, u32[]{:S(2)}, u32[]{:S(2)}) collective-permute-start(bf16[416,768]{1,0:T(8,128)(2,1)} %get-tuple-element.243), channel_id=1, source_target_pairs={{0,8},{2,10},{4,12},{6,14},{8,0},{10,2},{12,4},{14,6},{16,24},{18,... | collective-permute-start | bytes 1916936 | tf_op jit(solution)/shard_map/ppermute | solution.py:473
  40.2 13.6 %collective-permute-start.7 = (bf16[416,768]{1,0:T(8,128)(2,1)}, bf16[416,768]{1,0:T(8,128)(2,1)}, u32[]{:S(2)}, u32[]{:S(2)}) collective-permute-start(bf16[416,768]{1,0:T(8,128)(2,1)} %collective-permute-done.6.refs_4_), channel_id=1, source_target_pairs={{8,16},{10,18},{12,20},{14,22},{16,8},{18,10},{20,12},{22,14},{9,1... | collective-permute-start | bytes 1916936 | tf_op jit(solution)/shard_map/ppermute | solution.py:473
  41.7 14.7 %collective-permute-start.8 = (bf16[416,768]{1,0:T(8,128)(2,1)}, bf16[416,768]{1,0:T(8,128)(2,1)}, u32[]{:S(2)}, u32[]{:S(2)}) collective-permute-start(bf16[416,768]{1,0:T(8,128)(2,1)} %collective-permute-done.6.refs_4_), channel_id=1, source_target_pairs={{0,2},{2,0},{4,6},{6,4},{8,10},{10,8},{12,14},{14,12},{16,18},{18,... | collective-permute-start | bytes 1916936 | tf_op jit(solution)/shard_map/ppermute | solution.py:473
  42.2 14.4 %collective-permute-start.9 = (bf16[416,768]{1,0:T(8,128)(2,1)}, bf16[416,768]{1,0:T(8,128)(2,1)}, u32[]{:S(2)}, u32[]{:S(2)}) collective-permute-start(bf16[416,768]{1,0:T(8,128)(2,1)} %collective-permute-done.4.refs_2_), channel_id=1, source_target_pairs={{0,4},{2,6},{4,0},{6,2},{8,12},{10,14},{12,8},{14,10},{16,20},{18,... | collective-permute-start | bytes 1916936 | tf_op jit(solution)/shard_map/ppermute | solution.py:473
  59.9 15.8 %collective-permute-start.14 = (bf16[416,768]{1,0:T(8,128)(2,1)S(1)}, bf16[416,768]{1,0:T(8,128)(2,1)S(1)}, u32[]{:S(2)}, u32[]{:S(2)}) collective-permute-start(bf16[416,768]{1,0:T(8,128)(2,1)S(1)} %broadcast_select_fusion.2), channel_id=1, source_target_pairs={{0,8},{2,10},{4,12},{6,14},{8,0},{10,2},{12,4},{14,6},{16,24},{18,... | collective-permute-start | bytes 1916936 | tf_op jit(solution)/shard_map/ppermute | solution.py:473
  123.2 24.8 %collective-permute-start.22 = (bf16[1024,1536]{1,0:T(8,128)(2,1)}, bf16[1024,1536]{1,0:T(8,128)(2,1)}, u32[]{:S(2)}, u32[]{:S(2)}) collective-permute-start(bf16[1024,1536]{1,0:T(8,128)(2,1)} %get-tuple-element.307.up), channel_id=1, source_target_pairs={{0,1},{1,0},{2,3},{3,2},{4,5},{5,4},{6,7},{7,6},{8,9},{9,8},{10,11... | collective-permute-start | bytes 9437192 | tf_op jit(solution)/shard_map/ppermute | solution.py:1054
  123.2 93.1 %collective-permute-start.26 = (bf16[1536,768]{1,0:T(8,128)(2,1)S(1)}, bf16[1536,768]{1,0:T(8,128)(2,1)}, u32[]{:S(2)}, u32[]{:S(2)}) collective-permute-start(bf16[1536,768]{1,0:T(8,128)(2,1)S(1)} %copy-done.5), channel_id=1, source_target_pairs={{0,1},{1,0},{2,3},{3,2},{4,5},{5,4},{6,7},{7,6},{8,9},{9,8},{10,11... | collective-permute-start | bytes 7077896 | tf_op jit(solution)/shard_map/ppermute | solution.py:1054
  123.7 24.3 %collective-permute-start.23 = (bf16[768,384]{1,0:T(8,128)(2,1)}, bf16[768,384]{1,0:T(8,128)(2,1)}, u32[]{:S(2)}, u32[]{:S(2)}) collective-permute-start(bf16[768,384]{1,0:T(8,128)(2,1)} %get-tuple-element.321), channel_id=1, source_target_pairs={{0,1},{1,0},{2,3},{3,2},{4,5},{5,4},{6,7},{7,6},{8,9},{9,8},{10,11... | collective-permute-start | bytes 1769480 | tf_op jit(solution)/shard_map/ppermute | solution.py:1054
  169.4 46.8 %collective-permute-start.25 = (bf16[1024,768]{1,0:T(8,128)(2,1)}, bf16[1024,768]{1,0:T(8,128)(2,1)}, u32[]{:S(2)}, u32[]{:S(2)}) collective-permute-start(bf16[1024,768]{1,0:T(8,128)(2,1)} %get-tuple-element.326), channel_id=1, source_target_pairs={{0,1},{1,0},{2,3},{3,2},{4,5},{5,4},{6,7},{7,6},{8,9},{9,8},{10,11... | collective-permute-start | bytes 4718600 | tf_op jit(solution)/shard_map/ppermute | solution.py:1054
  172.5 72.8 %collective-permute-start.24 = (bf16[768,384]{1,0:T(8,128)(2,1)}, bf16[768,384]{1,0:T(8,128)(2,1)S(1)}, u32[]{:S(2)}, u32[]{:S(2)}) collective-permute-start(bf16[768,384]{1,0:T(8,128)(2,1)} %constant_dynamic-slice_fusion), channel_id=1, source_target_pairs={{0,1},{1,0},{2,3},{3,2},{4,5},{5,4},{6,7},{7,6},{8,9},{9,8},{10,11... | collective-permute-start | bytes 1769480 | tf_op jit(solution)/shard_map/ppermute | solution.py:1054
  249.0 14.5 %collective-permute-start.27 = (bf16[416,768]{1,0:T(8,128)(2,1)}, bf16[416,768]{1,0:T(8,128)(2,1)S(1)}, u32[]{:S(2)}, u32[]{:S(2)}) collective-permute-start(bf16[416,768]{1,0:T(8,128)(2,1)} %get-tuple-element.339), channel_id=1, source_target_pairs={{0,2},{2,0},{4,6},{6,4},{8,10},{10,8},{12,14},{14,12},{16,18},{18,... | collective-permute-start | bytes 1916936 | tf_op jit(solution)/shard_map/ppermute | solution.py:825
  249.7 14.7 %collective-permute-start.28 = (bf16[416,768]{1,0:T(8,128)(2,1)}, bf16[416,768]{1,0:T(8,128)(2,1)S(1)}, u32[]{:S(2)}, u32[]{:S(2)}) collective-permute-start(bf16[416,768]{1,0:T(8,128)(2,1)} %get-tuple-element.340), channel_id=1, source_target_pairs={{0,4},{2,6},{4,0},{6,2},{8,12},{10,14},{12,8},{14,10},{16,20},{18,... | collective-permute-start | bytes 1916936 | tf_op jit(solution)/shard_map/ppermute | solution.py:825
  251.2 14.8 %collective-permute-start.29 = (bf16[416,768]{1,0:T(8,128)(2,1)}, bf16[416,768]{1,0:T(8,128)(2,1)S(1)}, u32[]{:S(2)}, u32[]{:S(2)}) collective-permute-start(bf16[416,768]{1,0:T(8,128)(2,1)} %get-tuple-element.341), channel_id=1, source_target_pairs={{0,8},{2,10},{4,12},{6,14},{8,0},{10,2},{12,4},{14,6},{16,24},{18,... | collective-permute-start | bytes 1916936 | tf_op jit(solution)/shard_map/ppermute | solution.py:825
  270.7 24.4 %collective-permute-start.34 = (bf16[2,32,16,768]{3,2,1,0:T(8,128)(2,1)S(1)}, bf16[2,32,16,768]{3,2,1,0:T(8,128)(2,1)}, u32[]{:S(2)}, u32[]{:S(2)}) collective-permute-start(bf16[2,32,16,768]{3,2,1,0:T(8,128)(2,1)S(1)} %copy-done.15), channel_id=1, source_target_pairs={{0,1},{1,0},{2,3},{3,2},{4,5},{5,4},{6,7},{7,6},{8,9},{9,8},{10,11... | collective-permute-start | bytes 4718600 | tf_op jit(solution)/shard_map/ppermute | solution.py:1054
  274.7 16.6 %collective-permute-start.31 = (bf16[416,768]{1,0:T(8,128)(2,1)}, bf16[416,768]{1,0:T(8,128)(2,1)}, u32[]{:S(2)}, u32[]{:S(2)}) collective-permute-start(bf16[416,768]{1,0:T(8,128)(2,1)} %get-tuple-element.354), channel_id=1, source_target_pairs={{0,2},{2,0},{4,6},{6,4},{8,10},{10,8},{12,14},{14,12},{16,18},{18,... | collective-permute-start | bytes 1916936 | tf_op jit(solution)/shard_map/ppermute | solution.py:825
  276.4 16.3 %collective-permute-start.32 = (bf16[416,768]{1,0:T(8,128)(2,1)}, bf16[416,768]{1,0:T(8,128)(2,1)}, u32[]{:S(2)}, u32[]{:S(2)}) collective-permute-start(bf16[416,768]{1,0:T(8,128)(2,1)} %get-tuple-element.355), channel_id=1, source_target_pairs={{0,4},{2,6},{4,0},{6,2},{8,12},{10,14},{12,8},{14,10},{16,20},{18,... | collective-permute-start | bytes 1916936 | tf_op jit(solution)/shard_map/ppermute | solution.py:825
  276.6 18.4 %collective-permute-start.33 = (bf16[416,768]{1,0:T(8,128)(2,1)}, bf16[416,768]{1,0:T(8,128)(2,1)}, u32[]{:S(2)}, u32[]{:S(2)}) collective-permute-start(bf16[416,768]{1,0:T(8,128)(2,1)} %get-tuple-element.356), channel_id=1, source_target_pairs={{0,8},{2,10},{4,12},{6,14},{8,0},{10,2},{12,4},{14,6},{16,24},{18,... | collective-permute-start | bytes 1916936 | tf_op jit(solution)/shard_map/ppermute | solution.py:825
  300.9 15.2 %collective-permute-start.36 = (bf16[416,768]{1,0:T(8,128)(2,1)}, bf16[416,768]{1,0:T(8,128)(2,1)}, u32[]{:S(2)}, u32[]{:S(2)}) collective-permute-start(bf16[416,768]{1,0:T(8,128)(2,1)} %get-tuple-element.372), channel_id=1, source_target_pairs={{0,2},{2,0},{4,6},{6,4},{8,10},{10,8},{12,14},{14,12},{16,18},{18,... | collective-permute-start | bytes 1916936 | tf_op jit(solution)/shard_map/ppermute | solution.py:825
  301.3 15.0 %collective-permute-start.37 = (bf16[416,768]{1,0:T(8,128)(2,1)}, bf16[416,768]{1,0:T(8,128)(2,1)}, u32[]{:S(2)}, u32[]{:S(2)}) collective-permute-start(bf16[416,768]{1,0:T(8,128)(2,1)} %get-tuple-element.373), channel_id=1, source_target_pairs={{0,4},{2,6},{4,0},{6,2},{8,12},{10,14},{12,8},{14,10},{16,20},{18,... | collective-permute-start | bytes 1916936 | tf_op jit(solution)/shard_map/ppermute | solution.py:825
  302.9 15.0 %collective-permute-start.38 = (bf16[416,768]{1,0:T(8,128)(2,1)}, bf16[416,768]{1,0:T(8,128)(2,1)}, u32[]{:S(2)}, u32[]{:S(2)}) collective-permute-start(bf16[416,768]{1,0:T(8,128)(2,1)} %get-tuple-element.374), channel_id=1, source_target_pairs={{0,8},{2,10},{4,12},{6,14},{8,0},{10,2},{12,4},{14,6},{16,24},{18,... | collective-permute-start | bytes 1916936 | tf_op jit(solution)/shard_map/ppermute | solution.py:825
  325.5 15.2 %collective-permute-start.42 = (bf16[416,768]{1,0:T(8,128)(2,1)}, bf16[416,768]{1,0:T(8,128)(2,1)}, u32[]{:S(2)}, u32[]{:S(2)}) collective-permute-start(bf16[416,768]{1,0:T(8,128)(2,1)} %get-tuple-element.391), channel_id=1, source_target_pairs={{0,8},{2,10},{4,12},{6,14},{8,0},{10,2},{12,4},{14,6},{16,24},{18,... | collective-permute-start | bytes 1916936 | tf_op jit(solution)/shard_map/ppermute | solution.py:825
  (73 other events, 572.3 us)

commit v2 on v1

--- a/solution.py
+++ b/solution.py
@@ -291,11 +291,11 @@
 
 
 ROUNDS = (
-    {"y": "own", "z": "own", "x": "own", "o": "own", "m": "own"},
-    {"z": (0, "m"), "m": (0, "z"), "y": (0, "x"), "x": (0, "z"), "o": (0, "y")},
-    {"x": (1, "z"), "m": (1, "z"), "y": (1, "z"), "z": (1, "m"), "o": (1, "z")},
-    {"z": (0, "y"), "y": (2, "z"), "m": (2, "x"), "x": (2, "z"), "o": (0, "z")},
-    {"x": (3, "y"), "o": (3, "x"), "y": (2, "x"), "z": (1, "y")},
+    {"x": "own", "y": "own", "z": "own", "o": "own", "m": "own"},
+    {"x": (0, "y"), "y": (0, "z"), "z": (0, "m"), "o": (0, "x"), "m": (0, "z")},
+    {"x": (1, "y"), "y": (1, "z"), "z": (1, "m"), "o": (1, "z"), "m": (1, "y")},
+    {"x": (2, "z"), "y": (2, "z"), "z": (0, "x"), "o": (0, "x"), "m": (2, "x")},
+    {"x": (2, "y"), "y": (3, "x"), "z": (3, "x"), "o": (3, "x")},
 )
 PERMS = {
     "x": [(w, w ^ 1) for w in range(16)],
@@ -380,15 +380,19 @@
     return jnp.where(condition, 1.0, 0.0).astype(bf16)
 
 
-def pack_kernel(up, value, proj, out, rate, in_map, out_map, vectors, keep, send, rows):
+def pack_kernel(up, value, proj, out, rate, in_map, out_map, *refs):
+    *vectors, keep, send, rows = refs
     def lanes(n, first):
         return ones_where(iota((n, 256), 1) == iota((n, 256), 0) + first)
 
     rows[...] = jnp.zeros((16, 48), f32)
-    for k in range(6):
-        rows[k : k + 1, :] = vectors[:, 48 * k : 48 * k + 48]
-    for k, n in enumerate((24, 24, 24, 16)):
-        rows[6 + k : 7 + k, :n] = vectors[:, 288 + 24 * k : 288 + 24 * k + n]
+    k = 0
+    for ref in vectors:
+        v = ref[...].astype(f32)
+        for first in range(0, v.shape[0], 48):
+            part = v[first : first + 48]
+            rows[k, : part.shape[0]] = part
+            k += 1
     small = dot(rows[...].astype(bf16), lanes(16, 192), ((0,), (0,)))
     for k, ref in enumerate((rate, in_map, out_map)):
         small = small + dot(ref[...], lanes(64, 64 * k))
@@ -605,11 +609,12 @@
     rate, step, decay_log, decay, gap = mix_parameters(mine)
     weight = mine[:, 128:192] * gap * mine[:, 64:128]
     for v, three, row in ((decay_log, d3, drow), (weight, w3, wrow)):
-        rest = v
-        for k in range(3):
-            part = rest.astype(bf16)
-            three[:, 8 * k : 8 * k + 8, :] = part.reshape(96, 8, 64)
-            rest = rest - part.astype(f32)
+        parts, rest = [], v
+        for _ in range(3):
+            part = rest.astype(bf16).astype(f32)
+            parts.append(part.reshape(96, 8, 64))
+            rest = rest - part
+        three[...] = jnp.concatenate(parts, 1).astype(bf16)
         buf[...] = v
         for c in range(8):
             row[:, 64 * c : 64 * c + 64] = buf[pl.ds(c, 96, stride=8), :]
@@ -832,17 +837,11 @@
 def scatter_all(proj_mine, proj_theirs, out, out_theirs, up, value, small, work, state):
     full = slice(None)
 
-    def lanes():
-        return pl.ds(pl.multiple_of(core_index() * 384, 128), 384)
-
     pieces = [([(i, lambda w: (pl.ds(within_half(w, 192), 192), full)) for i in (0, 1)], (slice(0, 192), full))]
     for k in range(2):
         pieces.append(
             (
-                [
-                    (2, lambda w, k=k: (pl.ds(within_half(w, 96) + 48 * k, 48), lanes())),
-                    (3, lambda w, k=k: (pl.ds(within_half(w, 96) + 48 * k, 48), full)),
-                ],
+                [(i, lambda w, k=k: (pl.ds(within_half(w, 96) + 48 * k, 48), full)) for i in (2, 3)],
                 (slice(192, 240), slice(384 * k, 384 * k + 384)),
             )
         )
@@ -869,7 +868,8 @@
     return scatter_rounds(owns, pieces, 416, final, 248, "sum", work, state)
 
 
-def unpack_kernel(mine, recv, proj, out, up, value, rate, in_map, out_map, vectors, small):
+def unpack_kernel(mine, recv, proj, out, up, value, rate, in_map, out_map, *refs):
+    *vectors, small = refs
     for core in range(2):
 
         @pl.when(core_index() == core)
@@ -891,11 +891,16 @@
     rate[...] = small[:, :64]
     in_map[...] = small[:, 64:128]
     out_map[...] = small[:, 128:192]
-    vectors[...] = small[:, 128:].T[64:80, :]
+    rows = small[:, 128:].T
+    for k, ref in enumerate(vectors[:4] + vectors[5:]):
+        row = 64 + k if k < 4 else 66 + k
+        ref[...] = rows[row, : ref.shape[0]]
+    vectors[4][0:48] = rows[68, :]
+    vectors[4][48:96] = rows[69, :]
 
 
 def unpack(mine, recv):
-    dims = ((96, 1536), (48, 768), (24, 3072), (24, 1536), (48, 64), (48, 64), (48, 64), (16, 48))
+    dims = ((96, 1536), (48, 768), (24, 3072), (24, 1536), (48, 64), (48, 64), (48, 64)) + ((48,),) * 4 + ((96,), (24,), (24,), (24,))
     return pl.pallas_call(
         unpack_kernel,
         out_shape=tuple(shape(d, f32) for d in dims),
@@ -947,7 +952,7 @@
     )(unit, wide, up_w, up_b, value_w, value_b)
 
 
-def gate_kernel(up, up_other, g, mixed, proj_mine, proj_theirs, proj_b, out_a, out_b, gm, gated, gp, grad_b, grad_mine, grad_theirs, grad_out, acc, acc_out, out_w):
+def gate_kernel(up, up_other, g, mixed, proj_mine, proj_theirs, proj_b, out_a, out_b, gm, gated, gp, grad_b, grad_mine, grad_theirs, grad_out, grad_send, acc, acc_out, out_w):
     step, steps = pl.program_id(0), pl.num_programs(0)
 
     @pl.when(step == 0)
@@ -979,7 +984,12 @@
     def _():
         grad_mine[...] = acc[0].astype(bf16)
         grad_theirs[...] = acc[1].astype(bf16)
-        grad_out[...] = acc_out[...].astype(bf16)
+        for core in range(2):
+
+            @pl.when(core_index() == core)
+            def _(core=core):
+                grad_out[...] = acc_out[:, 384 * core : 384 * core + 384].astype(bf16)
+                grad_send[...] = acc_out[:, 384 - 384 * core : 768 - 384 * core].astype(bf16)
 
 
 def gate(up, up_other, g, mixed, proj_mine, proj_theirs, proj_b, out_a, out_b):
@@ -994,13 +1004,14 @@
             shape((1, c), f32),
             shape((f, c), bf16),
             shape((f, c), bf16),
-            shape((c, d), bf16),
+            shape((c, d // 2), bf16),
+            shape((c, d // 2), bf16),
         ),
         grid=(n // TILE,),
         in_specs=[tokens_by(f), tokens_by(f), tokens_by(d), by_tokens(c)]
         + [whole_block(*v.shape) for v in (proj_mine, proj_theirs, proj_b, out_a, out_b)],
         out_specs=(by_tokens(c), tokens_by(c), tokens_by(c), whole_block(1, c))
-        + (whole_block(f, c), whole_block(f, c), whole_block(c, d)),
+        + (whole_block(f, c), whole_block(f, c), whole_block(c, d // 2), whole_block(c, d // 2)),
         scratch_shapes=[pltpu.VMEM((2, f, c), f32), pltpu.VMEM((c, d), f32), pltpu.VMEM((c, d), bf16)],
         compiler_params=params(),
         name="gate",
@@ -1060,7 +1071,6 @@
         return x.reshape(blocks, T, width).transpose(1, 0, 2)
 
     labels = segment.reshape(blocks, T)[:, 0].astype(f32)
-    own_x, own_g = by_place(tokens), by_place(cotangent)
 
     def whole_chip(mine, other):
         return by_core(core, jnp.stack([mine, other], 1), jnp.stack([other, mine], 1)).reshape(2 * tok, width)
@@ -1074,23 +1084,28 @@
 
     if staged:
         vectors = (log_step, skip_gain, bias_value, bias_proj, bias_up, norm_gain, norm_bias, bias_out, labels)
-        vectors = jnp.concatenate([v.astype(f32) for v in vectors])[None]
-        keep, send = pack(w_up, w_value, w_proj, w_out, log_rate, input_map, output_map, vectors)
+        keep, send = pack(w_up, w_value, w_proj, w_out, log_rate, input_map, output_map, *vectors)
         recv = swap(send)
         other_labels = recv[192:208, 201]
         blob = merge(keep, recv)
-        other_x, other_g = swap(own_x), swap(own_g)
         idle = lambda state: state
 
+        def own_tokens(state):
+            return jnp.stack([by_place(v) for v in state])
+
+        def other_tokens(state):
+            return state, swap(state)
+
         def chip_tokens(state):
-            (mine_x, their_x), (mine_g, their_g) = state
-            return whole_chip(mine_x, their_x), whole_chip(mine_g, their_g)
+            mine, theirs = state
+            return mine, whole_chip(mine[0], theirs[0]), whole_chip(mine[1], theirs[1])
 
         def chip_unit(state):
-            return normalise(state[0])[0], state[1]
-
-        state = (own_x, other_x), (own_g, other_g)
-        placed, (unit_chip, g_chip) = gather_rounds(blob, [idle, chip_tokens, chip_unit, idle, idle], state)
+            mine, x, g = state
+            return mine, normalise(x)[0], g
+
+        work = [own_tokens, other_tokens, chip_tokens, chip_unit, idle]
+        placed, ((own_x, own_g), unit_chip, g_chip) = gather_rounds(blob, work, (tokens, cotangent))
         up_w, value_w, table, proj_mine, proj_theirs, out_mine, out_theirs = placed
         proj_cross = swap(proj_theirs)
         out_cross = swap(out_theirs)
@@ -1099,6 +1114,7 @@
         coefs = coefficients(table, label_row)
         decay3, weight3, decay_row, weight_row, skip_p, value_b, proj_b, up_b, wide, masks = coefs
     else:
+        own_x, own_g = by_place(tokens), by_place(cotangent)
         other_x, other_g = swap(own_x), swap(own_g)
         unit_chip, g_chip = normalise(whole_chip(own_x, other_x))[0], whole_chip(own_g, other_g)
         other_labels = swap(labels)
@@ -1133,7 +1149,7 @@
     normed_low, up_pre, up_low, value_pre = enter(unit_chip, wide, up_w, up_b, value_w, value_b)
     up_other = swap(up_low)
     mixed, entering = ssm_fwd(direction, value_pre, decay3, weight3, decay_row, weight_row, skip_p, masks)
-    grad_mixed, gated_low, grad_proj_low, grad_proj_b, grad_proj_mine, grad_proj_theirs, grad_out_w = gate(
+    grad_mixed, gated_low, grad_proj_low, grad_proj_b, grad_proj_mine, grad_proj_theirs, grad_out_mine, grad_out_send = gate(
         up_low, up_other, g_chip, mixed, proj_mine, proj_theirs, proj_b, out_mine, out_cross
     )
 
@@ -1182,14 +1198,12 @@
     if staged:
         vectors = (grad_skip, grad_value_b, grad_proj_b, grad_up_b, grad_gain, grad_shift, grad_out_b)
         small = small_sums(table, grad_mix, *vectors)
-        theirs = swap(half_of(grad_out_w, 1 - core, 1))
+        grad_out_cross = swap(grad_out_send)
         work = [split_parts, exchange_parts, finish_result, finish_tokens, idle]
-        grads = (grad_proj_mine, grad_proj_theirs, grad_out_w, theirs, grad_up_w, grad_value_w, small)
+        grads = (grad_proj_mine, grad_proj_theirs, grad_out_mine, grad_out_cross, grad_up_w, grad_value_w, small)
         (mine, send), (result, grad_tokens) = scatter_all(*grads, work, (gated_low, grad_part))
-        sum_proj_w, sum_out_w, sum_up_w, sum_value_w, sum_rate, sum_in, sum_out, sums = unpack(mine, swap(send))
-        sum_step, sum_skip, sum_value_b, sum_proj_b = (sums[k] for k in range(4))
-        sum_up_b = sums[4:6].reshape(96)
-        sum_gain, sum_shift, sum_out_b = (sums[6 + k, :24] for k in range(3))
+        sum_proj_w, sum_out_w, sum_up_w, sum_value_w, sum_rate, sum_in, sum_out, *vectors = unpack(mine, swap(send))
+        sum_step, sum_skip, sum_value_b, sum_proj_b, sum_up_b, sum_gain, sum_shift, sum_out_b = vectors
     else:
 
         grad_mix = grad_mix.T
@@ -1212,7 +1226,7 @@
         result, grad_tokens = finish_tokens(finish_result(exchange_parts(split_parts((gated_low, grad_part)))))
         sum_up_w, sum_value_w = halves(grad_up_w, 1), halves(grad_value_w, 1)
         sum_proj_w = halves(in_order(core, grad_proj_mine, grad_proj_theirs, 0), 1)
-        sum_out_w = halves(grad_out_w, 0)
+        sum_out_w = halves(in_order(core, grad_out_mine, grad_out_send, 1), 0)
         sum_rate, sum_in, sum_out, sum_step = (halves(v, 0) for v in grad_ssm)
         sum_step = sum_step[:, 0]
         sum_skip, sum_value_b, sum_proj_b = (halves(v, 0) for v in (grad_skip[:, 0], grad_value_b[:, 0], grad_proj_b[0]))

time: 382 us -> 377 us (0.987)
  local copies, waits for them, and re-layouts: 24.5 us -> 17.9 us
  waiting for transfers between devices: 89.4 us -> 95.5 us
  other arithmetic: 22.8 us -> 18.4 us
    ppermute x19, waiting for transfers between devices: 41.3 us -> 45.9 us  [gather_rounds(): lax.ppermute(block, 'wide', PERMS[d])]
  transfers between devices with their start and end apart: 48 -> 47, of which waited for: 30 -> 31; matrix products, arithmetic and copies ran while one was open for 16% -> 15% of each run, Pallas kernels for 26% -> 25%
where the time goes in v2:
time: 377 us; the launch traced here: 370 us
  Pallas kernels  140 us (37%)
  waiting for transfers between devices  95.5 us (25%)
  starting transfers between devices  67.6 us (18%)
  matrix products  28.7 us (8%)
  other arithmetic  18.4 us (5%)
  local copies, waits for them, and re-layouts  17.9 us (5%)
    pallas_call x2, Pallas kernels, mix_call(): pl.pallas_call(body, out_shape=out_shape, grid=(steps,), in_specs=in_spec...  60.4 us
    ppermute x19, waiting for transfers between devices, gather_rounds(): lax.ppermute(block, 'wide', PERMS[d])  45.9 us
    ppermute x19, waiting for transfers between devices, scatter_rounds(): lax.ppermute(block, 'wide', PERMS[slot[1]])  45.2 us
    ppermute x19, starting transfers between devices, gather_rounds(): lax.ppermute(block, 'wide', PERMS[d])  32.3 us
    ppermute x19, starting transfers between devices, scatter_rounds(): lax.ppermute(block, 'wide', PERMS[slot[1]])  31.2 us
    dot_general x7, matrix products, contract(): lax.dot_general(left, right, (((left_dim,), (right_dim,)), ((), ())), pre...  28.7 us
    pallas_call x6, Pallas kernels, sum_slots(): pl.pallas_call(functools.partial(sum_kernel, slots, pieces, len(owns), ar...  23.1 us
    pallas_call x1, Pallas kernels, gate(): pl.pallas_call(gate_kernel, out_shape=(shape((c, n), f32), shape((n, c),...  21.4 us
  transfers between devices with their start and end apart: 47, of which 31 were waited for; matrix products, arithmetic and copies ran while one was open for 15% of the time, Pallas kernels for 25%

profile of v2, /device:TPU:0, one launch (start us, length us, event | category | flops | bytes accessed | tf_op | source)
XLA Modules:
  0.0 370.0 jit_solution(13466577889488793359)
XLA Ops:
  15.3 4.4 %collective-permute-start.4 = (bf16[416,768]{1,0:T(8,128)(2,1)}, bf16[416,768]{1,0:T(8,128)(2,1)}, u32[]{:S(2)}, u32[]{:S(2)}) collective-permute-start(bf16[416,768]{1,0:T(8,128)(2,1)} %merge_pair.1.refs_0_), channel_id=1, source_target_pairs={{0,8},{2,10},{4,12},{6,14},{8,0},{10,2},{12,4},{14,6},{16,24},{18,... | collective-permute-start | bytes 1916936 | tf_op jit(solution)/shard_map/ppermute | solution.py:477
  20.7 8.0 %collective-permute-done.2.refs_2_ = bf16[416,768]{1,0:T(8,128)(2,1)S(1)} collective-permute-done((bf16[416,768]{1,0:T(8,128)(2,1)}, bf16[416,768]{1,0:T(8,128)(2,1)S(1)}, u32[]{:S(2)}, u32[]{:S(2)}) %collective-permute-start.2) | collective-permute-done | bytes 639008 | tf_op jit(solution)/shard_map/ppermute | solution.py:477
  39.9 12.7 %collective-permute-done.6.refs_6_ = bf16[416,768]{1,0:T(8,128)(2,1)} collective-permute-done((bf16[416,768]{1,0:T(8,128)(2,1)}, bf16[416,768]{1,0:T(8,128)(2,1)}, u32[]{:S(2)}, u32[]{:S(2)}) %collective-permute-start.6) | collective-permute-done | bytes 639008 | tf_op jit(solution)/shard_map/ppermute | solution.py:477
  66.2 5.7 %collective-permute-done.11.refs_10_ = bf16[416,768]{1,0:T(8,128)(2,1)S(1)} collective-permute-done((bf16[416,768]{1,0:T(8,128)(2,1)}, bf16[416,768]{1,0:T(8,128)(2,1)S(1)}, u32[]{:S(2)}, u32[]{:S(2)}) %collective-permute-start.11) | collective-permute-done | bytes 639008 | tf_op jit(solution)/shard_map/ppermute | solution.py:477
  83.8 6.2 %collective-permute-done.15.refs_14_ = bf16[416,768]{1,0:T(8,128)(2,1)S(1)} collective-permute-done((bf16[416,768]{1,0:T(8,128)(2,1)S(1)}, bf16[416,768]{1,0:T(8,128)(2,1)S(1)}, u32[]{:S(2)}, u32[]{:S(2)}) %collective-permute-start.15) | collective-permute-done | bytes 639008 | tf_op jit(solution)/shard_map/ppermute | solution.py:477
  98.6 6.4 %place_first.1 = (bf16[768,1536]{1,0:T(8,128)(2,1)}, bf16[768,768]{1,0:T(8,128)(2,1)}, bf16[1536,256]{1,0:T(8,128)(2,1)}, bf16[1536,768]{1,0:T(8,128)(2,1)}, bf1...) custom-call(bf16[416,768]{1,0:T(8,128)(2,1)} %merge_pair.1.refs_0_, ...), custom_call_target="tpu_custom_call" | custom-call | tf_op jit(solution)/shard_map/place_first/pallas_call | solution.py:534
  109.2 4.3 %coefficients.1 = (bf16[96,24,64]{2,1,0:T(8,128)(2,1)}, bf16[96,24,64]{2,1,0:T(8,128)(2,1)}, f32[96,512]{1,0:T(8,128)}, f32[96,512]{1,0:T(8,128)}, f32[768,1]{1,...) custom-call(bf16[1536,256]{1,0:T(8,128)(2,1)} %get-tuple-element.302, ...), custom_call_target="tpu_custom_call" | custom-call | tf_op jit(solution)/shard_map/coefficients/pallas_call | solution.py:647
  113.5 9.9 %enter.1 = (bf16[1024,768]{1,0:T(8,128)(2,1)}, f32[1024,1536]{1,0:T(8,128)}, bf16[1024,1536]{1,0:T(8,128)(2,1)}, f32[768,1024]{1,0:T(8,128)}) custom-call(f32[1024,768]{1,0:T(8,128)} %fusion.9.unit, f32[3,768]{1,0:T(4,128)} %get-tuple-element.303.wide, bf16[768,1536]{1,0:T(8,128)(2,1)} %get-tuple-element.304.up_w, f32[1,1536]{1,0:T(1,128)} %get-tuple-element.305.up_b, ...), custom_call_target="tpu_custom_call" | custom-call | tf_op jit(solution)/shard_map/enter/pallas_call | solution.py:944
  124.0 24.1 %mix_forward_0.1 = (f32[768,1024]{1,0:T(8,128)}, f32[96,64,256]{2,1,0:T(8,128)}) custom-call(s32[1]{0:T(128)} %bitcast.12.dir_ref, f32[768,1024]{1,0:T(8,128)} %get-tuple-element.310.x_ref, bf16[96,24,64]{2,1,0:T(8,128)(2,1)} %get-tuple-element.311.d3_ref, bf16[96,24,64]{2,1,0:T(8,128)(2,1)} %get-tuple-element.312.w3_ref, ...), custom_call_target="tpu_custom_call" | custom-call | tf_op jit(solution)/shard_map/mix_forward_0/pallas_call | solution.py:232
  148.9 21.4 %gate.1 = (f32[768,1024]{1,0:T(8,128)}, bf16[1024,768]{1,0:T(8,128)(2,1)}, bf16[1024,768]{1,0:T(8,128)(2,1)}, f32[1,768]{1,0:T(1,128)}, bf16[1536,768]{1,0:T(8,1...) custom-call(bf16[1024,1536]{1,0:T(8,128)(2,1)} %get-tuple-element.308.up, ...), custom_call_target="tpu_custom_call" | custom-call | tf_op jit(solution)/shard_map/gate/pallas_call | solution.py:998
  171.8 36.3 %mix_backward_0.1 = (bf16[768,1024]{1,0:T(8,128)(2,1)}, f32[128,768]{1,0:T(8,128)}, f32[768,1]{1,0:T(8,128)}, f32[768,1]{1,0:T(8,128)}) custom-call(s32[1]{0:T(128)} %bitcast.12.dir_ref, f32[768,1024]{1,0:T(8,128)} %get-tuple-element.310.x_ref, f32[768,1024]{1,0:T(8,128)} %get-tuple-element.330.gm_ref, f32[96,64,256]{2,1,0:T(8,128)} %get-tuple-element.331.enter_ref, ...), custom_call_target="tpu_custom_call" | custom-call | tf_op jit(solution)/shard_map/mix_backward_0/pallas_call | solution.py:232
  214.8 4.9 %fusion.42 = f32[1024,1536]{1,0:T(8,128)S(1)} fusion(bf16[1024,768]{1,0:T(8,128)(2,1)} %collective-permute-done.24, bf16[1536,768]{1,0:T(8,128)(2,1)} %collective-permute-done.25), kind=kOutput, calls=%fused_computation.84 | convolution fusion | flops 2415919104 | bytes 10223616 | tf_op jit(solution)/shard_map/dot_general | solution.py:1022
  219.8 5.6 %convert_reduce_fusion = (f32[1536]{0:T(1024)S(1)}, bf16[1024,1536]{1,0:T(8,128)(2,1)}) fusion(f32[1024,1536]{1,0:T(8,128)S(1)} %bitcast.111, f32[1024,1536]{1,0:T(8,128)S(1)} %fusion.41, f32[1024,1536]{1,0:T(8,128)S(1)} %fusion.42), kind=kLoop, calls=%fused_computation.11 | loop fusion | flops 34601472 | bytes 22026240 | tf_op jit(solution)/shard_map/reduce_sum | solution.py:1162
  225.5 4.7 %fusion.43 = f32[1024,768]{1,0:T(8,128)S(1)} fusion(bf16[1024,1536]{1,0:T(8,128)(2,1)} %get-tuple-element.446, bf16[768,1536]{1,0:T(8,128)(2,1)S(1)} %copy-done.5), kind=kOutput, calls=%fused_computation.85 | convolution fusion | flops 2415919104 | bytes 8650752 | tf_op jit(solution)/shard_map/dot_general | solution.py:1022
  235.2 5.1 %small_sums.1.refs_6_ = f32[16,32,768]{2,1,0:T(8,128)} custom-call(bf16[1536,256]{1,0:T(8,128)(2,1)} %get-tuple-element.302.table, f32[128,768]{1,0:T(8,128)} %get-tuple-element.333.grads, f32[768,1]{1,0:T(8,128)} %get-tuple-element.334.skip, f32[768,1]{1,0:T(8,128)} %get-tuple-element.335.value_b, f32[1,768]{1,0:T(1,128)} %get-tuple-element.336.proj_b, ...), custom_call_target="tpu_custom_call" | custom-call | tf_op jit(solution)/shard_map/small_sums/pallas_call | solution.py:693
  240.4 5.9 %convolution_convert_fusion.refs_4_ = bf16[768,1536]{1,0:T(8,128)(2,1)} fusion(bf16[1024,768]{1,0:T(8,128)(2,1)S(1)} %copy-done.38, bf16[1024,1536]{1,0:T(8,128)(2,1)} %get-tuple-element.446), kind=kOutput, calls=%fused_computation.16 | convolution fusion | flops 2417098752 | bytes 7077888 | tf_op jit(solution)/shard_map/dot_general | solution.py:1022
  260.3 4.2 %collective-permute-done.26.refs_8_ = bf16[416,768]{1,0:T(8,128)(2,1)S(1)} collective-permute-done((bf16[416,768]{1,0:T(8,128)(2,1)}, bf16[416,768]{1,0:T(8,128)(2,1)S(1)}, u32[]{:S(2)}, u32[]{:S(2)}) %collective-permute-start.26) | collective-permute-done | bytes 639008 | tf_op jit(solution)/shard_map/ppermute | solution.py:830
  276.4 4.3 %collective-permute-start.32 = (bf16[416,768]{1,0:T(8,128)(2,1)}, bf16[416,768]{1,0:T(8,128)(2,1)}, u32[]{:S(2)}, u32[]{:S(2)}) collective-permute-start(bf16[416,768]{1,0:T(8,128)(2,1)} %get-tuple-element.359), channel_id=1, source_target_pairs={{0,8},{2,10},{4,12},{6,14},{8,0},{10,2},{12,4},{14,6},{16,24},{18,... | collective-permute-start | bytes 1916936 | tf_op jit(solution)/shard_map/ppermute | solution.py:830
  280.8 10.5 %collective-permute-done.30.refs_9_ = bf16[416,768]{1,0:T(8,128)(2,1)} collective-permute-done((bf16[416,768]{1,0:T(8,128)(2,1)}, bf16[416,768]{1,0:T(8,128)(2,1)}, u32[]{:S(2)}, u32[]{:S(2)}) %collective-permute-start.30) | collective-permute-done | bytes 639008 | tf_op jit(solution)/shard_map/ppermute | solution.py:830
  310.0 4.9 %collective-permute-done.35.refs_7_ = bf16[416,768]{1,0:T(8,128)(2,1)} collective-permute-done((bf16[416,768]{1,0:T(8,128)(2,1)}, bf16[416,768]{1,0:T(8,128)(2,1)}, u32[]{:S(2)}, u32[]{:S(2)}) %collective-permute-start.35) | collective-permute-done | bytes 639008 | tf_op jit(solution)/shard_map/ppermute | solution.py:830
  318.0 4.1 %sum_1.1 = (bf16[416,768]{1,0:T(8,128)(2,1)}, bf16[416,768]{1,0:T(8,128)(2,1)}, bf16[416,768]{1,0:T(8,128)(2,1)}, bf16[416,768]{1,0:T(8,128)(2,1)}) custom-call(bf16[1536,768]{1,0:T(8,128)(2,1)} %get-tuple-element.323.refs_0_, bf16[1536,768]{1,0:T(8,128)(2,1)} %get-tuple-element.324.refs_1_, bf16[768,384]{1,0:T(8,128)(2,1)} %get-tuple-element.325.refs_2_, ...), custom_call_target="tpu_custom_call" | custom-call | tf_op jit(solution)/shard_map/sum_1/pallas_call | solution.py:804
  325.1 4.2 %collective-permute-start.41 = (bf16[416,768]{1,0:T(8,128)(2,1)}, bf16[416,768]{1,0:T(8,128)(2,1)}, u32[]{:S(2)}, u32[]{:S(2)}) collective-permute-start(bf16[416,768]{1,0:T(8,128)(2,1)} %get-tuple-element.394), channel_id=1, source_target_pairs={{0,8},{2,10},{4,12},{6,14},{8,0},{10,2},{12,4},{14,6},{16,24},{18,... | collective-permute-start | bytes 1916936 | tf_op jit(solution)/shard_map/ppermute | solution.py:830
  339.9 4.3 %sum_0.1 = (bf16[416,768]{1,0:T(8,128)(2,1)}, bf16[416,768]{1,0:T(8,128)(2,1)}, bf16[416,768]{1,0:T(8,128)(2,1)}, bf16[416,768]{1,0:T(8,128)(2,1)}) custom-call(bf16[1536,768]{1,0:T(8,128)(2,1)} %get-tuple-element.323.refs_0_, bf16[1536,768]{1,0:T(8,128)(2,1)} %get-tuple-element.324.refs_1_, bf16[768,384]{1,0:T(8,128)(2,1)} %get-tuple-element.325.refs_2_, ...), custom_call_target="tpu_custom_call" | custom-call | tf_op jit(solution)/shard_map/sum_0/pallas_call | solution.py:804
  350.7 5.8 %collective-permute-done.43.refs_7_ = bf16[416,768]{1,0:T(8,128)(2,1)S(1)} collective-permute-done((bf16[416,768]{1,0:T(8,128)(2,1)}, bf16[416,768]{1,0:T(8,128)(2,1)S(1)}, u32[]{:S(2)}, u32[]{:S(2)}) %collective-permute-start.43) | collective-permute-done | bytes 639008 | tf_op jit(solution)/shard_map/ppermute | solution.py:830
  (218 shorter events, 160.4 us)
Async XLA Ops:
  10.8 17.8 %collective-permute-start.2 = (bf16[416,768]{1,0:T(8,128)(2,1)}, bf16[416,768]{1,0:T(8,128)(2,1)S(1)}, u32[]{:S(2)}, u32[]{:S(2)}) collective-permute-start(bf16[416,768]{1,0:T(8,128)(2,1)} %merge_pair.1.refs_0_), channel_id=1, source_target_pairs={{0,2},{2,0},{4,6},{6,4},{8,10},{10,8},{12,14},{14,12},{16,18},{18,... | collective-permute-start | bytes 1916936 | tf_op jit(solution)/shard_map/ppermute | solution.py:477
  13.7 16.4 %collective-permute-start.3 = (bf16[416,768]{1,0:T(8,128)(2,1)}, bf16[416,768]{1,0:T(8,128)(2,1)S(1)}, u32[]{:S(2)}, u32[]{:S(2)}) collective-permute-start(bf16[416,768]{1,0:T(8,128)(2,1)} %merge_pair.1.refs_0_), channel_id=1, source_target_pairs={{0,4},{2,6},{4,0},{6,2},{8,12},{10,14},{12,8},{14,10},{16,20},{18,... | collective-permute-start | bytes 1916936 | tf_op jit(solution)/shard_map/ppermute | solution.py:477
  15.3 18.5 %collective-permute-start.4 = (bf16[416,768]{1,0:T(8,128)(2,1)}, bf16[416,768]{1,0:T(8,128)(2,1)}, u32[]{:S(2)}, u32[]{:S(2)}) collective-permute-start(bf16[416,768]{1,0:T(8,128)(2,1)} %merge_pair.1.refs_0_), channel_id=1, source_target_pairs={{0,8},{2,10},{4,12},{6,14},{8,0},{10,2},{12,4},{14,6},{16,24},{18,... | collective-permute-start | bytes 1916936 | tf_op jit(solution)/shard_map/ppermute | solution.py:477
  34.7 19.7 %collective-permute-start.9 = (bf16[2,32,16,768]{3,2,1,0:T(8,128)(2,1)S(1)}, bf16[2,32,16,768]{3,2,1,0:T(8,128)(2,1)}, u32[]{:S(2)}, u32[]{:S(2)}) collective-permute-start(bf16[2,32,16,768]{3,2,1,0:T(8,128)(2,1)S(1)} %pad_maximum_fusion), channel_id=1, source_target_pairs={{0,1},{1,0},{2,3},{3,2},{4,5},{5,4},{6,7},{7,6},{8,9},{9,8},{10,11... | collective-permute-start | bytes 4718600 | tf_op jit(solution)/shard_map/ppermute | solution.py:1065
  35.4 17.2 %collective-permute-start.6 = (bf16[416,768]{1,0:T(8,128)(2,1)}, bf16[416,768]{1,0:T(8,128)(2,1)}, u32[]{:S(2)}, u32[]{:S(2)}) collective-permute-start(bf16[416,768]{1,0:T(8,128)(2,1)} %copy-done.25), channel_id=1, source_target_pairs={{0,2},{2,0},{4,6},{6,4},{8,10},{10,8},{12,14},{14,12},{16,18},{18,... | collective-permute-start | bytes 1916936 | tf_op jit(solution)/shard_map/ppermute | solution.py:477
  36.0 16.8 %collective-permute-start.7 = (bf16[416,768]{1,0:T(8,128)(2,1)}, bf16[416,768]{1,0:T(8,128)(2,1)}, u32[]{:S(2)}, u32[]{:S(2)}) collective-permute-start(bf16[416,768]{1,0:T(8,128)(2,1)} %collective-permute-done.4.refs_4_), channel_id=1, source_target_pairs={{0,4},{2,6},{4,0},{6,2},{8,12},{10,14},{12,8},{14,10},{16,20},{18,... | collective-permute-start | bytes 1916936 | tf_op jit(solution)/shard_map/ppermute | solution.py:477
  36.5 17.9 %collective-permute-start.8 = (bf16[416,768]{1,0:T(8,128)(2,1)}, bf16[416,768]{1,0:T(8,128)(2,1)}, u32[]{:S(2)}, u32[]{:S(2)}) collective-permute-start(bf16[416,768]{1,0:T(8,128)(2,1)} %broadcast_select_fusion.1), channel_id=1, source_target_pairs={{0,8},{2,10},{4,12},{6,14},{8,0},{10,2},{12,4},{14,6},{16,24},{18,... | collective-permute-start | bytes 1916936 | tf_op jit(solution)/shard_map/ppermute | solution.py:477
  56.3 15.7 %collective-permute-start.11 = (bf16[416,768]{1,0:T(8,128)(2,1)}, bf16[416,768]{1,0:T(8,128)(2,1)S(1)}, u32[]{:S(2)}, u32[]{:S(2)}) collective-permute-start(bf16[416,768]{1,0:T(8,128)(2,1)} %collective-permute-done.7.refs_7_), channel_id=1, source_target_pairs={{0,2},{2,0},{4,6},{6,4},{8,10},{10,8},{12,14},{14,12},{16,18},{18,... | collective-permute-start | bytes 1916936 | tf_op jit(solution)/shard_map/ppermute | solution.py:477
  57.8 15.4 %collective-permute-start.12 = (bf16[416,768]{1,0:T(8,128)(2,1)}, bf16[416,768]{1,0:T(8,128)(2,1)}, u32[]{:S(2)}, u32[]{:S(2)}) collective-permute-start(bf16[416,768]{1,0:T(8,128)(2,1)} %collective-permute-done.8.refs_8_), channel_id=1, source_target_pairs={{0,4},{2,6},{4,0},{6,2},{8,12},{10,14},{12,8},{14,10},{16,20},{18,... | collective-permute-start | bytes 1916936 | tf_op jit(solution)/shard_map/ppermute | solution.py:477
  59.4 15.9 %collective-permute-start.13 = (bf16[416,768]{1,0:T(8,128)(2,1)S(1)}, bf16[416,768]{1,0:T(8,128)(2,1)S(1)}, u32[]{:S(2)}, u32[]{:S(2)}) collective-permute-start(bf16[416,768]{1,0:T(8,128)(2,1)S(1)} %broadcast_select_fusion), channel_id=1, source_target_pairs={{0,8},{2,10},{4,12},{6,14},{8,0},{10,2},{12,4},{14,6},{16,24},{18,... | collective-permute-start | bytes 1916936 | tf_op jit(solution)/shard_map/ppermute | solution.py:477
  123.4 24.7 %collective-permute-start.21 = (bf16[1024,1536]{1,0:T(8,128)(2,1)}, bf16[1024,1536]{1,0:T(8,128)(2,1)}, u32[]{:S(2)}, u32[]{:S(2)}) collective-permute-start(bf16[1024,1536]{1,0:T(8,128)(2,1)} %get-tuple-element.308.up), channel_id=1, source_target_pairs={{0,1},{1,0},{2,3},{3,2},{4,5},{5,4},{6,7},{7,6},{8,9},{9,8},{10,11... | collective-permute-start | bytes 9437192 | tf_op jit(solution)/shard_map/ppermute | solution.py:1065
  123.4 91.4 %collective-permute-start.25 = (bf16[1536,768]{1,0:T(8,128)(2,1)}, bf16[1536,768]{1,0:T(8,128)(2,1)}, u32[]{:S(2)}, u32[]{:S(2)}) collective-permute-start(bf16[1536,768]{1,0:T(8,128)(2,1)} %get-tuple-element.319.proj_theirs), channel_id=1, source_target_pairs={{0,1},{1,0},{2,3},{3,2},{4,5},{5,4},{6,7},{7,6},{8,9},{9,8},{10,11... | collective-permute-start | bytes 7077896 | tf_op jit(solution)/shard_map/ppermute | solution.py:1065
  123.9 24.2 %collective-permute-start.22 = (bf16[768,384]{1,0:T(8,128)(2,1)S(1)}, bf16[768,384]{1,0:T(8,128)(2,1)S(1)}, u32[]{:S(2)}, u32[]{:S(2)}) collective-permute-start(bf16[768,384]{1,0:T(8,128)(2,1)S(1)} %copy-done.35), channel_id=1, source_target_pairs={{0,1},{1,0},{2,3},{3,2},{4,5},{5,4},{6,7},{7,6},{8,9},{9,8},{10,11... | collective-permute-start | bytes 1769480 | tf_op jit(solution)/shard_map/ppermute | solution.py:1065
  170.3 44.5 %collective-permute-start.24 = (bf16[1024,768]{1,0:T(8,128)(2,1)}, bf16[1024,768]{1,0:T(8,128)(2,1)}, u32[]{:S(2)}, u32[]{:S(2)}) collective-permute-start(bf16[1024,768]{1,0:T(8,128)(2,1)} %get-tuple-element.328), channel_id=1, source_target_pairs={{0,1},{1,0},{2,3},{3,2},{4,5},{5,4},{6,7},{7,6},{8,9},{9,8},{10,11... | collective-permute-start | bytes 4718600 | tf_op jit(solution)/shard_map/ppermute | solution.py:1065
  171.3 74.9 %collective-permute-start.23 = (bf16[768,384]{1,0:T(8,128)(2,1)}, bf16[768,384]{1,0:T(8,128)(2,1)S(1)}, u32[]{:S(2)}, u32[]{:S(2)}) collective-permute-start(bf16[768,384]{1,0:T(8,128)(2,1)} %get-tuple-element.326), channel_id=1, source_target_pairs={{0,1},{1,0},{2,3},{3,2},{4,5},{5,4},{6,7},{7,6},{8,9},{9,8},{10,11... | collective-permute-start | bytes 1769480 | tf_op jit(solution)/shard_map/ppermute | solution.py:1065
  251.2 14.8 %collective-permute-start.27 = (bf16[416,768]{1,0:T(8,128)(2,1)}, bf16[416,768]{1,0:T(8,128)(2,1)}, u32[]{:S(2)}, u32[]{:S(2)}) collective-permute-start(bf16[416,768]{1,0:T(8,128)(2,1)} %get-tuple-element.343), channel_id=1, source_target_pairs={{0,4},{2,6},{4,0},{6,2},{8,12},{10,14},{12,8},{14,10},{16,20},{18,... | collective-permute-start | bytes 1916936 | tf_op jit(solution)/shard_map/ppermute | solution.py:830
  252.4 15.1 %collective-permute-start.28 = (bf16[416,768]{1,0:T(8,128)(2,1)}, bf16[416,768]{1,0:T(8,128)(2,1)}, u32[]{:S(2)}, u32[]{:S(2)}) collective-permute-start(bf16[416,768]{1,0:T(8,128)(2,1)} %get-tuple-element.344), channel_id=1, source_target_pairs={{0,8},{2,10},{4,12},{6,14},{8,0},{10,2},{12,4},{14,6},{16,24},{18,... | collective-permute-start | bytes 1916936 | tf_op jit(solution)/shard_map/ppermute | solution.py:830
  271.5 23.3 %collective-permute-start.33 = (bf16[2,32,16,768]{3,2,1,0:T(8,128)(2,1)S(1)}, bf16[2,32,16,768]{3,2,1,0:T(8,128)(2,1)}, u32[]{:S(2)}, u32[]{:S(2)}) collective-permute-start(bf16[2,32,16,768]{3,2,1,0:T(8,128)(2,1)S(1)} %pad_maximum_fusion.1), channel_id=1, source_target_pairs={{0,1},{1,0},{2,3},{3,2},{4,5},{5,4},{6,7},{7,6},{8,9},{9,8},{10,11... | collective-permute-start | bytes 4718600 | tf_op jit(solution)/shard_map/ppermute | solution.py:1065
  274.6 16.7 %collective-permute-start.30 = (bf16[416,768]{1,0:T(8,128)(2,1)}, bf16[416,768]{1,0:T(8,128)(2,1)}, u32[]{:S(2)}, u32[]{:S(2)}) collective-permute-start(bf16[416,768]{1,0:T(8,128)(2,1)} %get-tuple-element.357), channel_id=1, source_target_pairs={{0,2},{2,0},{4,6},{6,4},{8,10},{10,8},{12,14},{14,12},{16,18},{18,... | collective-permute-start | bytes 1916936 | tf_op jit(solution)/shard_map/ppermute | solution.py:830
  275.3 16.3 %collective-permute-start.31 = (bf16[416,768]{1,0:T(8,128)(2,1)}, bf16[416,768]{1,0:T(8,128)(2,1)}, u32[]{:S(2)}, u32[]{:S(2)}) collective-permute-start(bf16[416,768]{1,0:T(8,128)(2,1)} %get-tuple-element.358), channel_id=1, source_target_pairs={{0,4},{2,6},{4,0},{6,2},{8,12},{10,14},{12,8},{14,10},{16,20},{18,... | collective-permute-start | bytes 1916936 | tf_op jit(solution)/shard_map/ppermute | solution.py:830
  276.4 18.4 %collective-permute-start.32 = (bf16[416,768]{1,0:T(8,128)(2,1)}, bf16[416,768]{1,0:T(8,128)(2,1)}, u32[]{:S(2)}, u32[]{:S(2)}) collective-permute-start(bf16[416,768]{1,0:T(8,128)(2,1)} %get-tuple-element.359), channel_id=1, source_target_pairs={{0,8},{2,10},{4,12},{6,14},{8,0},{10,2},{12,4},{14,6},{16,24},{18,... | collective-permute-start | bytes 1916936 | tf_op jit(solution)/shard_map/ppermute | solution.py:830
  299.7 15.2 %collective-permute-start.35 = (bf16[416,768]{1,0:T(8,128)(2,1)}, bf16[416,768]{1,0:T(8,128)(2,1)}, u32[]{:S(2)}, u32[]{:S(2)}) collective-permute-start(bf16[416,768]{1,0:T(8,128)(2,1)} %get-tuple-element.375), channel_id=1, source_target_pairs={{0,2},{2,0},{4,6},{6,4},{8,10},{10,8},{12,14},{14,12},{16,18},{18,... | collective-permute-start | bytes 1916936 | tf_op jit(solution)/shard_map/ppermute | solution.py:830
  300.8 14.9 %collective-permute-start.36 = (bf16[416,768]{1,0:T(8,128)(2,1)}, bf16[416,768]{1,0:T(8,128)(2,1)}, u32[]{:S(2)}, u32[]{:S(2)}) collective-permute-start(bf16[416,768]{1,0:T(8,128)(2,1)} %get-tuple-element.376), channel_id=1, source_target_pairs={{0,4},{2,6},{4,0},{6,2},{8,12},{10,14},{12,8},{14,10},{16,20},{18,... | collective-permute-start | bytes 1916936 | tf_op jit(solution)/shard_map/ppermute | solution.py:830
  302.0 16.0 %collective-permute-start.37 = (bf16[416,768]{1,0:T(8,128)(2,1)}, bf16[416,768]{1,0:T(8,128)(2,1)}, u32[]{:S(2)}, u32[]{:S(2)}) collective-permute-start(bf16[416,768]{1,0:T(8,128)(2,1)} %get-tuple-element.377), channel_id=1, source_target_pairs={{0,8},{2,10},{4,12},{6,14},{8,0},{10,2},{12,4},{14,6},{16,24},{18,... | collective-permute-start | bytes 1916936 | tf_op jit(solution)/shard_map/ppermute | solution.py:830
  (65 other events, 647.6 us)

commit v3 on v2

--- a/solution.py
+++ b/solution.py
@@ -675,10 +675,11 @@
     for k, ref in enumerate((skip, value_b)):
         buf[half, 193 + k : 194 + k] = ref[...]
     buf[half, 195:196] = jnp.broadcast_to(proj_b[...], (8, 768)).T[:, :1]
+    units, widths = up_b[...], [ref[...] for ref in (gain, shift, out_b)]
     for q in range(32):
-        turn_buf[q : q + 1, 0:48] = up_b[:, 48 * q : 48 * q + 48]
-        for k, ref in enumerate((gain, shift, out_b)):
-            turn_buf[32 + 3 * q + k : 33 + 3 * q + k, 0:24] = ref[:, 24 * q : 24 * q + 24]
+        turn_buf[q, 0:48] = units[48 * q : 48 * q + 48]
+        for k, v in enumerate(widths):
+            turn_buf[32 + 3 * q + k, 0:24] = v[24 * q : 24 * q + 24]
     columns = turn_buf[...].T
     for q in range(16):
         buf[pl.ds(pl.multiple_of(core_index() * 768 + 48 * q, 16), 48), 196:198] = columns[:48, 2 * q : 2 * q + 2]
@@ -1159,7 +1160,7 @@
     )
     grad_up_act = contract(grad_proj_low, proj_mine, 1, 1) + contract(grad_proj_other, proj_cross, 1, 1)
     grad_up_low = (grad_up_act * gelu_grad(up_pre)).astype(bf16)
-    grad_up_b = jnp.sum(grad_up_low.astype(f32), axis=0, keepdims=True)
+    grad_up_b = jnp.sum(grad_up_low.astype(f32), axis=0)
     grad_up_w = contract(normed_low, grad_up_low, 0, 0).astype(bf16)
     grad_value_w = contract(normed_low, grad_value_low, 0, 1).astype(bf16)
 
@@ -1171,10 +1172,10 @@
         return x.transpose(1, 0, 2).reshape(tok, width)
 
     grad_part = contract(grad_up_low, up_w, 1, 1) + contract(grad_value_low, value_w, 0, 1)
-    grad_gain = jnp.sum(grad_part * unit_chip, axis=0, keepdims=True)
-    grad_shift = jnp.sum(grad_part, axis=0, keepdims=True)
+    grad_gain = jnp.sum(grad_part * unit_chip, axis=0)
+    grad_shift = jnp.sum(grad_part, axis=0)
     own_gf = own_g.astype(f32)
-    grad_out_b = jnp.sum(own_gf, axis=(0, 1))[None]
+    grad_out_b = jnp.sum(own_gf, axis=(0, 1))
 
     def split_parts(state):
         gated, part = state
@@ -1230,8 +1231,8 @@
         sum_rate, sum_in, sum_out, sum_step = (halves(v, 0) for v in grad_ssm)
         sum_step = sum_step[:, 0]
         sum_skip, sum_value_b, sum_proj_b = (halves(v, 0) for v in (grad_skip[:, 0], grad_value_b[:, 0], grad_proj_b[0]))
-        sum_up_b = halves(grad_up_b[0], 0)
-        sum_gain, sum_shift, sum_out_b = share(grad_gain[0]), share(grad_shift[0]), share(grad_out_b[0])
+        sum_up_b = halves(grad_up_b, 0)
+        sum_gain, sum_shift, sum_out_b = share(grad_gain), share(grad_shift), share(grad_out_b)
 
     return (
         result,

time: 377 us -> 377 us (level)
  no operation moved by 1% of the time
where the time goes in v3:
time: 377 us; the launch traced here: 369 us
  Pallas kernels  140 us (37%)
  waiting for transfers between devices  95.5 us (25%)
  starting transfers between devices  67.6 us (18%)
  matrix products  29.3 us (8%)
  other arithmetic  19.6 us (5%)
  local copies, waits for them, and re-layouts  15.6 us (4%)
    pallas_call x2, Pallas kernels, mix_call(): pl.pallas_call(body, out_shape=out_shape, grid=(steps,), in_specs=in_spec...  60.4 us
    ppermute x19, waiting for transfers between devices, gather_rounds(): lax.ppermute(block, 'wide', PERMS[d])  45.9 us
    ppermute x19, waiting for transfers between devices, scatter_rounds(): lax.ppermute(block, 'wide', PERMS[slot[1]])  45.2 us
    ppermute x19, starting transfers between devices, gather_rounds(): lax.ppermute(block, 'wide', PERMS[d])  32.3 us
    ppermute x19, starting transfers between devices, scatter_rounds(): lax.ppermute(block, 'wide', PERMS[slot[1]])  31.2 us
    dot_general x7, matrix products, contract(): lax.dot_general(left, right, (((left_dim,), (right_dim,)), ((), ())), pre...  29.3 us
    pallas_call x6, Pallas kernels, sum_slots(): pl.pallas_call(functools.partial(sum_kernel, slots, pieces, len(owns), ar...  23.1 us
    pallas_call x1, Pallas kernels, gate(): pl.pallas_call(gate_kernel, out_shape=(shape((c, n), f32), shape((n, c),...  21.6 us
  transfers between devices with their start and end apart: 47, of which 31 were waited for; matrix products, arithmetic and copies ran while one was open for 15% of the time, Pallas kernels for 25%

profile of v3, /device:TPU:0, one launch (start us, length us, event | category | flops | bytes accessed | tf_op | source)
XLA Modules:
  0.0 369.5 jit_solution(7401261718894513427)
XLA Ops:
  15.3 4.4 %collective-permute-start.4 = (bf16[416,768]{1,0:T(8,128)(2,1)}, bf16[416,768]{1,0:T(8,128)(2,1)}, u32[]{:S(2)}, u32[]{:S(2)}) collective-permute-start(bf16[416,768]{1,0:T(8,128)(2,1)} %merge_pair.1.refs_0_), channel_id=1, source_target_pairs={{0,8},{2,10},{4,12},{6,14},{8,0},{10,2},{12,4},{14,6},{16,24},{18,... | collective-permute-start | bytes 1916936 | tf_op jit(solution)/shard_map/ppermute | solution.py:477
  20.7 8.0 %collective-permute-done.2.refs_2_ = bf16[416,768]{1,0:T(8,128)(2,1)S(1)} collective-permute-done((bf16[416,768]{1,0:T(8,128)(2,1)}, bf16[416,768]{1,0:T(8,128)(2,1)S(1)}, u32[]{:S(2)}, u32[]{:S(2)}) %collective-permute-start.2) | collective-permute-done | bytes 639008 | tf_op jit(solution)/shard_map/ppermute | solution.py:477
  39.9 12.7 %collective-permute-done.6.refs_6_ = bf16[416,768]{1,0:T(8,128)(2,1)} collective-permute-done((bf16[416,768]{1,0:T(8,128)(2,1)}, bf16[416,768]{1,0:T(8,128)(2,1)}, u32[]{:S(2)}, u32[]{:S(2)}) %collective-permute-start.6) | collective-permute-done | bytes 639008 | tf_op jit(solution)/shard_map/ppermute | solution.py:477
  66.2 5.7 %collective-permute-done.11.refs_10_ = bf16[416,768]{1,0:T(8,128)(2,1)S(1)} collective-permute-done((bf16[416,768]{1,0:T(8,128)(2,1)}, bf16[416,768]{1,0:T(8,128)(2,1)S(1)}, u32[]{:S(2)}, u32[]{:S(2)}) %collective-permute-start.11) | collective-permute-done | bytes 639008 | tf_op jit(solution)/shard_map/ppermute | solution.py:477
  83.8 6.2 %collective-permute-done.15.refs_14_ = bf16[416,768]{1,0:T(8,128)(2,1)S(1)} collective-permute-done((bf16[416,768]{1,0:T(8,128)(2,1)S(1)}, bf16[416,768]{1,0:T(8,128)(2,1)S(1)}, u32[]{:S(2)}, u32[]{:S(2)}) %collective-permute-start.15) | collective-permute-done | bytes 639008 | tf_op jit(solution)/shard_map/ppermute | solution.py:477
  98.6 6.4 %place_first.1 = (bf16[768,1536]{1,0:T(8,128)(2,1)}, bf16[768,768]{1,0:T(8,128)(2,1)}, bf16[1536,256]{1,0:T(8,128)(2,1)}, bf16[1536,768]{1,0:T(8,128)(2,1)}, bf1...) custom-call(bf16[416,768]{1,0:T(8,128)(2,1)} %merge_pair.1.refs_0_, ...), custom_call_target="tpu_custom_call" | custom-call | tf_op jit(solution)/shard_map/place_first/pallas_call | solution.py:534
  109.2 4.3 %coefficients.1 = (bf16[96,24,64]{2,1,0:T(8,128)(2,1)}, bf16[96,24,64]{2,1,0:T(8,128)(2,1)}, f32[96,512]{1,0:T(8,128)}, f32[96,512]{1,0:T(8,128)}, f32[768,1]{1,...) custom-call(bf16[1536,256]{1,0:T(8,128)(2,1)} %get-tuple-element.302, ...), custom_call_target="tpu_custom_call" | custom-call | tf_op jit(solution)/shard_map/coefficients/pallas_call | solution.py:647
  113.5 9.9 %enter.1 = (bf16[1024,768]{1,0:T(8,128)(2,1)}, f32[1024,1536]{1,0:T(8,128)}, bf16[1024,1536]{1,0:T(8,128)(2,1)}, f32[768,1024]{1,0:T(8,128)}) custom-call(f32[1024,768]{1,0:T(8,128)} %fusion.9.unit, f32[3,768]{1,0:T(4,128)} %get-tuple-element.303.wide, bf16[768,1536]{1,0:T(8,128)(2,1)} %get-tuple-element.304.up_w, f32[1,1536]{1,0:T(1,128)} %get-tuple-element.305.up_b, ...), custom_call_target="tpu_custom_call" | custom-call | tf_op jit(solution)/shard_map/enter/pallas_call | solution.py:945
  124.0 24.1 %mix_forward_0.1 = (f32[768,1024]{1,0:T(8,128)}, f32[96,64,256]{2,1,0:T(8,128)}) custom-call(s32[1]{0:T(128)} %bitcast.12.dir_ref, f32[768,1024]{1,0:T(8,128)} %get-tuple-element.310.x_ref, bf16[96,24,64]{2,1,0:T(8,128)(2,1)} %get-tuple-element.311.d3_ref, bf16[96,24,64]{2,1,0:T(8,128)(2,1)} %get-tuple-element.312.w3_ref, ...), custom_call_target="tpu_custom_call" | custom-call | tf_op jit(solution)/shard_map/mix_forward_0/pallas_call | solution.py:232
  148.9 21.6 %gate.1 = (f32[768,1024]{1,0:T(8,128)}, bf16[1024,768]{1,0:T(8,128)(2,1)}, bf16[1024,768]{1,0:T(8,128)(2,1)}, f32[1,768]{1,0:T(1,128)}, bf16[1536,768]{1,0:T(8,1...) custom-call(bf16[1024,1536]{1,0:T(8,128)(2,1)} %get-tuple-element.308.up, ...), custom_call_target="tpu_custom_call" | custom-call | tf_op jit(solution)/shard_map/gate/pallas_call | solution.py:999
  171.9 36.3 %mix_backward_0.1 = (bf16[768,1024]{1,0:T(8,128)(2,1)}, f32[128,768]{1,0:T(8,128)}, f32[768,1]{1,0:T(8,128)}, f32[768,1]{1,0:T(8,128)}) custom-call(s32[1]{0:T(128)} %bitcast.12.dir_ref, f32[768,1024]{1,0:T(8,128)} %get-tuple-element.310.x_ref, f32[768,1024]{1,0:T(8,128)} %get-tuple-element.330.gm_ref, f32[96,64,256]{2,1,0:T(8,128)} %get-tuple-element.331.enter_ref, ...), custom_call_target="tpu_custom_call" | custom-call | tf_op jit(solution)/shard_map/mix_backward_0/pallas_call | solution.py:232
  214.9 4.9 %fusion.42 = f32[1024,1536]{1,0:T(8,128)S(1)} fusion(bf16[1024,768]{1,0:T(8,128)(2,1)} %collective-permute-done.24, bf16[1536,768]{1,0:T(8,128)(2,1)} %collective-permute-done.25), kind=kOutput, calls=%fused_computation.84 | convolution fusion | flops 2415919104 | bytes 10223616 | tf_op jit(solution)/shard_map/dot_general | solution.py:1023
  219.9 6.2 %convert_reduce_fusion = (f32[1536]{0:T(1024)}, bf16[1024,1536]{1,0:T(8,128)(2,1)}) fusion(f32[1024,1536]{1,0:T(8,128)S(1)} %bitcast.111, f32[1024,1536]{1,0:T(8,128)S(1)} %fusion.41, f32[1024,1536]{1,0:T(8,128)S(1)} %fusion.42), kind=kLoop, calls=%fused_computation.11 | loop fusion | flops 34601472 | bytes 22026240 | tf_op jit(solution)/shard_map/reduce_sum | solution.py:1163
  226.2 4.7 %fusion.43 = f32[1024,768]{1,0:T(8,128)S(1)} fusion(bf16[1024,1536]{1,0:T(8,128)(2,1)} %get-tuple-element.446, bf16[768,1536]{1,0:T(8,128)(2,1)S(1)} %copy-done.5), kind=kOutput, calls=%fused_computation.85 | convolution fusion | flops 2415919104 | bytes 8650752 | tf_op jit(solution)/shard_map/dot_general | solution.py:1023
  234.7 5.1 %small_sums.1.refs_6_ = f32[16,32,768]{2,1,0:T(8,128)} custom-call(bf16[1536,256]{1,0:T(8,128)(2,1)} %get-tuple-element.302.table, f32[128,768]{1,0:T(8,128)} %get-tuple-element.333.grads, f32[768,1]{1,0:T(8,128)} %get-tuple-element.334.skip, f32[768,1]{1,0:T(8,128)} %get-tuple-element.335.value_b, f32[1,768]{1,0:T(1,128)} %get-tuple-element.336.proj_b, ...), custom_call_target="tpu_custom_call" | custom-call | tf_op jit(solution)/shard_map/small_sums/pallas_call | solution.py:694
  239.8 5.9 %convolution_convert_fusion.refs_4_ = bf16[768,1536]{1,0:T(8,128)(2,1)} fusion(bf16[1024,768]{1,0:T(8,128)(2,1)S(1)} %copy-done.38, bf16[1024,1536]{1,0:T(8,128)(2,1)} %get-tuple-element.446), kind=kOutput, calls=%fused_computation.16 | convolution fusion | flops 2417098752 | bytes 7077888 | tf_op jit(solution)/shard_map/dot_general | solution.py:1023
  259.7 4.2 %collective-permute-done.26.refs_8_ = bf16[416,768]{1,0:T(8,128)(2,1)S(1)} collective-permute-done((bf16[416,768]{1,0:T(8,128)(2,1)}, bf16[416,768]{1,0:T(8,128)(2,1)S(1)}, u32[]{:S(2)}, u32[]{:S(2)}) %collective-permute-start.26) | collective-permute-done | bytes 639008 | tf_op jit(solution)/shard_map/ppermute | solution.py:831
  275.9 4.3 %collective-permute-start.32 = (bf16[416,768]{1,0:T(8,128)(2,1)}, bf16[416,768]{1,0:T(8,128)(2,1)}, u32[]{:S(2)}, u32[]{:S(2)}) collective-permute-start(bf16[416,768]{1,0:T(8,128)(2,1)} %get-tuple-element.359), channel_id=1, source_target_pairs={{0,8},{2,10},{4,12},{6,14},{8,0},{10,2},{12,4},{14,6},{16,24},{18,... | collective-permute-start | bytes 1916936 | tf_op jit(solution)/shard_map/ppermute | solution.py:831
  280.2 10.5 %collective-permute-done.30.refs_9_ = bf16[416,768]{1,0:T(8,128)(2,1)} collective-permute-done((bf16[416,768]{1,0:T(8,128)(2,1)}, bf16[416,768]{1,0:T(8,128)(2,1)}, u32[]{:S(2)}, u32[]{:S(2)}) %collective-permute-start.30) | collective-permute-done | bytes 639008 | tf_op jit(solution)/shard_map/ppermute | solution.py:831
  309.5 4.9 %collective-permute-done.35.refs_7_ = bf16[416,768]{1,0:T(8,128)(2,1)} collective-permute-done((bf16[416,768]{1,0:T(8,128)(2,1)}, bf16[416,768]{1,0:T(8,128)(2,1)}, u32[]{:S(2)}, u32[]{:S(2)}) %collective-permute-start.35) | collective-permute-done | bytes 639008 | tf_op jit(solution)/shard_map/ppermute | solution.py:831
  317.5 4.1 %sum_1.1 = (bf16[416,768]{1,0:T(8,128)(2,1)}, bf16[416,768]{1,0:T(8,128)(2,1)}, bf16[416,768]{1,0:T(8,128)(2,1)}, bf16[416,768]{1,0:T(8,128)(2,1)}) custom-call(bf16[1536,768]{1,0:T(8,128)(2,1)} %get-tuple-element.323.refs_0_, bf16[1536,768]{1,0:T(8,128)(2,1)} %get-tuple-element.324.refs_1_, bf16[768,384]{1,0:T(8,128)(2,1)} %get-tuple-element.325.refs_2_, ...), custom_call_target="tpu_custom_call" | custom-call | tf_op jit(solution)/shard_map/sum_1/pallas_call | solution.py:805
  324.6 4.2 %collective-permute-start.41 = (bf16[416,768]{1,0:T(8,128)(2,1)}, bf16[416,768]{1,0:T(8,128)(2,1)}, u32[]{:S(2)}, u32[]{:S(2)}) collective-permute-start(bf16[416,768]{1,0:T(8,128)(2,1)} %get-tuple-element.394), channel_id=1, source_target_pairs={{0,8},{2,10},{4,12},{6,14},{8,0},{10,2},{12,4},{14,6},{16,24},{18,... | collective-permute-start | bytes 1916936 | tf_op jit(solution)/shard_map/ppermute | solution.py:831
  339.3 4.3 %sum_0.1 = (bf16[416,768]{1,0:T(8,128)(2,1)}, bf16[416,768]{1,0:T(8,128)(2,1)}, bf16[416,768]{1,0:T(8,128)(2,1)}, bf16[416,768]{1,0:T(8,128)(2,1)}) custom-call(bf16[1536,768]{1,0:T(8,128)(2,1)} %get-tuple-element.323.refs_0_, bf16[1536,768]{1,0:T(8,128)(2,1)} %get-tuple-element.324.refs_1_, bf16[768,384]{1,0:T(8,128)(2,1)} %get-tuple-element.325.refs_2_, ...), custom_call_target="tpu_custom_call" | custom-call | tf_op jit(solution)/shard_map/sum_0/pallas_call | solution.py:805
  350.1 5.8 %collective-permute-done.43.refs_7_ = bf16[416,768]{1,0:T(8,128)(2,1)S(1)} collective-permute-done((bf16[416,768]{1,0:T(8,128)(2,1)}, bf16[416,768]{1,0:T(8,128)(2,1)S(1)}, u32[]{:S(2)}, u32[]{:S(2)}) %collective-permute-start.43) | collective-permute-done | bytes 639008 | tf_op jit(solution)/shard_map/ppermute | solution.py:831
  (214 shorter events, 159.2 us)
Async XLA Ops:
  10.8 17.8 %collective-permute-start.2 = (bf16[416,768]{1,0:T(8,128)(2,1)}, bf16[416,768]{1,0:T(8,128)(2,1)S(1)}, u32[]{:S(2)}, u32[]{:S(2)}) collective-permute-start(bf16[416,768]{1,0:T(8,128)(2,1)} %merge_pair.1.refs_0_), channel_id=1, source_target_pairs={{0,2},{2,0},{4,6},{6,4},{8,10},{10,8},{12,14},{14,12},{16,18},{18,... | collective-permute-start | bytes 1916936 | tf_op jit(solution)/shard_map/ppermute | solution.py:477
  13.7 16.4 %collective-permute-start.3 = (bf16[416,768]{1,0:T(8,128)(2,1)}, bf16[416,768]{1,0:T(8,128)(2,1)S(1)}, u32[]{:S(2)}, u32[]{:S(2)}) collective-permute-start(bf16[416,768]{1,0:T(8,128)(2,1)} %merge_pair.1.refs_0_), channel_id=1, source_target_pairs={{0,4},{2,6},{4,0},{6,2},{8,12},{10,14},{12,8},{14,10},{16,20},{18,... | collective-permute-start | bytes 1916936 | tf_op jit(solution)/shard_map/ppermute | solution.py:477
  15.3 18.5 %collective-permute-start.4 = (bf16[416,768]{1,0:T(8,128)(2,1)}, bf16[416,768]{1,0:T(8,128)(2,1)}, u32[]{:S(2)}, u32[]{:S(2)}) collective-permute-start(bf16[416,768]{1,0:T(8,128)(2,1)} %merge_pair.1.refs_0_), channel_id=1, source_target_pairs={{0,8},{2,10},{4,12},{6,14},{8,0},{10,2},{12,4},{14,6},{16,24},{18,... | collective-permute-start | bytes 1916936 | tf_op jit(solution)/shard_map/ppermute | solution.py:477
  34.7 19.7 %collective-permute-start.9 = (bf16[2,32,16,768]{3,2,1,0:T(8,128)(2,1)S(1)}, bf16[2,32,16,768]{3,2,1,0:T(8,128)(2,1)}, u32[]{:S(2)}, u32[]{:S(2)}) collective-permute-start(bf16[2,32,16,768]{3,2,1,0:T(8,128)(2,1)S(1)} %pad_maximum_fusion), channel_id=1, source_target_pairs={{0,1},{1,0},{2,3},{3,2},{4,5},{5,4},{6,7},{7,6},{8,9},{9,8},{10,11... | collective-permute-start | bytes 4718600 | tf_op jit(solution)/shard_map/ppermute | solution.py:1066
  35.4 17.2 %collective-permute-start.6 = (bf16[416,768]{1,0:T(8,128)(2,1)}, bf16[416,768]{1,0:T(8,128)(2,1)}, u32[]{:S(2)}, u32[]{:S(2)}) collective-permute-start(bf16[416,768]{1,0:T(8,128)(2,1)} %copy-done.25), channel_id=1, source_target_pairs={{0,2},{2,0},{4,6},{6,4},{8,10},{10,8},{12,14},{14,12},{16,18},{18,... | collective-permute-start | bytes 1916936 | tf_op jit(solution)/shard_map/ppermute | solution.py:477
  36.0 16.8 %collective-permute-start.7 = (bf16[416,768]{1,0:T(8,128)(2,1)}, bf16[416,768]{1,0:T(8,128)(2,1)}, u32[]{:S(2)}, u32[]{:S(2)}) collective-permute-start(bf16[416,768]{1,0:T(8,128)(2,1)} %collective-permute-done.4.refs_4_), channel_id=1, source_target_pairs={{0,4},{2,6},{4,0},{6,2},{8,12},{10,14},{12,8},{14,10},{16,20},{18,... | collective-permute-start | bytes 1916936 | tf_op jit(solution)/shard_map/ppermute | solution.py:477
  36.5 17.9 %collective-permute-start.8 = (bf16[416,768]{1,0:T(8,128)(2,1)}, bf16[416,768]{1,0:T(8,128)(2,1)}, u32[]{:S(2)}, u32[]{:S(2)}) collective-permute-start(bf16[416,768]{1,0:T(8,128)(2,1)} %broadcast_select_fusion.1), channel_id=1, source_target_pairs={{0,8},{2,10},{4,12},{6,14},{8,0},{10,2},{12,4},{14,6},{16,24},{18,... | collective-permute-start | bytes 1916936 | tf_op jit(solution)/shard_map/ppermute | solution.py:477
  56.3 15.7 %collective-permute-start.11 = (bf16[416,768]{1,0:T(8,128)(2,1)}, bf16[416,768]{1,0:T(8,128)(2,1)S(1)}, u32[]{:S(2)}, u32[]{:S(2)}) collective-permute-start(bf16[416,768]{1,0:T(8,128)(2,1)} %collective-permute-done.7.refs_7_), channel_id=1, source_target_pairs={{0,2},{2,0},{4,6},{6,4},{8,10},{10,8},{12,14},{14,12},{16,18},{18,... | collective-permute-start | bytes 1916936 | tf_op jit(solution)/shard_map/ppermute | solution.py:477
  57.8 15.4 %collective-permute-start.12 = (bf16[416,768]{1,0:T(8,128)(2,1)}, bf16[416,768]{1,0:T(8,128)(2,1)}, u32[]{:S(2)}, u32[]{:S(2)}) collective-permute-start(bf16[416,768]{1,0:T(8,128)(2,1)} %collective-permute-done.8.refs_8_), channel_id=1, source_target_pairs={{0,4},{2,6},{4,0},{6,2},{8,12},{10,14},{12,8},{14,10},{16,20},{18,... | collective-permute-start | bytes 1916936 | tf_op jit(solution)/shard_map/ppermute | solution.py:477
  59.4 15.9 %collective-permute-start.13 = (bf16[416,768]{1,0:T(8,128)(2,1)S(1)}, bf16[416,768]{1,0:T(8,128)(2,1)S(1)}, u32[]{:S(2)}, u32[]{:S(2)}) collective-permute-start(bf16[416,768]{1,0:T(8,128)(2,1)S(1)} %broadcast_select_fusion), channel_id=1, source_target_pairs={{0,8},{2,10},{4,12},{6,14},{8,0},{10,2},{12,4},{14,6},{16,24},{18,... | collective-permute-start | bytes 1916936 | tf_op jit(solution)/shard_map/ppermute | solution.py:477
  123.4 24.7 %collective-permute-start.21 = (bf16[1024,1536]{1,0:T(8,128)(2,1)}, bf16[1024,1536]{1,0:T(8,128)(2,1)}, u32[]{:S(2)}, u32[]{:S(2)}) collective-permute-start(bf16[1024,1536]{1,0:T(8,128)(2,1)} %get-tuple-element.308.up), channel_id=1, source_target_pairs={{0,1},{1,0},{2,3},{3,2},{4,5},{5,4},{6,7},{7,6},{8,9},{9,8},{10,11... | collective-permute-start | bytes 9437192 | tf_op jit(solution)/shard_map/ppermute | solution.py:1066
  123.4 91.5 %collective-permute-start.25 = (bf16[1536,768]{1,0:T(8,128)(2,1)}, bf16[1536,768]{1,0:T(8,128)(2,1)}, u32[]{:S(2)}, u32[]{:S(2)}) collective-permute-start(bf16[1536,768]{1,0:T(8,128)(2,1)} %get-tuple-element.319.proj_theirs), channel_id=1, source_target_pairs={{0,1},{1,0},{2,3},{3,2},{4,5},{5,4},{6,7},{7,6},{8,9},{9,8},{10,11... | collective-permute-start | bytes 7077896 | tf_op jit(solution)/shard_map/ppermute | solution.py:1066
  123.9 24.2 %collective-permute-start.22 = (bf16[768,384]{1,0:T(8,128)(2,1)S(1)}, bf16[768,384]{1,0:T(8,128)(2,1)S(1)}, u32[]{:S(2)}, u32[]{:S(2)}) collective-permute-start(bf16[768,384]{1,0:T(8,128)(2,1)S(1)} %copy-done.35), channel_id=1, source_target_pairs={{0,1},{1,0},{2,3},{3,2},{4,5},{5,4},{6,7},{7,6},{8,9},{9,8},{10,11... | collective-permute-start | bytes 1769480 | tf_op jit(solution)/shard_map/ppermute | solution.py:1066
  170.5 44.4 %collective-permute-start.24 = (bf16[1024,768]{1,0:T(8,128)(2,1)}, bf16[1024,768]{1,0:T(8,128)(2,1)}, u32[]{:S(2)}, u32[]{:S(2)}) collective-permute-start(bf16[1024,768]{1,0:T(8,128)(2,1)} %get-tuple-element.328), channel_id=1, source_target_pairs={{0,1},{1,0},{2,3},{3,2},{4,5},{5,4},{6,7},{7,6},{8,9},{9,8},{10,11... | collective-permute-start | bytes 4718600 | tf_op jit(solution)/shard_map/ppermute | solution.py:1066
  171.4 74.2 %collective-permute-start.23 = (bf16[768,384]{1,0:T(8,128)(2,1)}, bf16[768,384]{1,0:T(8,128)(2,1)S(1)}, u32[]{:S(2)}, u32[]{:S(2)}) collective-permute-start(bf16[768,384]{1,0:T(8,128)(2,1)} %get-tuple-element.326), channel_id=1, source_target_pairs={{0,1},{1,0},{2,3},{3,2},{4,5},{5,4},{6,7},{7,6},{8,9},{9,8},{10,11... | collective-permute-start | bytes 1769480 | tf_op jit(solution)/shard_map/ppermute | solution.py:1066
  250.6 14.8 %collective-permute-start.27 = (bf16[416,768]{1,0:T(8,128)(2,1)}, bf16[416,768]{1,0:T(8,128)(2,1)}, u32[]{:S(2)}, u32[]{:S(2)}) collective-permute-start(bf16[416,768]{1,0:T(8,128)(2,1)} %get-tuple-element.343), channel_id=1, source_target_pairs={{0,4},{2,6},{4,0},{6,2},{8,12},{10,14},{12,8},{14,10},{16,20},{18,... | collective-permute-start | bytes 1916936 | tf_op jit(solution)/shard_map/ppermute | solution.py:831
  251.9 15.1 %collective-permute-start.28 = (bf16[416,768]{1,0:T(8,128)(2,1)}, bf16[416,768]{1,0:T(8,128)(2,1)}, u32[]{:S(2)}, u32[]{:S(2)}) collective-permute-start(bf16[416,768]{1,0:T(8,128)(2,1)} %get-tuple-element.344), channel_id=1, source_target_pairs={{0,8},{2,10},{4,12},{6,14},{8,0},{10,2},{12,4},{14,6},{16,24},{18,... | collective-permute-start | bytes 1916936 | tf_op jit(solution)/shard_map/ppermute | solution.py:831
  271.0 23.3 %collective-permute-start.33 = (bf16[2,32,16,768]{3,2,1,0:T(8,128)(2,1)S(1)}, bf16[2,32,16,768]{3,2,1,0:T(8,128)(2,1)}, u32[]{:S(2)}, u32[]{:S(2)}) collective-permute-start(bf16[2,32,16,768]{3,2,1,0:T(8,128)(2,1)S(1)} %pad_maximum_fusion.1), channel_id=1, source_target_pairs={{0,1},{1,0},{2,3},{3,2},{4,5},{5,4},{6,7},{7,6},{8,9},{9,8},{10,11... | collective-permute-start | bytes 4718600 | tf_op jit(solution)/shard_map/ppermute | solution.py:1066
  274.1 16.7 %collective-permute-start.30 = (bf16[416,768]{1,0:T(8,128)(2,1)}, bf16[416,768]{1,0:T(8,128)(2,1)}, u32[]{:S(2)}, u32[]{:S(2)}) collective-permute-start(bf16[416,768]{1,0:T(8,128)(2,1)} %get-tuple-element.357), channel_id=1, source_target_pairs={{0,2},{2,0},{4,6},{6,4},{8,10},{10,8},{12,14},{14,12},{16,18},{18,... | collective-permute-start | bytes 1916936 | tf_op jit(solution)/shard_map/ppermute | solution.py:831
  274.8 16.3 %collective-permute-start.31 = (bf16[416,768]{1,0:T(8,128)(2,1)}, bf16[416,768]{1,0:T(8,128)(2,1)}, u32[]{:S(2)}, u32[]{:S(2)}) collective-permute-start(bf16[416,768]{1,0:T(8,128)(2,1)} %get-tuple-element.358), channel_id=1, source_target_pairs={{0,4},{2,6},{4,0},{6,2},{8,12},{10,14},{12,8},{14,10},{16,20},{18,... | collective-permute-start | bytes 1916936 | tf_op jit(solution)/shard_map/ppermute | solution.py:831
  275.9 18.4 %collective-permute-start.32 = (bf16[416,768]{1,0:T(8,128)(2,1)}, bf16[416,768]{1,0:T(8,128)(2,1)}, u32[]{:S(2)}, u32[]{:S(2)}) collective-permute-start(bf16[416,768]{1,0:T(8,128)(2,1)} %get-tuple-element.359), channel_id=1, source_target_pairs={{0,8},{2,10},{4,12},{6,14},{8,0},{10,2},{12,4},{14,6},{16,24},{18,... | collective-permute-start | bytes 1916936 | tf_op jit(solution)/shard_map/ppermute | solution.py:831
  299.1 15.2 %collective-permute-start.35 = (bf16[416,768]{1,0:T(8,128)(2,1)}, bf16[416,768]{1,0:T(8,128)(2,1)}, u32[]{:S(2)}, u32[]{:S(2)}) collective-permute-start(bf16[416,768]{1,0:T(8,128)(2,1)} %get-tuple-element.375), channel_id=1, source_target_pairs={{0,2},{2,0},{4,6},{6,4},{8,10},{10,8},{12,14},{14,12},{16,18},{18,... | collective-permute-start | bytes 1916936 | tf_op jit(solution)/shard_map/ppermute | solution.py:831
  300.2 14.9 %collective-permute-start.36 = (bf16[416,768]{1,0:T(8,128)(2,1)}, bf16[416,768]{1,0:T(8,128)(2,1)}, u32[]{:S(2)}, u32[]{:S(2)}) collective-permute-start(bf16[416,768]{1,0:T(8,128)(2,1)} %get-tuple-element.376), channel_id=1, source_target_pairs={{0,4},{2,6},{4,0},{6,2},{8,12},{10,14},{12,8},{14,10},{16,20},{18,... | collective-permute-start | bytes 1916936 | tf_op jit(solution)/shard_map/ppermute | solution.py:831
  301.5 16.0 %collective-permute-start.37 = (bf16[416,768]{1,0:T(8,128)(2,1)}, bf16[416,768]{1,0:T(8,128)(2,1)}, u32[]{:S(2)}, u32[]{:S(2)}) collective-permute-start(bf16[416,768]{1,0:T(8,128)(2,1)} %get-tuple-element.377), channel_id=1, source_target_pairs={{0,8},{2,10},{4,12},{6,14},{8,0},{10,2},{12,4},{14,6},{16,24},{18,... | collective-permute-start | bytes 1916936 | tf_op jit(solution)/shard_map/ppermute | solution.py:831
  (65 other events, 648.2 us)
